TPU v7x, 256 devices: a whole 4x4x8 slice. The times are simulated.
256 devices in a mesh: row: 32 (over x_hi, z, core), col: 8 (over x_lo, y).
Axes of the slice: x: 4 (x_hi: 2, x_lo: 2; x = x_hi * 2 + x_lo), y: 4, z: 8, core: 2. Of those that a mesh axis runs over, the one named last changes fastest.
Arguments:
- pair_input: bfloat16 [1024, 1024, 128], P('row', 'col'), may hold values from -16 to 16
- token_mask: int32 [1024], replicated, may hold values 0 or 1
- in_gain: float32 [2, 128], replicated, may hold values from 0.5 to 2
- proj_weight: bfloat16 [2, 128, 512], replicated, may hold values from -0.5 to 0.5
- gate_weight: bfloat16 [2, 128, 128], replicated, may hold values from -0.5 to 0.5
- out_gain: float32 [2, 128], replicated, may hold values from 0.5 to 2
- out_weight: bfloat16 [2, 128, 128], replicated, may hold values from -0.5 to 0.5
Outputs:
- pair_out: bfloat16 [1024, 1024, 128], P('row', 'col')
All inputs are finite; a program needn't handle non-finite values.
Results may differ from a plain program's by a relative error of at most 0.008.
Values may be sent and summed in bfloat16 or wider, within the bound.
No kernel may reach another device: no remote copies, remote signals or barrier semaphores. Data moves between devices by JAX's collectives and lax.ppermute only.
A program may use at most 64 MiB of HBM per device.

v0:
```python
import jax
import jax.numpy as jnp
from jax import lax
from jax.sharding import PartitionSpec as P

EPSILON = 1e-05


def norm_axis(values, gain, axis):
    average = jnp.mean(values, axis=axis, keepdims=True)
    centred = values - average
    variance = jnp.mean(centred * centred, axis=axis, keepdims=True)
    return centred * lax.rsqrt(variance + EPSILON) * gain


def gated_proj(normed, weights, pair_mask):
    both_parts = jnp.einsum("rqc,ce->erq", normed, weights, preferred_element_type=jnp.float32)
    half_width = weights.shape[1] // 2
    return (jax.nn.sigmoid(both_parts[:half_width]) * both_parts[half_width:] * pair_mask).astype(
        jnp.bfloat16
    )


def triangle(
    current, mask_rows, mask_cols, in_gain, proj_weight, gate_weight, out_gain, out_weight, outgoing
):
    hidden_width = out_weight.shape[0]
    normed = norm_axis(current.astype(jnp.float32), in_gain, -1).astype(jnp.bfloat16)
    pair_mask = mask_rows[:, None] * mask_cols[None, :]
    left_proj = gated_proj(normed, proj_weight[:, : 2 * hidden_width], pair_mask)
    right_proj = gated_proj(normed, proj_weight[:, 2 * hidden_width :], pair_mask)
    gate_values = jax.nn.sigmoid(
        jnp.einsum("rqc,cd->rqd", normed, gate_weight, preferred_element_type=jnp.float32)
    )
    left_split, right_split = (
        lax.all_to_all(left_proj, "row", split_axis=0, concat_axis=1, tiled=True),
        lax.all_to_all(right_proj, "row", split_axis=0, concat_axis=1, tiled=True),
    )
    if outgoing:
        left_rows = lax.all_to_all(left_split, "col", split_axis=1, concat_axis=2, tiled=True)
        product = jnp.einsum(
            "cik,cjk->cij",
            left_rows,
            lax.all_gather(right_split, "col", axis=2, tiled=True),
            preferred_element_type=jnp.float32,
        ).astype(jnp.bfloat16)
        product = lax.all_to_all(product, "col", split_axis=2, concat_axis=1, tiled=True)
    else:
        product = jnp.einsum(
            "cki,ckj->cij",
            left_split,
            lax.all_gather(right_split, "col", axis=2, tiled=True),
            preferred_element_type=jnp.float32,
        ).astype(jnp.bfloat16)
        product = lax.all_to_all(product, "col", split_axis=2, concat_axis=1, tiled=True)
    hidden_cells = lax.all_to_all(product, "row", split_axis=1, concat_axis=0, tiled=True)
    normed_hidden = norm_axis(hidden_cells.astype(jnp.float32), out_gain[:, None, None], 0).astype(
        jnp.bfloat16
    )
    update = jnp.einsum(
        "hrq,hc->rqc", normed_hidden, out_weight, preferred_element_type=jnp.float32
    )
    return (current.astype(jnp.float32) + gate_values * update).astype(jnp.bfloat16)


def per_device(pair_input, token_mask, in_gain, proj_weight, gate_weight, out_gain, out_weight):
    row_count = pair_input.shape[0]
    col_count = pair_input.shape[1]
    mask_float = token_mask.astype(jnp.float32)
    mask_rows = lax.dynamic_slice_in_dim(
        mask_float, lax.axis_index("row") * row_count, row_count, 0
    )
    mask_cols = lax.dynamic_slice_in_dim(
        mask_float, lax.axis_index("col") * col_count, col_count, 0
    )
    current = pair_input
    for module_index in range(2):
        current = triangle(
            current,
            mask_rows,
            mask_cols,
            in_gain[module_index],
            proj_weight[module_index],
            gate_weight[module_index],
            out_gain[module_index],
            out_weight[module_index],
            module_index == 0,
        )
    return current


def solution(mesh):
    placed = (P("row", "col", None), P(), P(), P(), P(), P(), P())
    return jax.shard_map(
        per_device, mesh=mesh, in_specs=placed, out_specs=P("row", "col", None), check_vma=False
    )
```

profile of v0, /device:TPU:1, one launch (start us, length us, event | category | flops | bytes accessed | tf_op | source)
XLA Modules:
  0.0 474.1 jit_solution(1863886801599536224)
XLA Ops:
  6.5 1.7 copy.117
  8.2 0.2 convert_reduce_fusion.1
  8.4 0.3 fusion.7
  8.8 2.8 convolution_bitcast_fusion.2
  11.6 2.7 convolution_bitcast_fusion.3
  14.4 0.1 dynamic_slice.6
  14.6 4.0 fusion.28
  18.6 1.7 copy.127
  20.3 40.3 %all_to_all.144 = bf16[128,32,128]{2,1,0:T(8,128)(2,1)S(1)} all-to-all(bf16[128,32,128]{2,1,0:T(8,128)(2,1)} %copy.127), channel_id=1, replica_groups=mesh['row'=32,'col'=8] {'row'}, dimensions={0} | all-to-all | bytes 2097152 | tf_op jit(solution)/shard_map/all_to_all | solution.py:37
  60.6 1.1 copy.128
  61.7 1.0 copy.121
  62.7 33.8 %all_to_all.145 = bf16[128,32,128]{2,1,0:T(8,128)(2,1)S(1)} all-to-all(bf16[128,32,128]{2,1,0:T(8,128)(2,1)S(1)} %copy.121), channel_id=1, replica_groups=mesh['row'=32,'col'=8] {'row'}, dimensions={0} | all-to-all | bytes 2097152 | tf_op jit(solution)/shard_map/all_to_all | solution.py:36
  96.6 0.8 copy.123
  97.4 31.3 %all_to_all.146 = bf16[4,1024,128]{2,0,1:T(4,128)(2,1)S(1)} all-to-all(bf16[4,1024,128]{2,0,1:T(4,128)(2,1)S(1)} %copy.123), channel_id=1, replica_groups=mesh['row'=32,'col'=8] {'col'}, dimensions={1} | all-to-all | bytes 2097152 | tf_op jit(solution)/shard_map/all_to_all | solution.py:40
  128.6 0.1 copy.124
  128.8 51.4 %all-gather.3.cloned.1.call-done = bf16[4,1024,1024]{2,1,0:T(8,128)(2,1)} async-done(((bf16[4,1024,128]{2,1,0:T(8,128)(2,1)}), bf16[4,1024,1024]{2,1,0:T(8,128)(2,1)}) %all-gather.3.cloned.1.call-update) | async-done | bytes 8388624 | tf_op jit(solution)/shard_map/all_gather | solution.py:44
  180.1 6.3 %convolution_convert_fusion.1 = bf16[4,128,1024]{2,1,0:T(8,128)(2,1)S(1)} fusion(bf16[4,1024,1024]{2,1,0:T(8,128)(2,1)} %all-gather.3.cloned.1.call-done, bf16[4,8,16,8,128]{4,3,2,1,0:T(8,128)(2,1)S(1)} %bitcast.126), kind=kOutput, calls=%fused_computation.67 | convolution fusion | flops 1074266112 | bytes 10485760 | tf_op jit(solution)/shard_map/cik,cjk->cij/dot_general | solution.py:41
  186.4 0.8 copy.129
  187.2 14.1 %all_to_all.147 = bf16[4,128,1024]{1,0,2:T(4,128)(2,1)S(1)} all-to-all(bf16[4,128,1024]{1,0,2:T(4,128)(2,1)S(1)} %copy.129), channel_id=1, replica_groups=mesh['row'=32,'col'=8] {'col'}, dimensions={2} | all-to-all | bytes 2097152 | tf_op jit(solution)/shard_map/all_to_all | solution.py:47
  201.3 0.1 copy.130
  201.4 0.7 copy.131
  202.1 1.8 copy.132
  203.9 16.2 %all-to-all-start.4 = ((bf16[4,1024,128]{2,0,1:T(4,128)(2,1)}), bf16[4,1024,128]{2,0,1:T(4,128)(2,1)S(1)}, u32[]{:S(2)}, u32[]{:S(2)}) async-start(bf16[4,1024,128]{2,0,1:T(4,128)(2,1)} %copy.132), calls=%async_computation.4 | async-start | bytes 2097152 | tf_op jit(solution)/shard_map/all_to_all | solution.py:56
  220.1 0.2 all-gather.5.cloned.1.call-start
  220.4 0.1 mul.183
  220.5 0.1 copy.134
  220.6 1.9 fusion.51
  222.4 25.4 %all-to-all-done.4 = bf16[4,1024,128]{2,0,1:T(4,128)(2,1)S(1)} async-done(((bf16[4,1024,128]{2,0,1:T(4,128)(2,1)}), bf16[4,1024,128]{2,0,1:T(4,128)(2,1)S(1)}, u32[]{:S(2)}, u32[]{:S(2)}) %all-to-all-start.4) | async-done | bytes 1048608 | tf_op jit(solution)/shard_map/all_to_all | solution.py:56
  247.9 0.1 copy.133
  248.0 0.2 fusion.40
  248.2 0.3 fusion.43
  248.6 0.4 fusion.45
  248.9 0.1 copy.135
  249.1 1.1 copy-done
  250.1 1.2 convert_reduce_fusion
  251.3 0.3 fusion.4
  251.7 0.8 convolution_bitcast_fusion.1
  252.5 0.8 convolution_bitcast_fusion
  253.4 1.2 fusion.13
  254.6 1.7 copy.144
  256.3 34.0 %all_to_all.148 = bf16[128,32,128]{2,1,0:T(8,128)(2,1)S(1)} all-to-all(bf16[128,32,128]{2,1,0:T(8,128)(2,1)} %copy.144), channel_id=1, replica_groups=mesh['row'=32,'col'=8] {'row'}, dimensions={0} | all-to-all | bytes 2097152 | tf_op jit(solution)/shard_map/all_to_all | solution.py:37
  290.2 1.1 copy.145
  291.3 1.0 copy.141
  292.3 33.8 %all_to_all.149 = bf16[128,32,128]{2,1,0:T(8,128)(2,1)S(1)} all-to-all(bf16[128,32,128]{2,1,0:T(8,128)(2,1)S(1)} %copy.141), channel_id=1, replica_groups=mesh['row'=32,'col'=8] {'row'}, dimensions={0} | all-to-all | bytes 2097152 | tf_op jit(solution)/shard_map/all_to_all | solution.py:36
  326.1 0.1 copy.142
  326.2 70.7 %all-gather.5.cloned.1.call-done = bf16[4,1024,1024]{2,1,0:T(8,128)(2,1)} async-done(((bf16[4,1024,128]{2,1,0:T(8,128)(2,1)}), bf16[4,1024,1024]{2,1,0:T(8,128)(2,1)}) %all-gather.5.cloned.1.call-update) | async-done | bytes 8388624 | tf_op jit(solution)/shard_map/all_gather | solution.py:52
  396.8 4.7 convolution_convert_fusion
  401.6 0.8 copy.147
  402.3 14.1 %all_to_all.150 = bf16[4,128,1024]{1,0,2:T(4,128)(2,1)S(1)} all-to-all(bf16[4,128,1024]{1,0,2:T(4,128)(2,1)S(1)} %copy.147), channel_id=1, replica_groups=mesh['row'=32,'col'=8] {'col'}, dimensions={2} | all-to-all | bytes 2097152 | tf_op jit(solution)/shard_map/all_to_all | solution.py:55
  416.5 0.1 copy.148
  416.6 0.7 copy.149
  417.3 1.8 copy.150
  419.1 15.9 %all-to-all-start.8 = ((bf16[4,1024,128]{2,0,1:T(4,128)(2,1)}), bf16[4,1024,128]{2,0,1:T(4,128)(2,1)S(1)}, u32[]{:S(2)}, u32[]{:S(2)}) async-start(bf16[4,1024,128]{2,0,1:T(4,128)(2,1)} %copy.150), calls=%async_computation.8 | async-start | bytes 2097152 | tf_op jit(solution)/shard_map/all_to_all | solution.py:56
  434.9 0.1 mul.200
  435.1 1.9 fusion.54
  437.0 25.7 %all-to-all-done.8 = bf16[4,1024,128]{2,0,1:T(4,128)(2,1)S(1)} async-done(((bf16[4,1024,128]{2,0,1:T(4,128)(2,1)}), bf16[4,1024,128]{2,0,1:T(4,128)(2,1)S(1)}, u32[]{:S(2)}, u32[]{:S(2)}) %all-to-all-start.8) | async-done | bytes 1048608 | tf_op jit(solution)/shard_map/all_to_all | solution.py:56
  462.7 0.1 copy.151
  462.8 0.2 fusion.33
  463.0 0.3 fusion.36
  463.4 0.4 fusion.38
  463.7 0.1 copy.153
  463.9 1.1 copy-done.1
  464.9 1.0 fusion.11
  465.9 1.3 copy.156
  (33 shorter events, 0.5 us)
Async XLA Ops:
  6.5 2.2 copy-start.5
  6.5 2.3 copy-start.2
  6.5 173.6 %all-gather.3.cloned.1.call-start = ((), (), s32[]{:S(2)}) async-start(), calls=%async_computation.9 | async-start | bytes 9437184 | tf_op jit(solution)/shard_map/all_gather | solution.py:44
  11.6 2.8 copy-start.4
  202.1 18.2 %copy-start.6 = (f32[2,128]{1,0:T(2,128)S(1)}, f32[2,128]{1,0:T(2,128)}, u32[]{:S(2)}) copy-start(f32[2,128]{1,0:T(2,128)} %param.12) | copy-start | bytes 3076
  202.1 18.4 %copy-start.3 = (bf16[2,128,128]{2,1,0:T(8,128)(2,1)S(1)}, bf16[2,128,128]{2,1,0:T(8,128)(2,1)}, u32[]{:S(2)}) copy-start(bf16[2,128,128]{2,1,0:T(8,128)(2,1)} %param.11) | copy-start | bytes 196612
  203.9 43.9 %all-to-all-start.4 = ((bf16[4,1024,128]{2,0,1:T(4,128)(2,1)}), bf16[4,1024,128]{2,0,1:T(4,128)(2,1)S(1)}, u32[]{:S(2)}, u32[]{:S(2)}) async-start(bf16[4,1024,128]{2,0,1:T(4,128)(2,1)} %copy.132), calls=%async_computation.4 | async-start | bytes 2097152 | tf_op jit(solution)/shard_map/all_to_all | solution.py:56
  220.1 176.7 %all-gather.5.cloned.1.call-start = ((), (), s32[]{:S(2)}) async-start(), calls=%async_computation.10 | async-start | bytes 9437184 | tf_op jit(solution)/shard_map/all_gather | solution.py:52
  248.5 1.6 copy-start
  248.6 1.6 copy-start.7
  419.1 43.6 %all-to-all-start.8 = ((bf16[4,1024,128]{2,0,1:T(4,128)(2,1)}), bf16[4,1024,128]{2,0,1:T(4,128)(2,1)S(1)}, u32[]{:S(2)}, u32[]{:S(2)}) async-start(bf16[4,1024,128]{2,0,1:T(4,128)(2,1)} %copy.150), calls=%async_computation.8 | async-start | bytes 2097152 | tf_op jit(solution)/shard_map/all_to_all | solution.py:56
  463.4 1.6 copy-start.1
Sparse Core Ops, SparseCore 0:
  61.9 118.2 all-gather.2
  291.4 105.3 all-gather.4
where the time goes:
time: 476 us; the launch traced here: 474 us
  blocking collectives  201 us (42%)
  waiting for transfers between devices  173 us (36%)
  starting transfers between devices  32.3 us (7%)
  matrix products  24.1 us (5%)
  local copies, waits for them, and re-layouts  21.4 us (4%)
  between operations  13.8 us (3%)
  other arithmetic  8.04 us (2%)
    all_gather x2, waiting for transfers between devices, triangle(): lax.all_gather(right_split, 'col', axis=2, tiled=True)  122 us
    all_to_all x2, blocking collectives, triangle(): lax.all_to_all(right_proj, 'row', split_axis=0, concat_axis=1, tiled=True)  74.3 us
    all_to_all x2, blocking collectives, triangle(): lax.all_to_all(left_proj, 'row', split_axis=0, concat_axis=1, tiled=True)  67.5 us
    all_to_all x2, waiting for transfers between devices, triangle(): lax.all_to_all(product, 'row', split_axis=1, concat_axis=0, tiled=True)  51.1 us
    all_to_all x2, starting transfers between devices, triangle(): lax.all_to_all(product, 'row', split_axis=1, concat_axis=0, tiled=True)  32.1 us
    all_to_all x1, blocking collectives, triangle(): lax.all_to_all(left_split, 'col', split_axis=1, concat_axis=2, tiled=True)  31.3 us
    all_to_all x2, blocking collectives, triangle(): lax.all_to_all(product, 'col', split_axis=2, concat_axis=1, tiled=True)  28.3 us
  transfers between devices with their start and end apart: 4, of which 4 were waited for; matrix products, arithmetic and copies ran while one was open for 2% of the time, Pallas kernels for 0%

commit v1 on v0

v1 whole, which is shorter than its diff:
```python
import functools

import jax
import jax.numpy as jnp
from jax import lax
from jax.experimental import pallas as pl
from jax.experimental.pallas import tpu as pltpu
from jax.sharding import Mesh, PartitionSpec as P

EPSILON = 1e-05
CHAN = 128
ROWS = 32
COLS = 128
STEP = 16
SUB = 4
PEERS = ("xh", "z", "xl", "y")
F32 = jnp.float32
BF16 = jnp.bfloat16
PARAMS = pltpu.CompilerParams(vmem_limit_bytes=40 * 1024 * 1024)


def sigmoid(values):
    return 0.5 * jnp.tanh(0.5 * values) + 0.5


def whole(shape):
    return pl.BlockSpec(shape, lambda *_: (0,) * len(shape))


SMEM = pl.BlockSpec(memory_space=pltpu.SMEM)


def layer_norm_lanes(cells, factor):
    average = jnp.mean(cells, axis=-1, keepdims=True)
    centred = cells - average
    variance = jnp.mean(centred * centred, axis=-1, keepdims=True)
    return centred * lax.rsqrt(variance + EPSILON) * factor


def project_rows(rows, row_masks, gain_mask, weight_ref, left_scratch, right_scratch, first):
    normed = [
        layer_norm_lanes(row, gain_mask * row_mask).astype(BF16)
        for row, row_mask in zip(rows, row_masks)
    ]
    flat = jnp.concatenate(normed, axis=0)
    projected = lax.dot_general(
        weight_ref[...], flat, (((1,), (1,)), ((), ())), preferred_element_type=F32
    )
    left = sigmoid(projected[:CHAN]) * projected[CHAN : 2 * CHAN]
    right = sigmoid(projected[2 * CHAN : 3 * CHAN]) * projected[3 * CHAN :]
    for index in range(len(rows)):
        place = pl.ds((first + index) * CHAN, CHAN)
        lanes = slice(index * COLS, (index + 1) * COLS)
        left_scratch[place, :] = left[:, lanes]
        right_scratch[place, :] = right[:, lanes]


def emit_projections(left_scratch, right_scratch, out_ref):
    def body(chan, carry):
        place = pl.ds(chan, STEP, stride=CHAN)
        out_ref[chan, 0] = left_scratch[place, :].astype(BF16)
        out_ref[chan, 1] = right_scratch[place, :].astype(BF16)
        return carry

    lax.fori_loop(0, CHAN, body, 0, unroll=8)


def project_kernel(row_mask_ref, cells_ref, gain_mask_ref, weight_ref, out_ref, left_scratch, right_scratch):
    base = pl.program_id(0) * STEP
    for first in range(0, STEP, SUB):
        rows = [cells_ref[first + index].astype(F32) for index in range(SUB)]
        masks = [row_mask_ref[base + first + index] for index in range(SUB)]
        project_rows(rows, masks, gain_mask_ref[...], weight_ref, left_scratch, right_scratch, first)
    emit_projections(left_scratch, right_scratch, out_ref)


CELLS = pl.BlockSpec((STEP, COLS, CHAN), lambda step: (step, 0, 0))
PAIRS = pl.BlockSpec((CHAN, 2, STEP, COLS), lambda step: (0, 0, step, 0))
HIDDEN = pl.BlockSpec((CHAN, STEP, COLS), lambda step: (0, step, 0))
PROJ_SCRATCH = [pltpu.VMEM((STEP * CHAN, COLS), F32)] * 2


def project(cells, row_mask, gain_mask, weight):
    return pl.pallas_call(
        project_kernel,
        grid=(ROWS // STEP,),
        in_specs=[SMEM, CELLS, whole((COLS, CHAN)), whole((4 * CHAN, CHAN))],
        out_specs=PAIRS,
        out_shape=jax.ShapeDtypeStruct((CHAN, 2, ROWS, COLS), BF16),
        scratch_shapes=PROJ_SCRATCH,
        compiler_params=PARAMS,
        name="project",
    )(row_mask, cells, gain_mask, weight)


def gate_kernel(cells_ref, gain_ref, weight_ref, out_ref):
    cells = cells_ref[...].astype(F32).reshape(STEP * COLS, CHAN)
    normed = layer_norm_lanes(cells, gain_ref[...]).astype(BF16)
    gate = sigmoid(jnp.dot(normed, weight_ref[...], preferred_element_type=F32))
    out_ref[...] = gate.reshape(STEP, COLS, CHAN)


def output_gate(cells, gain, weight):
    return pl.pallas_call(
        gate_kernel,
        grid=(ROWS // STEP,),
        in_specs=[CELLS, whole((1, CHAN)), whole((CHAN, CHAN))],
        out_specs=CELLS,
        out_shape=jax.ShapeDtypeStruct((ROWS, COLS, CHAN), F32),
        compiler_params=PARAMS,
        cost_estimate=pl.CostEstimate(
            flops=2 * ROWS * COLS * CHAN * CHAN, bytes_accessed=3 << 20, transcendentals=ROWS * COLS * CHAN
        ),
        name="output_gate",
    )(cells, gain.reshape(1, CHAN), weight)


def normed_hidden_rows(gain_ref, hidden_ref, scratch):
    hidden = hidden_ref[...].astype(F32)
    average = jnp.mean(hidden, axis=0)
    centred = hidden - average[None]
    scale = lax.rsqrt(jnp.mean(centred * centred, axis=0) + EPSILON)

    def body(chan, carry):
        values = (hidden_ref[chan].astype(F32) - average) * scale * gain_ref[chan]
        scratch[pl.ds(pl.multiple_of(chan * STEP, STEP), STEP), :] = values
        return carry

    lax.fori_loop(0, CHAN, body, 0, unroll=8)


def updated_row(index, scratch, weight_ref, cells_ref, gate_ref):
    hidden = scratch[pl.ds(index, CHAN, stride=STEP), :].astype(BF16)
    update = lax.dot_general(
        hidden, weight_ref[...], (((0,), (0,)), ((), ())), preferred_element_type=F32
    )
    return (cells_ref[index].astype(F32) + gate_ref[index] * update).astype(BF16)


def finish_kernel(gain_ref, hidden_ref, cells_ref, gate_ref, weight_ref, out_ref, scratch):
    normed_hidden_rows(gain_ref, hidden_ref, scratch)
    for index in range(STEP):
        out_ref[index] = updated_row(index, scratch, weight_ref, cells_ref, gate_ref)


def finish(hidden, cells, gate, gain, weight):
    return pl.pallas_call(
        finish_kernel,
        grid=(ROWS // STEP,),
        in_specs=[SMEM, HIDDEN, CELLS, CELLS, whole((CHAN, CHAN))],
        out_specs=CELLS,
        out_shape=jax.ShapeDtypeStruct((ROWS, COLS, CHAN), BF16),
        scratch_shapes=[pltpu.VMEM((CHAN * STEP, COLS), F32)],
        compiler_params=PARAMS,
        name="finish",
    )(gain, hidden, cells, gate, weight)


def finish_project_kernel(
    gain_ref, row_mask_ref, hidden_ref, cells_ref, gate_ref, weight_ref, gain_mask_ref, proj_ref,
    cells_out, pairs_out, scratch, left_scratch, right_scratch,
):
    base = pl.program_id(0) * STEP
    normed_hidden_rows(gain_ref, hidden_ref, scratch)
    for first in range(0, STEP, SUB):
        rows = []
        for index in range(first, first + SUB):
            row = updated_row(index, scratch, weight_ref, cells_ref, gate_ref)
            cells_out[index] = row
            rows.append(row.astype(F32))
        masks = [row_mask_ref[base + first + index] for index in range(SUB)]
        project_rows(rows, masks, gain_mask_ref[...], proj_ref, left_scratch, right_scratch, first)
    emit_projections(left_scratch, right_scratch, pairs_out)


def finish_project(hidden, cells, gate, gain, weight, row_mask, gain_mask, proj):
    return pl.pallas_call(
        finish_project_kernel,
        grid=(ROWS // STEP,),
        in_specs=[
            SMEM, SMEM, HIDDEN, CELLS, CELLS, whole((CHAN, CHAN)), whole((COLS, CHAN)), whole((4 * CHAN, CHAN)),
        ],
        out_specs=[CELLS, PAIRS],
        out_shape=[
            jax.ShapeDtypeStruct((ROWS, COLS, CHAN), BF16),
            jax.ShapeDtypeStruct((CHAN, 2, ROWS, COLS), BF16),
        ],
        scratch_shapes=[pltpu.VMEM((CHAN * STEP, COLS), F32)] + PROJ_SCRATCH,
        compiler_params=PARAMS,
        name="finish_project",
    )(gain, row_mask, hidden, cells, gate, weight, gain_mask, proj)


GROUPS = 16
BLOCKS = 8
TOKENS = BLOCKS * COLS


def outgoing_kernel(core_ref, pairs_ref, other_ref, out_ref, left, right):
    core = core_ref[0]
    for block in range(BLOCKS):
        lanes = slice(block * COLS, (block + 1) * COLS)
        left[:, :, lanes] = pairs_ref[:, block, 0]
        right[:, core, :, lanes] = pairs_ref[:, block, 1]
        right[:, 1 - core, :, lanes] = other_ref[:, block]
    left_rows = left[...].reshape(GROUPS * ROWS, TOKENS)
    for block in range(0, BLOCKS, 2):
        groups = slice(block * 2, block * 2 + 4)
        product = lax.dot_general(
            left_rows,
            right[groups].reshape(2 * COLS, TOKENS),
            (((1,), (1,)), ((), ())),
            preferred_element_type=F32,
        ).astype(BF16)
        for half in range(2):
            out_ref[:, block + half] = product[:, half * COLS : (half + 1) * COLS].reshape(GROUPS, ROWS, COLS)


def outgoing(core, pairs, other):
    return pl.pallas_call(
        outgoing_kernel,
        in_specs=[SMEM, whole((GROUPS, BLOCKS, 2, ROWS, COLS)), whole((GROUPS, BLOCKS, ROWS, COLS))],
        out_specs=whole((GROUPS, BLOCKS, ROWS, COLS)),
        grid=(1,),
        out_shape=jax.ShapeDtypeStruct((GROUPS, BLOCKS, ROWS, COLS), BF16),
        scratch_shapes=[
            pltpu.VMEM((GROUPS, ROWS, TOKENS), BF16),
            pltpu.VMEM((GROUPS, 2, ROWS, TOKENS), BF16),
        ],
        compiler_params=PARAMS,
        name="outgoing",
    )(core, pairs, other)


def incoming_kernel(core_ref, left_ref, right_ref, send_ref, keep_ref, right, total):
    core = core_ref[0]

    @pl.when(pl.program_id(0) == 0)
    def _():
        for block in range(BLOCKS):
            lanes = slice(block * COLS, (block + 1) * COLS)
            right[:, lanes] = right_ref[:, block, 0].reshape(GROUPS * ROWS, COLS)

    total[...] = lax.dot_general(
        left_ref[:, 0, 0].reshape(GROUPS * ROWS, COLS),
        right[...],
        (((0,), (0,)), ((), ())),
        preferred_element_type=F32,
    ).reshape(4, ROWS, TOKENS)
    for half in range(2):
        send_ref[half] = total[2 * half + 1 - core].astype(BF16)
        keep_ref[half] = total[2 * half + core]


def incoming(core, pairs):
    part = pl.BlockSpec((2, ROWS, TOKENS), lambda step: (step, 0, 0))
    return pl.pallas_call(
        incoming_kernel,
        grid=(BLOCKS,),
        in_specs=[
            SMEM,
            pl.BlockSpec((GROUPS, 1, 1, ROWS, COLS), lambda step: (0, step, 0, 0, 0)),
            pl.BlockSpec((GROUPS, BLOCKS, 1, ROWS, COLS), lambda step: (0, 0, 1, 0, 0)),
        ],
        out_specs=[part, part],
        out_shape=[
            jax.ShapeDtypeStruct((GROUPS, ROWS, TOKENS), BF16),
            jax.ShapeDtypeStruct((GROUPS, ROWS, TOKENS), F32),
        ],
        scratch_shapes=[pltpu.VMEM((GROUPS * ROWS, TOKENS), BF16), pltpu.VMEM((4, ROWS, TOKENS), F32)],
        compiler_params=PARAMS,
        name="incoming",
    )(core, pairs, pairs)


def join_kernel(keep_ref, other_ref, out_ref):
    total = (keep_ref[...] + other_ref[...].astype(F32)).astype(BF16)
    for block in range(BLOCKS):
        out_ref[:, block] = total[:, :, block * COLS : (block + 1) * COLS]


def join(keep, other):
    part = pl.BlockSpec((4, ROWS, TOKENS), lambda step: (step, 0, 0))
    return pl.pallas_call(
        join_kernel,
        grid=(GROUPS // 4,),
        in_specs=[part, part],
        out_specs=pl.BlockSpec((4, BLOCKS, ROWS, COLS), lambda step: (step, 0, 0, 0)),
        out_shape=jax.ShapeDtypeStruct((GROUPS, BLOCKS, ROWS, COLS), BF16),
        compiler_params=PARAMS,
        name="join",
    )(keep, other)


def exchange(values):
    return lax.all_to_all(values, PEERS, split_axis=0, concat_axis=0, tiled=True)


def to_other_core(values):
    return lax.ppermute(values, "c", [(0, 1), (1, 0)])


def per_device(pair_input, token_mask, in_gain, proj_weight, gate_weight, out_gain, out_weight):
    mask = token_mask.astype(F32)
    core = lax.axis_index("c").astype(jnp.int32).reshape(1)
    row_mask = lax.dynamic_slice_in_dim(mask, lax.axis_index(("xh", "z", "c")) * ROWS, ROWS, 0)
    col_mask = lax.dynamic_slice_in_dim(mask, lax.axis_index(("xl", "y")) * COLS, COLS, 0)
    gain_mask = col_mask[None, :, None] * in_gain[:, None, :]
    proj = jnp.swapaxes(proj_weight, 1, 2)

    pairs = exchange(project(pair_input, row_mask, gain_mask[0], proj[0]))
    gate = output_gate(pair_input, in_gain[0], gate_weight[0])
    pairs = pairs.reshape(GROUPS, BLOCKS, 2, ROWS, COLS)
    other = to_other_core(pairs[:, :, 1])
    product = outgoing(core, pairs, other)
    hidden = exchange(product.reshape(CHAN, ROWS, COLS))
    cells, pairs = finish_project(
        hidden, pair_input, gate, out_gain[0], out_weight[0], row_mask, gain_mask[1], proj[1]
    )

    pairs = exchange(pairs)
    gate = output_gate(cells, in_gain[1], gate_weight[1])
    send, keep = incoming(core, pairs.reshape(GROUPS, BLOCKS, 2, ROWS, COLS))
    product = join(keep, to_other_core(send))
    hidden = exchange(product.reshape(CHAN, ROWS, COLS))
    return finish(hidden, cells, gate, out_gain[1], out_weight[1])


def solution(mesh):
    split = Mesh(mesh.devices.reshape(2, 8, 2, 2, 4), ("xh", "z", "c", "xl", "y"))
    cells = P(("xh", "z", "c"), ("xl", "y"), None)
    return jax.shard_map(
        per_device, mesh=split, in_specs=(cells, P(), P(), P(), P(), P(), P()), out_specs=cells, check_vma=False
    )
```

time: 476 us -> 243 us (0.51)
  waiting for transfers between devices: 173 us -> 61.7 us
  blocking collectives: 201 us -> 125 us
  Pallas kernels: 0 us -> 30.2 us
  matrix products: 24.1 us -> 0 us
  local copies, waits for them, and re-layouts: 21.4 us -> 1.78 us
  between operations: 13.8 us -> 0.21 us
  starting transfers between devices: 32.3 us -> 22.3 us
  other arithmetic: 8.04 us -> 1.53 us
    all_gather x2 -> x0, waiting for transfers between devices: 122 us -> none  [triangle(): lax.all_gather(right_split, 'col', axis=2, tiled=True)]
    all_to_all x7 -> x2, blocking collectives: 201 us -> 125 us  [exchange(): lax.all_to_all(values, PEERS, split_axis=0, concat_axis=0, tiled=True)]
    pallas_call x0 -> x8, Pallas kernels: none -> 30.2 us  [the longest x1 9.39 us: finish_project(): pl.pallas_call(finish_project_kernel, grid=(ROWS // STEP,), in_specs=[SME...]
    dot_general x10 -> x0, matrix products: 24.1 us -> none  [the longest x4 7.22 us: gated_proj(): jnp.einsum('rqc,ce->erq', normed, weights, preferred_element_type=jnp.flo...]
    all_to_all x2, starting transfers between devices: 32.1 us -> 14.9 us  [exchange(): lax.all_to_all(values, PEERS, split_axis=0, concat_axis=0, tiled=True)]
    convert_element_type x9 -> x0, local copies, waits for them, and re-layouts: 8.36 us -> none  [the longest x4 5.3 us: gated_proj(): (jax.nn.sigmoid(both_parts[:half_width]) * both_parts[half_width:] * pair...]
    all_to_all x14 -> x1, local copies, waits for them, and re-layouts: 8.69 us -> 0.36 us  [exchange(): lax.all_to_all(values, PEERS, split_axis=0, concat_axis=0, tiled=True)]
    ppermute x0 -> x2, starting transfers between devices: none -> 7.36 us  [to_other_core(): return lax.ppermute(values, 'c', [(0, 1), (1, 0)])]
  transfers between devices with their start and end apart: 4 -> 4, of which waited for: 4 -> 4; matrix products, arithmetic and copies ran while one was open for 2% -> 0% of each run, Pallas kernels for 0% -> 1%
where the time goes in v1:
time: 243 us
  blocking collectives  125 us (51%)
  waiting for transfers between devices  61.7 us (25%)
  Pallas kernels  30.2 us (12%)
  starting transfers between devices  22.3 us (9%)
    all_to_all x2, blocking collectives, exchange(): lax.all_to_all(values, PEERS, split_axis=0, concat_axis=0, tiled=True)  125 us
    all_to_all x2, waiting for transfers between devices, exchange(): lax.all_to_all(values, PEERS, split_axis=0, concat_axis=0, tiled=True)  57.2 us
    all_to_all x2, starting transfers between devices, exchange(): lax.all_to_all(values, PEERS, split_axis=0, concat_axis=0, tiled=True)  14.9 us
    pallas_call x1, Pallas kernels, finish_project(): pl.pallas_call(finish_project_kernel, grid=(ROWS // STEP,), in_specs=[SME...  9.39 us
    ppermute x2, starting transfers between devices, to_other_core(): return lax.ppermute(values, 'c', [(0, 1), (1, 0)])  7.36 us
    pallas_call x1, Pallas kernels, project(): pl.pallas_call(project_kernel, grid=(ROWS // STEP,), in_specs=[SMEM, CELL...  5.53 us
  transfers between devices with their start and end apart: 4, of which 4 were waited for; matrix products, arithmetic and copies ran while one was open for 0% of the time, Pallas kernels for 1%

profile of v1, /device:TPU:1, one launch (start us, length us, event | category | flops | bytes accessed | tf_op | source)
XLA Modules:
  0.0 243.0 jit_solution(6319050241202894637)
XLA Ops:
  0.0 0.0 copy-start
  0.0 0.8 convert_element_type.3
  0.8 0.1 dynamic_slice.6.row_mask_ref
  0.9 0.1 dynamic_slice.7
  0.9 0.8 broadcast_multiply_fusion
  1.7 1.1 copy.8
  2.9 0.0 copy-done
  2.9 5.5 %project.1 = bf16[128,2,32,128]{3,2,1,0:T(8,128)(2,1)S(1)} custom-call(f32[32]{0:T(128)S(1)} %dynamic_slice.6.row_mask_ref, bf16[32,128,128]{2,1,0:T(8,128)(2,1)S(1)} %copy-done, f32[128,128]{1,0:T(8,128)S(1)} %get-tuple-element.16.gain_mask_ref, bf16[512,128]{1,0:T(8,128)(2,1)S(1)} %get-tuple-element.14.weight_ref), custom_call_target="tpu_custom_call" | custom-call | tf_op jit(solution)/shard_map/project/pallas_call | solution.py:84
  8.4 68.5 %all_to_all.20 = bf16[128,2,32,128]{3,2,1,0:T(8,128)(2,1)S(1)} all-to-all(bf16[128,2,32,128]{3,2,1,0:T(8,128)(2,1)S(1)} %project.1), channel_id=1, replica_groups=mesh['xh'=2,'z'=8,'c'=2,'xl'=2,'y'=4] {'xh','z','xl','y'}, dimensions={0} | all-to-all | bytes 4194304 | tf_op jit(solution)/shard_map/all_to_all | solution.py:296
  76.9 0.4 copy.9
  77.3 0.1 slice_bitcast_fusion
  77.3 3.0 %collective-permute-start = (bf16[16,8,32,128]{3,2,1,0:T(8,128)(2,1)S(1)}, bf16[16,8,32,128]{3,2,1,0:T(8,128)(2,1)S(1)}, u32[]{:S(2)}, u32[]{:S(2)}) collective-permute-start(bf16[16,8,32,128]{3,2,1,0:T(8,128)(2,1)S(1)} %slice_bitcast_fusion), channel_id=1, source_target_pairs={{0,8},{8,0},{1,9},{9,1},{2,10},{10,2},{3,11},{11,3},{4,12},{12,4},... | collective-permute-start | bytes 3145736 | tf_op jit(solution)/shard_map/ppermute | solution.py:300
  80.3 2.3 collective-permute-done.other_ref
  82.6 2.9 %outgoing.1 = bf16[16,8,32,128]{3,2,1,0:T(8,128)(2,1)} custom-call(s32[1]{0:T(128)} %bitcast.1.core_ref, bf16[16,8,2,32,128]{4,3,2,1,0:T(8,128)(2,1)S(1)} %bitcast.29, bf16[16,8,32,128]{3,2,1,0:T(8,128)(2,1)S(1)} %collective-permute-done.other_ref), custom_call_target="tpu_custom_call" | custom-call | tf_op jit(solution)/shard_map/outgoing/pallas_call | solution.py:220
  85.5 0.0 copy-start.5
  85.5 0.0 copy-start.3
  85.5 7.5 %all-to-all-start.1 = ((bf16[128,32,128]{2,1,0:T(8,128)(2,1)}), bf16[128,32,128]{2,1,0:T(8,128)(2,1)}, u32[]{:S(2)}, u32[]{:S(2)}) async-start(bf16[128,32,128]{2,1,0:T(8,128)(2,1)} %bitcast.9), calls=%async_computation.1 | async-start | bytes 2097152 | tf_op jit(solution)/shard_map/all_to_all | solution.py:296
  93.0 0.0 copy-done.5
  93.0 0.0 copy-start.6
  93.0 0.0 copy-start.4
  93.0 0.0 copy-done.3
  93.1 1.6 output_gate.2.gate_ref
  94.7 0.0 copy-done.6
  94.7 0.0 copy-done.4
  94.7 28.5 %all-to-all-done.1.hidden_ref = bf16[128,32,128]{2,1,0:T(8,128)(2,1)} async-done(((bf16[128,32,128]{2,1,0:T(8,128)(2,1)}), bf16[128,32,128]{2,1,0:T(8,128)(2,1)}, u32[]{:S(2)}, u32[]{:S(2)}) %all-to-all-start.1) | async-done | bytes 1048608 | tf_op jit(solution)/shard_map/all_to_all | solution.py:296
  123.3 9.4 %finish_project.1 = (bf16[32,128,128]{2,1,0:T(8,128)(2,1)S(1)}, bf16[128,2,32,128]{3,2,1,0:T(8,128)(2,1)S(1)}) custom-call(f32[128]{0:T(128)S(1)} %get-tuple-element.23.gain_ref, f32[32]{0:T(128)S(1)} %dynamic_slice.6.row_mask_ref, bf16[128,32,128]{2,1,0:T(8,128)(2,1)} %all-to-all-done.1.hidden_ref, bf16[32,128,128]{2,1,0:T(8,128)(2,1)S(1)} %copy-done, ...), custom_call_target="tpu_custom_call" | custom-call | tf_op jit(solution)/shard_map/finish_project/pallas_call | solution.py:177
  132.7 0.0 copy-start.1
  132.7 56.8 %all_to_all.21 = bf16[128,2,32,128]{3,2,1,0:T(8,128)(2,1)S(1)} all-to-all(bf16[128,2,32,128]{3,2,1,0:T(8,128)(2,1)S(1)} %get-tuple-element.9), channel_id=1, replica_groups=mesh['xh'=2,'z'=8,'c'=2,'xl'=2,'y'=4] {'xh','z','xl','y'}, dimensions={0} | all-to-all | bytes 4194304 | tf_op jit(solution)/shard_map/all_to_all | solution.py:296
  189.5 0.0 copy-done.1
  189.5 3.6 %incoming.1 = (bf16[16,32,1024]{2,1,0:T(8,128)(2,1)S(1)}, f32[16,32,1024]{2,1,0:T(8,128)S(1)}) custom-call(s32[1]{0:T(128)} %bitcast.1.core_ref, bf16[16,8,2,32,128]{4,3,2,1,0:T(8,128)(2,1)S(1)} %bitcast.30, bf16[16,8,2,32,128]{4,3,2,1,0:T(8,128)(2,1)S(1)} %bitcast.31), custom_call_target="tpu_custom_call" | custom-call | tf_op jit(solution)/shard_map/incoming/pallas_call | solution.py:257
  193.0 4.4 %collective-permute-start.1 = (bf16[16,32,1024]{2,1,0:T(8,128)(2,1)S(1)}, bf16[16,32,1024]{2,1,0:T(8,128)(2,1)S(1)}, u32[]{:S(2)}, u32[]{:S(2)}) collective-permute-start(bf16[16,32,1024]{2,1,0:T(8,128)(2,1)S(1)} %get-tuple-element.11), channel_id=1, source_target_pairs={{0,8},{8,0},{1,9},{9,1},{2,10},{10,2},{3,11},{11,3},{4,12},{12,4},... | collective-permute-start | bytes 3145736 | tf_op jit(solution)/shard_map/ppermute | solution.py:300
  197.4 2.3 collective-permute-done.1.other_ref
  199.7 1.6 join.1
  201.3 0.0 copy-start.2
  201.3 7.5 %all-to-all-start.3 = ((bf16[128,32,128]{2,1,0:T(8,128)(2,1)}), bf16[128,32,128]{2,1,0:T(8,128)(2,1)}, u32[]{:S(2)}, u32[]{:S(2)}) async-start(bf16[128,32,128]{2,1,0:T(8,128)(2,1)} %bitcast.15), calls=%async_computation.3 | async-start | bytes 2097152 | tf_op jit(solution)/shard_map/all_to_all | solution.py:296
  208.7 0.0 copy-done.2
  208.8 1.6 output_gate.3.gate_ref
  210.4 28.6 %all-to-all-done.3.hidden_ref = bf16[128,32,128]{2,1,0:T(8,128)(2,1)} async-done(((bf16[128,32,128]{2,1,0:T(8,128)(2,1)}), bf16[128,32,128]{2,1,0:T(8,128)(2,1)}, u32[]{:S(2)}, u32[]{:S(2)}) %all-to-all-start.3) | async-done | bytes 1048608 | tf_op jit(solution)/shard_map/all_to_all | solution.py:296
  239.0 3.9 %finish.1 = bf16[32,128,128]{2,1,0:T(8,128)(2,1)} custom-call(f32[128]{0:T(128)S(1)} %get-tuple-element.24.gain_ref, bf16[128,32,128]{2,1,0:T(8,128)(2,1)} %all-to-all-done.3.hidden_ref, bf16[32,128,128]{2,1,0:T(8,128)(2,1)S(1)} %copy-done.2, f32[32,128,128]{2,1,0:T(8,128)S(1)} %output_gate.3.gate_ref, bf16[128,128]{1,0:T(8,128)(2,1)S(1)} %get-tuple-element.17.weight_ref), custom_call_target="tpu_custom_call" | custom-call | tf_op jit(solution)/shard_map/finish/pallas_call | solution.py:147
  (6 shorter events, 0.1 us)
Async XLA Ops:
  0.0 2.9 %copy-start = (bf16[32,128,128]{2,1,0:T(8,128)(2,1)S(1)}, bf16[32,128,128]{2,1,0:T(8,128)(2,1)}, u32[]{:S(2)}) copy-start(bf16[32,128,128]{2,1,0:T(8,128)(2,1)} %cells_ref.5) | copy-start | bytes 3145732
  77.3 5.3 %collective-permute-start = (bf16[16,8,32,128]{3,2,1,0:T(8,128)(2,1)S(1)}, bf16[16,8,32,128]{3,2,1,0:T(8,128)(2,1)S(1)}, u32[]{:S(2)}, u32[]{:S(2)}) collective-permute-start(bf16[16,8,32,128]{3,2,1,0:T(8,128)(2,1)S(1)} %slice_bitcast_fusion), channel_id=1, source_target_pairs={{0,8},{8,0},{1,9},{9,1},{2,10},{10,2},{3,11},{11,3},{4,12},{12,4},... | collective-permute-start | bytes 3145736 | tf_op jit(solution)/shard_map/ppermute | solution.py:300
  85.5 7.5 %copy-start.5 = (f32[2,128]{1,0:T(2,128)S(1)}, f32[2,128]{1,0:T(2,128)}, u32[]{:S(2)}) copy-start(f32[2,128]{1,0:T(2,128)} %param.9) | copy-start | bytes 3076
  85.5 7.5 %copy-start.3 = (bf16[2,128,128]{2,1,0:T(8,128)(2,1)S(1)}, bf16[2,128,128]{2,1,0:T(8,128)(2,1)}, u32[]{:S(2)}) copy-start(bf16[2,128,128]{2,1,0:T(8,128)(2,1)} %param.11) | copy-start | bytes 196612
  85.5 37.7 %all-to-all-start.1 = ((bf16[128,32,128]{2,1,0:T(8,128)(2,1)}), bf16[128,32,128]{2,1,0:T(8,128)(2,1)}, u32[]{:S(2)}, u32[]{:S(2)}) async-start(bf16[128,32,128]{2,1,0:T(8,128)(2,1)} %bitcast.9), calls=%async_computation.1 | async-start | bytes 2097152 | tf_op jit(solution)/shard_map/all_to_all | solution.py:296
  93.0 1.7 copy-start.6
  93.0 1.7 copy-start.4
  132.7 56.8 %copy-start.1 = (bf16[32,128,128]{2,1,0:T(8,128)(2,1)}, bf16[32,128,128]{2,1,0:T(8,128)(2,1)S(1)}, u32[]{:S(2)}) copy-start(bf16[32,128,128]{2,1,0:T(8,128)(2,1)S(1)} %get-tuple-element.12.cells_ref) | copy-start | bytes 3145732
  193.0 6.7 %collective-permute-start.1 = (bf16[16,32,1024]{2,1,0:T(8,128)(2,1)S(1)}, bf16[16,32,1024]{2,1,0:T(8,128)(2,1)S(1)}, u32[]{:S(2)}, u32[]{:S(2)}) collective-permute-start(bf16[16,32,1024]{2,1,0:T(8,128)(2,1)S(1)} %get-tuple-element.11), channel_id=1, source_target_pairs={{0,8},{8,0},{1,9},{9,1},{2,10},{10,2},{3,11},{11,3},{4,12},{12,4},... | collective-permute-start | bytes 3145736 | tf_op jit(solution)/shard_map/ppermute | solution.py:300
  201.3 7.5 %copy-start.2 = (bf16[32,128,128]{2,1,0:T(8,128)(2,1)S(1)}, bf16[32,128,128]{2,1,0:T(8,128)(2,1)}, u32[]{:S(2)}) copy-start(bf16[32,128,128]{2,1,0:T(8,128)(2,1)} %copy-done.1) | copy-start | bytes 3145732
  201.3 37.7 %all-to-all-start.3 = ((bf16[128,32,128]{2,1,0:T(8,128)(2,1)}), bf16[128,32,128]{2,1,0:T(8,128)(2,1)}, u32[]{:S(2)}, u32[]{:S(2)}) async-start(bf16[128,32,128]{2,1,0:T(8,128)(2,1)} %bitcast.15), calls=%async_computation.3 | async-start | bytes 2097152 | tf_op jit(solution)/shard_map/all_to_all | solution.py:296

commit v2 on v0

v2 whole, which is shorter than its diff:
```python
import functools

import jax
import jax.numpy as jnp
from jax import lax
from jax.experimental import pallas as pl
from jax.experimental.pallas import tpu as pltpu
from jax.sharding import Mesh, PartitionSpec as P

EPSILON = 1e-05
CHAN = 128
ROWS = 32
COLS = 128
SUB = 4
CHAN_PITCH = CHAN + 1
ROW_PITCH = ROWS + 1
PEERS = ("xh", "z", "xl", "y")
F32 = jnp.float32
BF16 = jnp.bfloat16
PARAMS = pltpu.CompilerParams(vmem_limit_bytes=40 * 1024 * 1024)


def sigmoid(values):
    return 0.5 * jnp.tanh(0.5 * values) + 0.5


SMEM = pl.BlockSpec(memory_space=pltpu.SMEM)
VMEM = pl.BlockSpec(memory_space=pltpu.VMEM)


def kernel_call(kernel, name, in_specs, out_shape, scratch_shapes=(), cost=None):
    return pl.pallas_call(
        kernel,
        in_specs=in_specs,
        out_specs=jax.tree.map(lambda _: VMEM, out_shape),
        out_shape=out_shape,
        scratch_shapes=scratch_shapes,
        compiler_params=PARAMS,
        cost_estimate=cost,
        name=name,
    )


def layer_norm_lanes(cells, factor):
    average = jnp.mean(cells, axis=-1, keepdims=True)
    centred = cells - average
    variance = jnp.mean(centred * centred, axis=-1, keepdims=True)
    return centred * lax.rsqrt(variance + EPSILON) * factor


def masked_gain(place_ref, gain_ref, module, col_mask_ref):
    cols = col_mask_ref[pl.ds(place_ref[1], 1), :].astype(F32)
    return jnp.transpose(jnp.broadcast_to(cols, (CHAN, COLS))) * gain_ref[module : module + 1, :]


def row_mask(place_ref, row_mask_ref, index):
    return row_mask_ref[place_ref[0] + index].astype(F32)


def project_rows(rows, row_masks, gain_mask, weight_ref, left_scratch, right_scratch, first):
    normed = [
        layer_norm_lanes(row, gain_mask * mask).astype(BF16) for row, mask in zip(rows, row_masks)
    ]
    projected = lax.dot_general(
        weight_ref[...], jnp.concatenate(normed, axis=0), (((1,), (1,)), ((), ())), preferred_element_type=F32
    )
    left = sigmoid(projected[:CHAN]) * projected[CHAN : 2 * CHAN]
    right = sigmoid(projected[2 * CHAN : 3 * CHAN]) * projected[3 * CHAN :]
    for index in range(len(rows)):
        place = pl.ds((first + index) * CHAN_PITCH, CHAN)
        lanes = slice(index * COLS, (index + 1) * COLS)
        left_scratch[place, :] = left[:, lanes]
        right_scratch[place, :] = right[:, lanes]


def emit_projections(left_scratch, right_scratch, out_ref):
    def body(chan, carry):
        place = pl.ds(chan, ROWS, stride=CHAN_PITCH)
        out_ref[chan, 0] = left_scratch[place, :].astype(BF16)
        out_ref[chan, 1] = right_scratch[place, :].astype(BF16)
        return carry

    lax.fori_loop(0, CHAN, body, 0, unroll=8)


def project_kernel(place_ref, row_mask_ref, col_mask_ref, gain_ref, cells_ref, weight_ref, out_ref, left, right):
    gain_mask = masked_gain(place_ref, gain_ref, 0, col_mask_ref)
    for first in range(0, ROWS, SUB):
        rows = [cells_ref[first + index].astype(F32) for index in range(SUB)]
        masks = [row_mask(place_ref, row_mask_ref, first + index) for index in range(SUB)]
        project_rows(rows, masks, gain_mask, weight_ref, left, right, first)
    emit_projections(left, right, out_ref)


PROJ_SCRATCH = [pltpu.VMEM((ROWS * CHAN_PITCH, COLS), F32)] * 2
PAIRS = jax.ShapeDtypeStruct((CHAN, 2, ROWS, COLS), BF16)
CELLS = jax.ShapeDtypeStruct((ROWS, COLS, CHAN), BF16)


def project(place, mask, mask_rows, gain, cells, weight):
    call = kernel_call(
        project_kernel, "project", [SMEM, SMEM, VMEM, VMEM, VMEM, VMEM], PAIRS, PROJ_SCRATCH
    )
    return call(place, mask, mask_rows, gain, cells, weight)


def gate_kernel(module, gain_ref, cells_ref, weight_ref, out_ref):
    for first in range(0, ROWS, SUB):
        cells = cells_ref[first : first + SUB].astype(F32).reshape(SUB * COLS, CHAN)
        normed = layer_norm_lanes(cells, gain_ref[module : module + 1, :]).astype(BF16)
        gate = sigmoid(jnp.dot(normed, weight_ref[module], preferred_element_type=F32))
        out_ref[first : first + SUB] = gate.reshape(SUB, COLS, CHAN)


def output_gate(module, gain, cells, weight):
    call = kernel_call(
        functools.partial(gate_kernel, module),
        "output_gate",
        [VMEM, VMEM, VMEM],
        jax.ShapeDtypeStruct((ROWS, COLS, CHAN), F32),
        cost=pl.CostEstimate(
            flops=2 * ROWS * COLS * CHAN * CHAN, bytes_accessed=3 << 20, transcendentals=ROWS * COLS * CHAN
        ),
    )
    return call(gain, cells, weight)


def normed_hidden_rows(module, gain_ref, hidden_ref, scratch):
    for first in range(0, ROWS, 16):
        rows = slice(first, first + 16)
        hidden = hidden_ref[:, rows].astype(F32)
        average = jnp.mean(hidden, axis=0)
        centred = hidden - average[None]
        scale = lax.rsqrt(jnp.mean(centred * centred, axis=0) + EPSILON)

        def body(chan, carry):
            values = (hidden_ref[chan, rows].astype(F32) - average) * scale * gain_ref[module, chan]
            scratch[pl.ds(chan * ROW_PITCH + first, 16), :] = values
            return carry

        lax.fori_loop(0, CHAN, body, 0, unroll=8)


def updated_row(module, index, scratch, weight_ref, cells_ref, gate_ref):
    hidden = scratch[pl.ds(index, CHAN, stride=ROW_PITCH), :].astype(BF16)
    update = lax.dot_general(
        hidden, weight_ref[module], (((0,), (0,)), ((), ())), preferred_element_type=F32
    )
    return (cells_ref[index].astype(F32) + gate_ref[index] * update).astype(BF16)


HIDDEN_SCRATCH = pltpu.VMEM((CHAN * ROW_PITCH, COLS), F32)


def finish_kernel(gain_ref, hidden_ref, cells_ref, gate_ref, weight_ref, out_ref, scratch):
    normed_hidden_rows(1, gain_ref, hidden_ref, scratch)
    for index in range(ROWS):
        out_ref[index] = updated_row(1, index, scratch, weight_ref, cells_ref, gate_ref)


def finish(gain, hidden, cells, gate, weight):
    call = kernel_call(finish_kernel, "finish", [SMEM, VMEM, VMEM, VMEM, VMEM], CELLS, [HIDDEN_SCRATCH])
    return call(gain, hidden, cells, gate, weight)


def finish_project_kernel(
    place_ref, row_mask_ref, col_mask_ref, in_gain_ref, out_gain_ref, hidden_ref, cells_ref, gate_ref,
    weight_ref, proj_ref, cells_out, pairs_out, scratch, left, right,
):
    gain_mask = masked_gain(place_ref, in_gain_ref, 1, col_mask_ref)
    normed_hidden_rows(0, out_gain_ref, hidden_ref, scratch)
    for first in range(0, ROWS, SUB):
        rows = []
        for index in range(first, first + SUB):
            row = updated_row(0, index, scratch, weight_ref, cells_ref, gate_ref)
            cells_out[index] = row
            rows.append(row.astype(F32))
        masks = [row_mask(place_ref, row_mask_ref, first + index) for index in range(SUB)]
        project_rows(rows, masks, gain_mask, proj_ref, left, right, first)
    emit_projections(left, right, pairs_out)


def finish_project(place, mask, mask_rows, in_gain, out_gain, hidden, cells, gate, weight, proj):
    call = kernel_call(
        finish_project_kernel,
        "finish_project",
        [SMEM, SMEM, VMEM, VMEM, SMEM] + [VMEM] * 5,
        [CELLS, PAIRS],
        [HIDDEN_SCRATCH] + PROJ_SCRATCH,
    )
    return call(place, mask, mask_rows, in_gain, out_gain, hidden, cells, gate, weight, proj)


GROUPS = 16
BLOCKS = 8
TOKENS = BLOCKS * COLS
HALF = GROUPS * ROWS
PRODUCT = jax.ShapeDtypeStruct((GROUPS, BLOCKS, ROWS, COLS), BF16)


def block_lanes(block):
    return slice(block * COLS, (block + 1) * COLS)


def outgoing_kernel(place_ref, pairs_ref, other_ref, out_ref, left, right):
    core = place_ref[2]
    for block in range(BLOCKS):
        left[:, :, block_lanes(block)] = pairs_ref[:, block, 0]
        right[:, core, :, block_lanes(block)] = pairs_ref[:, block, 1]
        right[:, 1 - core, :, block_lanes(block)] = other_ref[:, block]
    left_rows = left[...].reshape(HALF, TOKENS)
    for block in range(0, BLOCKS, 2):
        groups = slice(block * 2, block * 2 + 4)
        product = lax.dot_general(
            left_rows,
            right[groups].reshape(2 * COLS, TOKENS),
            (((1,), (1,)), ((), ())),
            preferred_element_type=F32,
        ).astype(BF16)
        for half in range(2):
            out_ref[:, block + half] = product[:, block_lanes(half)].reshape(GROUPS, ROWS, COLS)


def outgoing(place, pairs, other):
    call = kernel_call(
        outgoing_kernel,
        "outgoing",
        [SMEM, VMEM, VMEM],
        PRODUCT,
        [pltpu.VMEM((GROUPS, ROWS, TOKENS), BF16), pltpu.VMEM((GROUPS, 2, ROWS, TOKENS), BF16)],
    )
    return call(place, pairs, other)


def incoming_send_kernel(place_ref, pairs_ref, send_ref, left_ref, right_ref, turned):
    core = place_ref[2]
    for block in range(BLOCKS):
        right_ref[:, block_lanes(block)] = pairs_ref[:, block, 1].reshape(HALF, COLS)
        left = pairs_ref[:, block, 0].reshape(HALF, COLS)
        turned[2 * block : 2 * block + 2] = jnp.transpose(left).reshape(2, 2, ROWS, HALF)
    left_ref[...] = turned[:, core].reshape(HALF, HALF)
    send_ref[...] = jnp.dot(
        turned[:, 1 - core].reshape(HALF, HALF), right_ref[...], preferred_element_type=F32
    ).astype(BF16)


def incoming_send(place, pairs):
    call = kernel_call(
        incoming_send_kernel,
        "incoming_send",
        [SMEM, VMEM],
        [
            jax.ShapeDtypeStruct((HALF, TOKENS), BF16),
            jax.ShapeDtypeStruct((HALF, HALF), BF16),
            jax.ShapeDtypeStruct((HALF, TOKENS), BF16),
        ],
        [pltpu.VMEM((GROUPS, 2, ROWS, HALF), BF16)],
    )
    return call(place, pairs)


def incoming_kernel(left_ref, right_ref, other_ref, out_ref):
    left = left_ref[...]
    for block in range(0, BLOCKS, 2):
        lanes = slice(block * COLS, (block + 2) * COLS)
        total = jnp.dot(left, right_ref[:, lanes], preferred_element_type=F32)
        product = (total + other_ref[:, lanes].astype(F32)).astype(BF16)
        for half in range(2):
            out_ref[:, block + half] = product[:, block_lanes(half)].reshape(GROUPS, ROWS, COLS)


def incoming(left, right, other):
    return kernel_call(incoming_kernel, "incoming", [VMEM, VMEM, VMEM], PRODUCT)(left, right, other)


def exchange(values):
    return lax.all_to_all(values, PEERS, split_axis=0, concat_axis=0, tiled=True)


def to_other_core(values):
    return lax.ppermute(values, "c", [(0, 1), (1, 0)])


def per_device(pair_input, token_mask, in_gain, proj_weight, gate_weight, out_gain, out_weight):
    place = jnp.stack(
        [lax.axis_index(("xh", "z", "c")) * ROWS, lax.axis_index(("xl", "y")), lax.axis_index("c")]
    ).astype(jnp.int32)
    masks = (place, token_mask, token_mask.reshape(BLOCKS, COLS))
    proj = jnp.swapaxes(proj_weight, 1, 2)

    pairs = exchange(project(*masks, in_gain, pair_input, proj[0])).reshape(GROUPS, BLOCKS, 2, ROWS, COLS)
    other = to_other_core(pairs[:, :, 1])
    gate = output_gate(0, in_gain, pair_input, gate_weight)
    product, gate = lax.optimization_barrier((outgoing(place, pairs, other), gate))
    hidden = exchange(product.reshape(CHAN, ROWS, COLS))
    cells, pairs = finish_project(
        *masks, in_gain, out_gain, hidden, pair_input, gate, out_weight, proj[1]
    )

    pairs = exchange(pairs).reshape(GROUPS, BLOCKS, 2, ROWS, COLS)
    send, left, right = incoming_send(place, pairs)
    other = to_other_core(send)
    gate = output_gate(1, in_gain, cells, gate_weight)
    product, gate = lax.optimization_barrier((incoming(left, right, other), gate))
    hidden = exchange(product.reshape(CHAN, ROWS, COLS))
    return finish(out_gain, hidden, cells, gate, out_weight)


def solution(mesh):
    split = Mesh(mesh.devices.reshape(2, 8, 2, 2, 4), ("xh", "z", "c", "xl", "y"))
    cells = P(("xh", "z", "c"), ("xl", "y"), None)
    return jax.shard_map(
        per_device, mesh=split, in_specs=(cells, P(), P(), P(), P(), P(), P()), out_specs=cells, check_vma=False
    )
```

time: 476 us -> 232 us (0.49)
  waiting for transfers between devices: 173 us -> 1.73 us
  starting transfers between devices: 32.3 us -> 7.32 us
  matrix products: 24.1 us -> 0 us
  Pallas kernels: 0 us -> 20.3 us
  local copies, waits for them, and re-layouts: 21.4 us -> 4.22 us
  between operations: 13.8 us -> 0.16 us
  other arithmetic: 8.04 us -> 0.08 us
    all_gather x2 -> x0, waiting for transfers between devices: 122 us -> none  [triangle(): lax.all_gather(right_split, 'col', axis=2, tiled=True)]
    all_to_all x2 -> x0, waiting for transfers between devices: 51.1 us -> none  [triangle(): lax.all_to_all(product, 'row', split_axis=1, concat_axis=0, tiled=True)]
    all_to_all x2 -> x0, starting transfers between devices: 32.1 us -> none  [triangle(): lax.all_to_all(product, 'row', split_axis=1, concat_axis=0, tiled=True)]
    dot_general x10 -> x0, matrix products: 24.1 us -> none  [the longest x4 7.22 us: gated_proj(): jnp.einsum('rqc,ce->erq', normed, weights, preferred_element_type=jnp.flo...]
    pallas_call x0 -> x8, Pallas kernels: none -> 20.3 us  [the longest x1 6.31 us: finish_project(): call(place, mask, mask_rows, in_gain, out_gain, hidden, cells, gate, weig...]
    convert_element_type x9 -> x0, local copies, waits for them, and re-layouts: 8.36 us -> none  [the longest x4 5.3 us: gated_proj(): (jax.nn.sigmoid(both_parts[:half_width]) * both_parts[half_width:] * pair...]
    all_to_all x14 -> x1, local copies, waits for them, and re-layouts: 8.69 us -> 0.36 us  [exchange(): lax.all_to_all(values, PEERS, split_axis=0, concat_axis=0, tiled=True)]
    ppermute x0 -> x2, starting transfers between devices: none -> 7.32 us  [to_other_core(): return lax.ppermute(values, 'c', [(0, 1), (1, 0)])]
  transfers between devices with their start and end apart: 4 -> 2, of which waited for: 4 -> 2; matrix products, arithmetic and copies ran while one was open for 2% -> 0% of each run, Pallas kernels for 0% -> 1%
where the time goes in v2:
time: 232 us; the launch traced here: 231 us
  blocking collectives  198 us (85%)
  Pallas kernels  20.3 us (9%)
  starting transfers between devices  7.32 us (3%)
  local copies, waits for them, and re-layouts  4.22 us (2%)
    all_to_all x4, blocking collectives, exchange(): lax.all_to_all(values, PEERS, split_axis=0, concat_axis=0, tiled=True)  198 us
    ppermute x2, starting transfers between devices, to_other_core(): return lax.ppermute(values, 'c', [(0, 1), (1, 0)])  7.32 us
    pallas_call x1, Pallas kernels, finish_project(): call(place, mask, mask_rows, in_gain, out_gain, hidden, cells, gate, weig...  6.31 us
  transfers between devices with their start and end apart: 2, of which 2 were waited for; matrix products, arithmetic and copies ran while one was open for 0% of the time, Pallas kernels for 1%

profile of v2, /device:TPU:1, one launch (start us, length us, event | category | flops | bytes accessed | tf_op | source)
XLA Modules:
  0.0 231.5 jit_solution(4040562204382621270)
XLA Ops:
  0.0 1.1 copy.8
  1.2 0.1 pad_add_fusion.place_ref
  1.2 0.0 copy-start
  1.3 1.2 copy-done
  2.5 0.0 copy-start.4
  2.5 0.7 copy-done.4
  3.2 0.0 copy-start.6
  3.2 0.7 copy-done.6
  3.8 3.0 %project.1 = bf16[128,2,32,128]{3,2,1,0:T(8,128)(2,1)S(1)} custom-call(s32[3]{0:T(128)S(1)} %pad_add_fusion.place_ref, s32[1024]{0:T(1024)S(1)} %copy-done.4, s32[8,128]{1,0:T(8,128)S(1)} %bitcast.20, f32[2,128]{1,0:T(2,128)S(1)} %copy-done.6, bf16[32,128,128]{2,1,0:T(8,128)(2,1)S(1)} %copy-done, bf16[512,128]{1,0:T(8,128)(2,1)S(1)} %get-tuple-element.24.weight_ref), custom_call_target="tpu_custom_call" | custom-call | tf_op jit(solution)/shard_map/project/pallas_call | solution.py:104
  6.9 68.5 %all_to_all.20 = bf16[128,2,32,128]{3,2,1,0:T(8,128)(2,1)S(1)} all-to-all(bf16[128,2,32,128]{3,2,1,0:T(8,128)(2,1)S(1)} %project.1), channel_id=1, replica_groups=mesh['xh'=2,'z'=8,'c'=2,'xl'=2,'y'=4] {'xh','z','xl','y'}, dimensions={0} | all-to-all | bytes 4194304 | tf_op jit(solution)/shard_map/all_to_all | solution.py:277
  75.3 0.4 copy.9
  75.7 0.0 copy-start.1
  75.7 0.0 copy-start.3
  75.7 0.0 copy-start.7
  75.7 0.1 slice_bitcast_fusion
  75.8 3.0 %collective-permute-start = (bf16[16,8,32,128]{3,2,1,0:T(8,128)(2,1)S(1)}, bf16[16,8,32,128]{3,2,1,0:T(8,128)(2,1)S(1)}, u32[]{:S(2)}, u32[]{:S(2)}) collective-permute-start(bf16[16,8,32,128]{3,2,1,0:T(8,128)(2,1)S(1)} %slice_bitcast_fusion), channel_id=1, source_target_pairs={{0,8},{8,0},{1,9},{9,1},{2,10},{10,2},{3,11},{11,3},{4,12},{12,4},... | collective-permute-start | bytes 3145736 | tf_op jit(solution)/shard_map/ppermute | solution.py:281
  78.8 0.0 copy-done.1
  78.8 0.0 copy-done.3
  78.8 0.0 copy-done.7
  78.8 1.4 output_gate.2.gate_ref
  80.3 0.9 collective-permute-done.other_ref
  81.1 2.5 %outgoing.1 = bf16[16,8,32,128]{3,2,1,0:T(8,128)(2,1)S(1)} custom-call(s32[3]{0:T(128)S(1)} %pad_add_fusion.place_ref, bf16[16,8,2,32,128]{4,3,2,1,0:T(8,128)(2,1)S(1)} %bitcast.16, bf16[16,8,32,128]{3,2,1,0:T(8,128)(2,1)S(1)} %collective-permute-done.other_ref), custom_call_target="tpu_custom_call" | custom-call | tf_op jit(solution)/shard_map/outgoing/pallas_call | solution.py:232
  83.6 0.0 copy-start.2
  83.6 0.0 copy-start.5
  83.6 0.0 copy-start.8
  83.6 36.3 %all_to_all.21.hidden_ref = bf16[128,32,128]{2,1,0:T(8,128)(2,1)S(1)} all-to-all(bf16[128,32,128]{2,1,0:T(8,128)(2,1)S(1)} %bitcast.19), channel_id=1, replica_groups=mesh['xh'=2,'z'=8,'c'=2,'xl'=2,'y'=4] {'xh','z','xl','y'}, dimensions={0} | all-to-all | bytes 2097152 | tf_op jit(solution)/shard_map/all_to_all | solution.py:277
  119.9 0.0 copy-done.2
  119.9 0.0 copy-done.5
  119.9 0.0 copy-done.8
  119.9 6.3 %finish_project.1 = (bf16[32,128,128]{2,1,0:T(8,128)(2,1)S(1)}, bf16[128,2,32,128]{3,2,1,0:T(8,128)(2,1)S(1)}) custom-call(s32[3]{0:T(128)S(1)} %pad_add_fusion.place_ref, s32[1024]{0:T(1024)S(1)} %copy-done.5, s32[8,128]{1,0:T(8,128)S(1)} %bitcast.21, f32[2,128]{1,0:T(2,128)S(1)} %copy-done.7, f32[2,128]{1,0:T(2,128)S(1)} %copy-done.8, ...), custom_call_target="tpu_custom_call" | custom-call | tf_op jit(solution)/shard_map/finish_project/pallas_call | solution.py:191
  126.2 56.8 %all_to_all.22 = bf16[128,2,32,128]{3,2,1,0:T(8,128)(2,1)S(1)} all-to-all(bf16[128,2,32,128]{3,2,1,0:T(8,128)(2,1)S(1)} %get-tuple-element.16), channel_id=1, replica_groups=mesh['xh'=2,'z'=8,'c'=2,'xl'=2,'y'=4] {'xh','z','xl','y'}, dimensions={0} | all-to-all | bytes 4194304 | tf_op jit(solution)/shard_map/all_to_all | solution.py:277
  183.0 1.7 incoming_send.1
  184.7 4.3 %collective-permute-start.1 = (bf16[512,1024]{1,0:T(8,128)(2,1)S(1)}, bf16[512,1024]{1,0:T(8,128)(2,1)S(1)}, u32[]{:S(2)}, u32[]{:S(2)}) collective-permute-start(bf16[512,1024]{1,0:T(8,128)(2,1)S(1)} %get-tuple-element.19), channel_id=1, source_target_pairs={{0,8},{8,0},{1,9},{9,1},{2,10},{10,2},{3,11},{11,3},{4,12},{12,4},... | collective-permute-start | bytes 3145736 | tf_op jit(solution)/shard_map/ppermute | solution.py:281
  189.0 1.4 output_gate.3.gate_ref
  190.4 0.9 collective-permute-done.1.other_ref
  191.3 0.7 incoming.1
  192.0 36.1 %all_to_all.23.hidden_ref = bf16[128,32,128]{2,1,0:T(8,128)(2,1)S(1)} all-to-all(bf16[128,32,128]{2,1,0:T(8,128)(2,1)S(1)} %bitcast.18), channel_id=1, replica_groups=mesh['xh'=2,'z'=8,'c'=2,'xl'=2,'y'=4] {'xh','z','xl','y'}, dimensions={0} | all-to-all | bytes 2097152 | tf_op jit(solution)/shard_map/all_to_all | solution.py:277
  228.2 3.3 %finish.1 = bf16[32,128,128]{2,1,0:T(8,128)(2,1)} custom-call(f32[2,128]{1,0:T(2,128)S(1)} %copy-done.8, bf16[128,32,128]{2,1,0:T(8,128)(2,1)S(1)} %all_to_all.23.hidden_ref, bf16[32,128,128]{2,1,0:T(8,128)(2,1)S(1)} %get-tuple-element.20.cells_ref, f32[32,128,128]{2,1,0:T(8,128)S(1)} %output_gate.3.gate_ref, bf16[2,128,128]{2,1,0:T(8,128)(2,1)S(1)} %copy-done.2), custom_call_target="tpu_custom_call" | custom-call | tf_op jit(solution)/shard_map/finish/pallas_call | solution.py:163
  (1 shorter events, 0.0 us)
Async XLA Ops:
  1.2 1.2 copy-start
  2.5 0.7 copy-start.4
  3.2 0.7 copy-start.6
  75.7 3.1 %copy-start.1 = (bf16[32,128,128]{2,1,0:T(8,128)(2,1)S(1)}, bf16[32,128,128]{2,1,0:T(8,128)(2,1)}, u32[]{:S(2)}) copy-start(bf16[32,128,128]{2,1,0:T(8,128)(2,1)} %cells_ref.5) | copy-start | bytes 3145732
  75.7 3.1 %copy-start.3 = (bf16[2,128,128]{2,1,0:T(8,128)(2,1)S(1)}, bf16[2,128,128]{2,1,0:T(8,128)(2,1)}, u32[]{:S(2)}) copy-start(bf16[2,128,128]{2,1,0:T(8,128)(2,1)} %weight_ref.6) | copy-start | bytes 196612
  75.7 3.1 %copy-start.7 = (f32[2,128]{1,0:T(2,128)S(1)}, f32[2,128]{1,0:T(2,128)}, u32[]{:S(2)}) copy-start(f32[2,128]{1,0:T(2,128)} %gain_ref.6) | copy-start | bytes 3076
  75.8 5.3 %collective-permute-start = (bf16[16,8,32,128]{3,2,1,0:T(8,128)(2,1)S(1)}, bf16[16,8,32,128]{3,2,1,0:T(8,128)(2,1)S(1)}, u32[]{:S(2)}, u32[]{:S(2)}) collective-permute-start(bf16[16,8,32,128]{3,2,1,0:T(8,128)(2,1)S(1)} %slice_bitcast_fusion), channel_id=1, source_target_pairs={{0,8},{8,0},{1,9},{9,1},{2,10},{10,2},{3,11},{11,3},{4,12},{12,4},... | collective-permute-start | bytes 3145736 | tf_op jit(solution)/shard_map/ppermute | solution.py:281
  83.6 36.3 %copy-start.2 = (bf16[2,128,128]{2,1,0:T(8,128)(2,1)S(1)}, bf16[2,128,128]{2,1,0:T(8,128)(2,1)}, u32[]{:S(2)}) copy-start(bf16[2,128,128]{2,1,0:T(8,128)(2,1)} %weight_ref.7) | copy-start | bytes 196612
  83.6 36.3 %copy-start.5 = (s32[1024]{0:T(1024)S(1)}, s32[1024]{0:T(1024)}, u32[]{:S(2)}) copy-start(s32[1024]{0:T(1024)} %row_mask_ref.3) | copy-start | bytes 12292
  83.6 36.3 %copy-start.8 = (f32[2,128]{1,0:T(2,128)S(1)}, f32[2,128]{1,0:T(2,128)}, u32[]{:S(2)}) copy-start(f32[2,128]{1,0:T(2,128)} %gain_ref.7) | copy-start | bytes 3076
  184.7 6.6 %collective-permute-start.1 = (bf16[512,1024]{1,0:T(8,128)(2,1)S(1)}, bf16[512,1024]{1,0:T(8,128)(2,1)S(1)}, u32[]{:S(2)}, u32[]{:S(2)}) collective-permute-start(bf16[512,1024]{1,0:T(8,128)(2,1)S(1)} %get-tuple-element.19), channel_id=1, source_target_pairs={{0,8},{8,0},{1,9},{9,1},{2,10},{10,2},{3,11},{11,3},{4,12},{12,4},... | collective-permute-start | bytes 3145736 | tf_op jit(solution)/shard_map/ppermute | solution.py:281

commit v3 on v2

--- a/solution.py
+++ b/solution.py
@@ -12,12 +12,13 @@
 ROWS = 32
 COLS = 128
 SUB = 4
+CHUNK = 8
 CHAN_PITCH = CHAN + 1
 ROW_PITCH = ROWS + 1
 PEERS = ("xh", "z", "xl", "y")
 F32 = jnp.float32
 BF16 = jnp.bfloat16
-PARAMS = pltpu.CompilerParams(vmem_limit_bytes=40 * 1024 * 1024)
+MIB = 1024 * 1024
 
 
 def sigmoid(values):
@@ -28,42 +29,50 @@
 VMEM = pl.BlockSpec(memory_space=pltpu.VMEM)
 
 
-def kernel_call(kernel, name, in_specs, out_shape, scratch_shapes=(), cost=None):
+def kernel_call(kernel, name, in_specs, out_shape, scratch_shapes=(), cost=None, vmem=40):
     return pl.pallas_call(
         kernel,
         in_specs=in_specs,
         out_specs=jax.tree.map(lambda _: VMEM, out_shape),
         out_shape=out_shape,
         scratch_shapes=scratch_shapes,
-        compiler_params=PARAMS,
+        compiler_params=pltpu.CompilerParams(vmem_limit_bytes=vmem * MIB),
         cost_estimate=cost,
         name=name,
     )
 
 
-def layer_norm_lanes(cells, factor):
-    average = jnp.mean(cells, axis=-1, keepdims=True)
-    centred = cells - average
-    variance = jnp.mean(centred * centred, axis=-1, keepdims=True)
+HBM = pl.BlockSpec(memory_space=pltpu.HBM)
+PROJ_SCRATCH = [pltpu.VMEM((ROWS * CHAN_PITCH, COLS), F32)] * 2
+HIDDEN_SCRATCH = pltpu.VMEM((CHAN * ROW_PITCH, COLS), F32)
+PAIRS = jax.ShapeDtypeStruct((CHAN, 2, ROWS, COLS), BF16)
+CELLS = jax.ShapeDtypeStruct((ROWS, COLS, CHAN), BF16)
+TURNED = jax.ShapeDtypeStruct((ROWS, CHAN, COLS), BF16)
+GATE = jax.ShapeDtypeStruct((ROWS, CHAN, COLS), F32)
+
+
+def layer_norm(turned, factor):
+    average = jnp.mean(turned, axis=0, keepdims=True)
+    centred = turned - average
+    variance = jnp.mean(centred * centred, axis=0, keepdims=True)
     return centred * lax.rsqrt(variance + EPSILON) * factor
 
 
+def channel_column(gain_ref, module):
+    return jnp.transpose(jnp.broadcast_to(gain_ref[module : module + 1, :], (COLS, CHAN)))
+
+
 def masked_gain(place_ref, gain_ref, module, col_mask_ref):
-    cols = col_mask_ref[pl.ds(place_ref[1], 1), :].astype(F32)
-    return jnp.transpose(jnp.broadcast_to(cols, (CHAN, COLS))) * gain_ref[module : module + 1, :]
+    return channel_column(gain_ref, module) * col_mask_ref[pl.ds(place_ref[1], 1), :].astype(F32)
 
 
 def row_mask(place_ref, row_mask_ref, index):
     return row_mask_ref[place_ref[0] + index].astype(F32)
 
 
-def project_rows(rows, row_masks, gain_mask, weight_ref, left_scratch, right_scratch, first):
-    normed = [
-        layer_norm_lanes(row, gain_mask * mask).astype(BF16) for row, mask in zip(rows, row_masks)
-    ]
-    projected = lax.dot_general(
-        weight_ref[...], jnp.concatenate(normed, axis=0), (((1,), (1,)), ((), ())), preferred_element_type=F32
-    )
+def project_rows(rows, row_masks, gain_mask, weight, left_scratch, right_scratch, first):
+    normed = [layer_norm(row, gain_mask * mask).astype(BF16) for row, mask in zip(rows, row_masks)]
+    projected = jnp.dot(weight[...], jnp.concatenate(normed, axis=1), preferred_element_type=F32)
     left = sigmoid(projected[:CHAN]) * projected[CHAN : 2 * CHAN]
     right = sigmoid(projected[2 * CHAN : 3 * CHAN]) * projected[3 * CHAN :]
     for index in range(len(rows)):
@@ -83,33 +92,68 @@
     lax.fori_loop(0, CHAN, body, 0, unroll=8)
 
 
-def project_kernel(place_ref, row_mask_ref, col_mask_ref, gain_ref, cells_ref, weight_ref, out_ref, left, right):
+def project_kernel(
+    place_ref, row_mask_ref, col_mask_hbm, gain_hbm, cells_hbm, weight_hbm, out_ref, turned_out,
+    cells_ref, weight_ref, col_mask_ref, gain_ref, weight_turned, left, right, sems,
+):
+    cell_copies = [
+        pltpu.make_async_copy(
+            cells_hbm.at[pl.ds(first, CHUNK)], cells_ref.at[pl.ds(first, CHUNK)], sems.at[first // CHUNK]
+        )
+        for first in range(0, ROWS, CHUNK)
+    ]
+    small_copies = [
+        pltpu.make_async_copy(weight_hbm.at[0], weight_ref, sems.at[ROWS // CHUNK]),
+        pltpu.make_async_copy(col_mask_hbm, col_mask_ref, sems.at[ROWS // CHUNK + 1]),
+        pltpu.make_async_copy(gain_hbm, gain_ref, sems.at[ROWS // CHUNK + 2]),
+    ]
+    for copy in small_copies + cell_copies:
+        copy.start()
+    for copy in small_copies:
+        copy.wait()
     gain_mask = masked_gain(place_ref, gain_ref, 0, col_mask_ref)
+    weight_turned[...] = jnp.transpose(weight_ref[...])
     for first in range(0, ROWS, SUB):
-        rows = [cells_ref[first + index].astype(F32) for index in range(SUB)]
+        if first % CHUNK == 0:
+            cell_copies[first // CHUNK].wait()
+        rows = []
+        for index in range(first, first + SUB):
+            row = jnp.transpose(cells_ref[index])
+            turned_out[index] = row
+            rows.append(row.astype(F32))
         masks = [row_mask(place_ref, row_mask_ref, first + index) for index in range(SUB)]
-        project_rows(rows, masks, gain_mask, weight_ref, left, right, first)
+        project_rows(rows, masks, gain_mask, weight_turned, left, right, first)
     emit_projections(left, right, out_ref)
 
 
-PROJ_SCRATCH = [pltpu.VMEM((ROWS * CHAN_PITCH, COLS), F32)] * 2
-PAIRS = jax.ShapeDtypeStruct((CHAN, 2, ROWS, COLS), BF16)
-CELLS = jax.ShapeDtypeStruct((ROWS, COLS, CHAN), BF16)
-
-
 def project(place, mask, mask_rows, gain, cells, weight):
     call = kernel_call(
-        project_kernel, "project", [SMEM, SMEM, VMEM, VMEM, VMEM, VMEM], PAIRS, PROJ_SCRATCH
+        project_kernel,
+        "project",
+        [SMEM, SMEM, HBM, HBM, HBM, HBM],
+        [PAIRS, TURNED],
+        [
+            pltpu.VMEM((ROWS, COLS, CHAN), BF16),
+            pltpu.VMEM((CHAN, 4 * CHAN), BF16),
+            pltpu.VMEM(mask_rows.shape, jnp.int32),
+            pltpu.VMEM(gain.shape, F32),
+            pltpu.VMEM((4 * CHAN, CHAN), BF16),
+        ]
+        + PROJ_SCRATCH
+        + [pltpu.SemaphoreType.DMA((ROWS // CHUNK + 3,))],
+        vmem=56,
     )
     return call(place, mask, mask_rows, gain, cells, weight)
 
 
 def gate_kernel(module, gain_ref, cells_ref, weight_ref, out_ref):
+    gain = channel_column(gain_ref, module)
+    weight = jnp.transpose(weight_ref[module])
     for first in range(0, ROWS, SUB):
-        cells = cells_ref[first : first + SUB].astype(F32).reshape(SUB * COLS, CHAN)
-        normed = layer_norm_lanes(cells, gain_ref[module : module + 1, :]).astype(BF16)
-        gate = sigmoid(jnp.dot(normed, weight_ref[module], preferred_element_type=F32))
-        out_ref[first : first + SUB] = gate.reshape(SUB, COLS, CHAN)
+        rows = [layer_norm(cells_ref[first + index].astype(F32), gain).astype(BF16) for index in range(SUB)]
+        gate = sigmoid(jnp.dot(weight, jnp.concatenate(rows, axis=1), preferred_element_type=F32))
+        for index in range(SUB):
+            out_ref[first + index] = gate[:, index * COLS : (index + 1) * COLS]
 
 
 def output_gate(module, gain, cells, weight):
@@ -117,7 +161,7 @@
         functools.partial(gate_kernel, module),
         "output_gate",
         [VMEM, VMEM, VMEM],
-        jax.ShapeDtypeStruct((ROWS, COLS, CHAN), F32),
+        GATE,
         cost=pl.CostEstimate(
             flops=2 * ROWS * COLS * CHAN * CHAN, bytes_accessed=3 << 20, transcendentals=ROWS * COLS * CHAN
         ),
@@ -141,42 +185,66 @@
         lax.fori_loop(0, CHAN, body, 0, unroll=8)
 
 
-def updated_row(module, index, scratch, weight_ref, cells_ref, gate_ref):
-    hidden = scratch[pl.ds(index, CHAN, stride=ROW_PITCH), :].astype(BF16)
-    update = lax.dot_general(
-        hidden, weight_ref[module], (((0,), (0,)), ((), ())), preferred_element_type=F32
-    )
-    return (cells_ref[index].astype(F32) + gate_ref[index] * update).astype(BF16)
-
-
-HIDDEN_SCRATCH = pltpu.VMEM((CHAN * ROW_PITCH, COLS), F32)
-
-
-def finish_kernel(gain_ref, hidden_ref, cells_ref, gate_ref, weight_ref, out_ref, scratch):
+def updated_rows(first, scratch, weight, cells_ref, gate_ref):
+    hidden = [
+        scratch[pl.ds(first + index, CHAN, stride=ROW_PITCH), :].astype(BF16) for index in range(SUB)
+    ]
+    update = jnp.dot(weight, jnp.concatenate(hidden, axis=1), preferred_element_type=F32)
+    return [
+        (
+            cells_ref[first + index].astype(F32)
+            + gate_ref[first + index] * update[:, index * COLS : (index + 1) * COLS]
+        ).astype(BF16)
+        for index in range(SUB)
+    ]
+
+
+def finish_kernel(gain_ref, hidden_ref, cells_ref, gate_ref, weight_ref, out_hbm, scratch, out_ref, sems):
     normed_hidden_rows(1, gain_ref, hidden_ref, scratch)
-    for index in range(ROWS):
-        out_ref[index] = updated_row(1, index, scratch, weight_ref, cells_ref, gate_ref)
+    weight = jnp.transpose(weight_ref[1])
+    copies = []
+    for first in range(0, ROWS, SUB):
+        for index, row in enumerate(updated_rows(first, scratch, weight, cells_ref, gate_ref)):
+            out_ref[first + index] = jnp.transpose(row)
+        if (first + SUB) % CHUNK == 0:
+            rows = pl.ds(first + SUB - CHUNK, CHUNK)
+            copies.append(pltpu.make_async_copy(out_ref.at[rows], out_hbm.at[rows], sems.at[first // CHUNK]))
+            copies[-1].start()
+    for copy in copies:
+        copy.wait()
 
 
 def finish(gain, hidden, cells, gate, weight):
-    call = kernel_call(finish_kernel, "finish", [SMEM, VMEM, VMEM, VMEM, VMEM], CELLS, [HIDDEN_SCRATCH])
-    return call(gain, hidden, cells, gate, weight)
+    return pl.pallas_call(
+        finish_kernel,
+        in_specs=[SMEM, VMEM, VMEM, VMEM, VMEM],
+        out_specs=HBM,
+        out_shape=CELLS,
+        scratch_shapes=[
+            HIDDEN_SCRATCH,
+            pltpu.VMEM((ROWS, COLS, CHAN), BF16),
+            pltpu.SemaphoreType.DMA((ROWS // CHUNK,)),
+        ],
+        compiler_params=pltpu.CompilerParams(vmem_limit_bytes=40 * MIB),
+        name="finish",
+    )(gain, hidden, cells, gate, weight)
 
 
 def finish_project_kernel(
     place_ref, row_mask_ref, col_mask_ref, in_gain_ref, out_gain_ref, hidden_ref, cells_ref, gate_ref,
-    weight_ref, proj_ref, cells_out, pairs_out, scratch, left, right,
+    weight_ref, proj_ref, cells_out, pairs_out, scratch, proj_turned, left, right,
 ):
     gain_mask = masked_gain(place_ref, in_gain_ref, 1, col_mask_ref)
     normed_hidden_rows(0, out_gain_ref, hidden_ref, scratch)
+    weight = jnp.transpose(weight_ref[0])
+    proj_turned[...] = jnp.transpose(proj_ref[1])
     for first in range(0, ROWS, SUB):
-        rows = []
-        for index in range(first, first + SUB):
-            row = updated_row(0, index, scratch, weight_ref, cells_ref, gate_ref)
-            cells_out[index] = row
-            rows.append(row.astype(F32))
+        rows = updated_rows(first, scratch, weight, cells_ref, gate_ref)
+        for index, row in enumerate(rows):
+            cells_out[first + index] = row
         masks = [row_mask(place_ref, row_mask_ref, first + index) for index in range(SUB)]
-        project_rows(rows, masks, gain_mask, proj_ref, left, right, first)
+        rows = [row.astype(F32) for row in rows]
+        project_rows(rows, masks, gain_mask, proj_turned, left, right, first)
     emit_projections(left, right, pairs_out)
 
 
@@ -185,8 +253,8 @@
         finish_project_kernel,
         "finish_project",
         [SMEM, SMEM, VMEM, VMEM, SMEM] + [VMEM] * 5,
-        [CELLS, PAIRS],
-        [HIDDEN_SCRATCH] + PROJ_SCRATCH,
+        [TURNED, PAIRS],
+        [HIDDEN_SCRATCH, pltpu.VMEM((4 * CHAN, CHAN), BF16)] + PROJ_SCRATCH,
     )
     return call(place, mask, mask_rows, in_gain, out_gain, hidden, cells, gate, weight, proj)
 
@@ -286,16 +354,14 @@
         [lax.axis_index(("xh", "z", "c")) * ROWS, lax.axis_index(("xl", "y")), lax.axis_index("c")]
     ).astype(jnp.int32)
     masks = (place, token_mask, token_mask.reshape(BLOCKS, COLS))
-    proj = jnp.swapaxes(proj_weight, 1, 2)
-
-    pairs = exchange(project(*masks, in_gain, pair_input, proj[0])).reshape(GROUPS, BLOCKS, 2, ROWS, COLS)
+
+    pairs, cells = project(*masks, in_gain, pair_input, proj_weight)
+    pairs = exchange(pairs).reshape(GROUPS, BLOCKS, 2, ROWS, COLS)
     other = to_other_core(pairs[:, :, 1])
-    gate = output_gate(0, in_gain, pair_input, gate_weight)
+    gate = output_gate(0, in_gain, cells, gate_weight)
     product, gate = lax.optimization_barrier((outgoing(place, pairs, other), gate))
     hidden = exchange(product.reshape(CHAN, ROWS, COLS))
-    cells, pairs = finish_project(
-        *masks, in_gain, out_gain, hidden, pair_input, gate, out_weight, proj[1]
-    )
+    cells, pairs = finish_project(*masks, in_gain, out_gain, hidden, cells, gate, out_weight, proj_weight)
 
     pairs = exchange(pairs).reshape(GROUPS, BLOCKS, 2, ROWS, COLS)
     send, left, right = incoming_send(place, pairs)

time: 232 us -> 231 us (level)
  local copies, waits for them, and re-layouts: 4.22 us -> 0.49 us
    unnamed x19 -> x16, local copies, waits for them, and re-layouts: 3.74 us -> 0.05 us
    pallas_call x1, Pallas kernels: 3 us -> 6.32 us  [project(): return call(place, mask, mask_rows, gain, cells, weight)]
where the time goes in v3:
time: 231 us
  blocking collectives  198 us (86%)
  Pallas kernels  21.7 us (9%)
  starting transfers between devices  7.32 us (3%)
  waiting for transfers between devices  2.45 us (1%)
    all_to_all x4, blocking collectives, exchange(): lax.all_to_all(values, PEERS, split_axis=0, concat_axis=0, tiled=True)  198 us
    ppermute x2, starting transfers between devices, to_other_core(): return lax.ppermute(values, 'c', [(0, 1), (1, 0)])  7.32 us
    pallas_call x1, Pallas kernels, project(): return call(place, mask, mask_rows, gain, cells, weight)  6.32 us
    pallas_call x1, Pallas kernels, finish_project(): call(place, mask, mask_rows, in_gain, out_gain, hidden, cells, gate, weig...  5.25 us
  transfers between devices with their start and end apart: 2, of which 2 were waited for; matrix products, arithmetic and copies ran while one was open for 0% of the time, Pallas kernels for 1%

profile of v3, /device:TPU:1, one launch (start us, length us, event | category | flops | bytes accessed | tf_op | source)
XLA Modules:
  0.0 230.8 jit_solution(17837376288632675919)
XLA Ops:
  0.0 0.6 pad_add_fusion.place_ref
  0.6 6.3 %project.1 = (bf16[128,2,32,128]{3,2,1,0:T(8,128)(2,1)}, bf16[32,128,128]{2,1,0:T(8,128)(2,1)}) custom-call(s32[3]{0:T(128)} %pad_add_fusion.place_ref, s32[1024]{0:T(1024)} %row_mask_ref.3, s32[8,128]{1,0:T(8,128)} %bitcast.15, f32[2,128]{1,0:T(2,128)} %gain_ref.4, bf16[32,128,128]{2,1,0:T(8,128)(2,1)} %cells_hbm.1, bf16[2,128,512]{2,1,0:T(8,128)(2,1)} %proj_ref.1), custom_call_target="tpu_custom_call" | custom-call | tf_op jit(solution)/shard_map/project/pallas_call | solution.py:146
  6.9 68.7 %all_to_all.20 = bf16[128,2,32,128]{3,2,1,0:T(8,128)(2,1)S(1)} all-to-all(bf16[128,2,32,128]{3,2,1,0:T(8,128)(2,1)} %get-tuple-element.16), channel_id=1, replica_groups=mesh['xh'=2,'z'=8,'c'=2,'xl'=2,'y'=4] {'xh','z','xl','y'}, dimensions={0} | all-to-all | bytes 4194304 | tf_op jit(solution)/shard_map/all_to_all | solution.py:345
  75.6 0.4 copy.8
  76.0 0.0 copy-start
  76.0 0.0 copy-start.3
  76.0 0.0 copy-start.5
  76.0 0.1 slice_bitcast_fusion
  76.1 0.0 copy-start.6
  76.1 3.0 %collective-permute-start = (bf16[16,8,32,128]{3,2,1,0:T(8,128)(2,1)S(1)}, bf16[16,8,32,128]{3,2,1,0:T(8,128)(2,1)S(1)}, u32[]{:S(2)}, u32[]{:S(2)}) collective-permute-start(bf16[16,8,32,128]{3,2,1,0:T(8,128)(2,1)S(1)} %slice_bitcast_fusion), channel_id=1, source_target_pairs={{0,8},{8,0},{1,9},{9,1},{2,10},{10,2},{3,11},{11,3},{4,12},{12,4},... | collective-permute-start | bytes 3145736 | tf_op jit(solution)/shard_map/ppermute | solution.py:349
  79.1 0.0 copy-done
  79.1 0.0 copy-done.3
  79.1 0.0 copy-done.5
  79.1 1.1 output_gate.2.gate_ref
  80.1 1.2 collective-permute-done.other_ref
  81.4 0.0 copy-done.6
  81.4 2.5 %outgoing.1 = bf16[16,8,32,128]{3,2,1,0:T(8,128)(2,1)S(1)} custom-call(s32[3]{0:T(128)S(1)} %copy-done.6, bf16[16,8,2,32,128]{4,3,2,1,0:T(8,128)(2,1)S(1)} %bitcast.11, bf16[16,8,32,128]{3,2,1,0:T(8,128)(2,1)S(1)} %collective-permute-done.other_ref), custom_call_target="tpu_custom_call" | custom-call | tf_op jit(solution)/shard_map/outgoing/pallas_call | solution.py:300
  83.8 0.0 copy-start.1
  83.8 0.0 copy-start.2
  83.9 0.0 copy-start.4
  83.9 0.0 copy-start.7
  83.9 36.3 %all_to_all.21.hidden_ref = bf16[128,32,128]{2,1,0:T(8,128)(2,1)S(1)} all-to-all(bf16[128,32,128]{2,1,0:T(8,128)(2,1)S(1)} %bitcast.14), channel_id=1, replica_groups=mesh['xh'=2,'z'=8,'c'=2,'xl'=2,'y'=4] {'xh','z','xl','y'}, dimensions={0} | all-to-all | bytes 2097152 | tf_op jit(solution)/shard_map/all_to_all | solution.py:345
  120.2 0.0 copy-done.1
  120.2 0.0 copy-done.2
  120.2 0.0 copy-done.4
  120.2 0.0 copy-done.7
  120.2 5.2 %finish_project.1 = (bf16[32,128,128]{2,1,0:T(8,128)(2,1)S(1)}, bf16[128,2,32,128]{3,2,1,0:T(8,128)(2,1)S(1)}) custom-call(s32[3]{0:T(128)S(1)} %copy-done.6, s32[1024]{0:T(1024)S(1)} %copy-done.4, s32[8,128]{1,0:T(8,128)S(1)} %bitcast.16, f32[2,128]{1,0:T(2,128)S(1)} %copy-done.5, f32[2,128]{1,0:T(2,128)S(1)} %copy-done.7, ...), custom_call_target="tpu_custom_call" | custom-call | tf_op jit(solution)/shard_map/finish_project/pallas_call | solution.py:259
  125.4 56.8 %all_to_all.22 = bf16[128,2,32,128]{3,2,1,0:T(8,128)(2,1)S(1)} all-to-all(bf16[128,2,32,128]{3,2,1,0:T(8,128)(2,1)S(1)} %get-tuple-element.20), channel_id=1, replica_groups=mesh['xh'=2,'z'=8,'c'=2,'xl'=2,'y'=4] {'xh','z','xl','y'}, dimensions={0} | all-to-all | bytes 4194304 | tf_op jit(solution)/shard_map/all_to_all | solution.py:345
  182.3 1.6 incoming_send.1
  183.9 4.3 %collective-permute-start.1 = (bf16[512,1024]{1,0:T(8,128)(2,1)S(1)}, bf16[512,1024]{1,0:T(8,128)(2,1)S(1)}, u32[]{:S(2)}, u32[]{:S(2)}) collective-permute-start(bf16[512,1024]{1,0:T(8,128)(2,1)S(1)} %get-tuple-element.23), channel_id=1, source_target_pairs={{0,8},{8,0},{1,9},{9,1},{2,10},{10,2},{3,11},{11,3},{4,12},{12,4},... | collective-permute-start | bytes 3145736 | tf_op jit(solution)/shard_map/ppermute | solution.py:349
  188.2 1.0 output_gate.3.gate_ref
  189.3 1.2 collective-permute-done.1.other_ref
  190.5 0.7 incoming.1
  191.3 36.1 %all_to_all.23.hidden_ref = bf16[128,32,128]{2,1,0:T(8,128)(2,1)S(1)} all-to-all(bf16[128,32,128]{2,1,0:T(8,128)(2,1)S(1)} %bitcast.13), channel_id=1, replica_groups=mesh['xh'=2,'z'=8,'c'=2,'xl'=2,'y'=4] {'xh','z','xl','y'}, dimensions={0} | all-to-all | bytes 2097152 | tf_op jit(solution)/shard_map/all_to_all | solution.py:345
  227.4 3.2 %finish.1 = bf16[32,128,128]{2,1,0:T(8,128)(2,1)} custom-call(f32[2,128]{1,0:T(2,128)S(1)} %copy-done.7, bf16[128,32,128]{2,1,0:T(8,128)(2,1)S(1)} %all_to_all.23.hidden_ref, bf16[32,128,128]{2,1,0:T(8,128)(2,1)S(1)} %get-tuple-element.24.cells_ref, f32[32,128,128]{2,1,0:T(8,128)S(1)} %output_gate.3.gate_ref, bf16[2,128,128]{2,1,0:T(8,128)(2,1)S(1)} %copy-done.2), custom_call_target="tpu_custom_call" | custom-call | tf_op jit(solution)/shard_map/finish/pallas_call | solution.py:218
Async XLA Ops:
  76.0 3.1 %copy-start = (bf16[32,128,128]{2,1,0:T(8,128)(2,1)S(1)}, bf16[32,128,128]{2,1,0:T(8,128)(2,1)}, u32[]{:S(2)}) copy-start(bf16[32,128,128]{2,1,0:T(8,128)(2,1)} %get-tuple-element.17.cells_ref) | copy-start | bytes 3145732
  76.0 3.1 %copy-start.3 = (bf16[2,128,128]{2,1,0:T(8,128)(2,1)S(1)}, bf16[2,128,128]{2,1,0:T(8,128)(2,1)}, u32[]{:S(2)}) copy-start(bf16[2,128,128]{2,1,0:T(8,128)(2,1)} %weight_ref.6) | copy-start | bytes 196612
  76.0 3.1 %copy-start.5 = (f32[2,128]{1,0:T(2,128)S(1)}, f32[2,128]{1,0:T(2,128)}, u32[]{:S(2)}) copy-start(f32[2,128]{1,0:T(2,128)} %gain_ref.4) | copy-start | bytes 3076
  76.1 5.3 %copy-start.6 = (s32[3]{0:T(128)S(1)}, s32[3]{0:T(128)}, u32[]{:S(2)}) copy-start(s32[3]{0:T(128)} %pad_add_fusion.place_ref) | copy-start | bytes 40
  76.1 5.3 %collective-permute-start = (bf16[16,8,32,128]{3,2,1,0:T(8,128)(2,1)S(1)}, bf16[16,8,32,128]{3,2,1,0:T(8,128)(2,1)S(1)}, u32[]{:S(2)}, u32[]{:S(2)}) collective-permute-start(bf16[16,8,32,128]{3,2,1,0:T(8,128)(2,1)S(1)} %slice_bitcast_fusion), channel_id=1, source_target_pairs={{0,8},{8,0},{1,9},{9,1},{2,10},{10,2},{3,11},{11,3},{4,12},{12,4},... | collective-permute-start | bytes 3145736 | tf_op jit(solution)/shard_map/ppermute | solution.py:349
  83.8 36.3 %copy-start.1 = (bf16[2,128,512]{2,1,0:T(8,128)(2,1)S(1)}, bf16[2,128,512]{2,1,0:T(8,128)(2,1)}, u32[]{:S(2)}) copy-start(bf16[2,128,512]{2,1,0:T(8,128)(2,1)} %proj_ref.1) | copy-start | bytes 786436
  83.8 36.3 %copy-start.2 = (bf16[2,128,128]{2,1,0:T(8,128)(2,1)S(1)}, bf16[2,128,128]{2,1,0:T(8,128)(2,1)}, u32[]{:S(2)}) copy-start(bf16[2,128,128]{2,1,0:T(8,128)(2,1)} %weight_ref.7) | copy-start | bytes 196612
  83.9 36.3 %copy-start.4 = (s32[1024]{0:T(1024)S(1)}, s32[1024]{0:T(1024)}, u32[]{:S(2)}) copy-start(s32[1024]{0:T(1024)} %row_mask_ref.3) | copy-start | bytes 12292
  83.9 36.3 %copy-start.7 = (f32[2,128]{1,0:T(2,128)S(1)}, f32[2,128]{1,0:T(2,128)}, u32[]{:S(2)}) copy-start(f32[2,128]{1,0:T(2,128)} %gain_ref.5) | copy-start | bytes 3076
  183.9 6.6 %collective-permute-start.1 = (bf16[512,1024]{1,0:T(8,128)(2,1)S(1)}, bf16[512,1024]{1,0:T(8,128)(2,1)S(1)}, u32[]{:S(2)}, u32[]{:S(2)}) collective-permute-start(bf16[512,1024]{1,0:T(8,128)(2,1)S(1)} %get-tuple-element.23), channel_id=1, source_target_pairs={{0,8},{8,0},{1,9},{9,1},{2,10},{10,2},{3,11},{11,3},{4,12},{12,4},... | collective-permute-start | bytes 3145736 | tf_op jit(solution)/shard_map/ppermute | solution.py:349

commit v4 on v3

--- a/solution.py
+++ b/solution.py
@@ -11,8 +11,9 @@
 CHAN = 128
 ROWS = 32
 COLS = 128
-SUB = 4
-CHUNK = 8
+SUB = 16
+CHUNK = 16
+SPAN = 32
 CHAN_PITCH = CHAN + 1
 ROW_PITCH = ROWS + 1
 PEERS = ("xh", "z", "xl", "y")
@@ -25,7 +26,6 @@
     return 0.5 * jnp.tanh(0.5 * values) + 0.5
 
 
-SMEM = pl.BlockSpec(memory_space=pltpu.SMEM)
 VMEM = pl.BlockSpec(memory_space=pltpu.VMEM)
 
 
@@ -43,8 +43,8 @@
 
 
 HBM = pl.BlockSpec(memory_space=pltpu.HBM)
-PROJ_SCRATCH = [pltpu.VMEM((ROWS * CHAN_PITCH, COLS), F32)] * 2
-HIDDEN_SCRATCH = pltpu.VMEM((CHAN * ROW_PITCH, COLS), F32)
+PROJ_SCRATCH = [pltpu.VMEM((COLS, COLS), F32)] + [pltpu.VMEM((ROWS * CHAN_PITCH, COLS), F32)] * 2
+HIDDEN_SCRATCH = [pltpu.VMEM((CHAN, COLS), F32), pltpu.VMEM((CHAN * ROW_PITCH, COLS), F32)]
 PAIRS = jax.ShapeDtypeStruct((CHAN, 2, ROWS, COLS), BF16)
 CELLS = jax.ShapeDtypeStruct((ROWS, COLS, CHAN), BF16)
 TURNED = jax.ShapeDtypeStruct((ROWS, CHAN, COLS), BF16)
@@ -62,12 +62,20 @@
     return jnp.transpose(jnp.broadcast_to(gain_ref[module : module + 1, :], (COLS, CHAN)))
 
 
-def masked_gain(place_ref, gain_ref, module, col_mask_ref):
-    return channel_column(gain_ref, module) * col_mask_ref[pl.ds(place_ref[1], 1), :].astype(F32)
-
-
-def row_mask(place_ref, row_mask_ref, index):
-    return row_mask_ref[place_ref[0] + index].astype(F32)
+def masked_gain(gain_ref, module, col_mask_ref):
+    block = lax.axis_index(("xl", "y"))
+    return channel_column(gain_ref, module) * col_mask_ref[pl.ds(block, 1), :].astype(F32)
+
+
+def set_row_masks(mask_ref, scratch):
+    block = lax.axis_index(("xh", "z", "c")) // (COLS // ROWS)
+    tokens = jnp.broadcast_to(mask_ref[pl.ds(block, 1), :].astype(F32), (COLS, COLS))
+    scratch[...] = jnp.transpose(tokens)
+
+
+def row_mask(scratch, index):
+    start = lax.axis_index(("xh", "z", "c")) % (COLS // ROWS) * ROWS
+    return scratch[pl.ds(start + index, 1), :]
 
 
 def project_rows(rows, row_masks, gain_mask, weight, left_scratch, right_scratch, first):
@@ -82,36 +90,41 @@
         right_scratch[place, :] = right[:, lanes]
 
 
-def emit_projections(left_scratch, right_scratch, out_ref):
+def emit_projections(left_scratch, right_scratch, out_ref, first=0, count=CHAN):
     def body(chan, carry):
         place = pl.ds(chan, ROWS, stride=CHAN_PITCH)
         out_ref[chan, 0] = left_scratch[place, :].astype(BF16)
         out_ref[chan, 1] = right_scratch[place, :].astype(BF16)
         return carry
 
-    lax.fori_loop(0, CHAN, body, 0, unroll=8)
+    lax.fori_loop(first, first + count, body, 0, unroll=8)
 
 
 def project_kernel(
-    place_ref, row_mask_ref, col_mask_hbm, gain_hbm, cells_hbm, weight_hbm, out_ref, turned_out,
-    cells_ref, weight_ref, col_mask_ref, gain_ref, weight_turned, left, right, sems,
+    mask_hbm, gain_hbm, cells_hbm, weight_hbm, pairs_hbm, turned_hbm,
+    cells_ref, weight_ref, mask_ref, gain_ref, weight_turned, row_masks, left, right, pairs_ref, turned_ref, sems,
 ):
+    chunks = ROWS // CHUNK
+    rows_of = [pl.ds(index * CHUNK, CHUNK) for index in range(chunks)]
+    small_copies = [
+        pltpu.make_async_copy(weight_hbm.at[0], weight_ref, sems.at[0]),
+        pltpu.make_async_copy(mask_hbm, mask_ref, sems.at[1]),
+        pltpu.make_async_copy(gain_hbm, gain_ref, sems.at[2]),
+    ]
     cell_copies = [
-        pltpu.make_async_copy(
-            cells_hbm.at[pl.ds(first, CHUNK)], cells_ref.at[pl.ds(first, CHUNK)], sems.at[first // CHUNK]
-        )
-        for first in range(0, ROWS, CHUNK)
+        pltpu.make_async_copy(cells_hbm.at[rows], cells_ref.at[rows], sems.at[3 + index])
+        for index, rows in enumerate(rows_of)
     ]
-    small_copies = [
-        pltpu.make_async_copy(weight_hbm.at[0], weight_ref, sems.at[ROWS // CHUNK]),
-        pltpu.make_async_copy(col_mask_hbm, col_mask_ref, sems.at[ROWS // CHUNK + 1]),
-        pltpu.make_async_copy(gain_hbm, gain_ref, sems.at[ROWS // CHUNK + 2]),
+    turned_copies = [
+        pltpu.make_async_copy(turned_ref.at[rows], turned_hbm.at[rows], sems.at[3 + chunks + index])
+        for index, rows in enumerate(rows_of)
     ]
     for copy in small_copies + cell_copies:
         copy.start()
     for copy in small_copies:
         copy.wait()
-    gain_mask = masked_gain(place_ref, gain_ref, 0, col_mask_ref)
+    gain_mask = masked_gain(gain_ref, 0, mask_ref)
+    set_row_masks(mask_ref, row_masks)
     weight_turned[...] = jnp.transpose(weight_ref[...])
     for first in range(0, ROWS, SUB):
         if first % CHUNK == 0:
@@ -119,31 +132,46 @@
         rows = []
         for index in range(first, first + SUB):
             row = jnp.transpose(cells_ref[index])
-            turned_out[index] = row
+            turned_ref[index] = row
             rows.append(row.astype(F32))
-        masks = [row_mask(place_ref, row_mask_ref, first + index) for index in range(SUB)]
+        if (first + SUB) % CHUNK == 0:
+            turned_copies[first // CHUNK].start()
+        masks = [row_mask(row_masks, first + index) for index in range(SUB)]
         project_rows(rows, masks, gain_mask, weight_turned, left, right, first)
-    emit_projections(left, right, out_ref)
-
-
-def project(place, mask, mask_rows, gain, cells, weight):
-    call = kernel_call(
+    pair_copies = []
+    for first in range(0, CHAN, SPAN):
+        emit_projections(left, right, pairs_ref, first, SPAN)
+        span = pl.ds(first, SPAN)
+        pair_copies.append(
+            pltpu.make_async_copy(
+                pairs_ref.at[span], pairs_hbm.at[span], sems.at[3 + 2 * chunks + first // SPAN]
+            )
+        )
+        pair_copies[-1].start()
+    for copy in turned_copies + pair_copies:
+        copy.wait()
+
+
+def project(mask, gain, cells, weight):
+    return pl.pallas_call(
         project_kernel,
-        "project",
-        [SMEM, SMEM, HBM, HBM, HBM, HBM],
-        [PAIRS, TURNED],
-        [
+        in_specs=[HBM, HBM, HBM, HBM],
+        out_specs=[HBM, HBM],
+        out_shape=[PAIRS, TURNED],
+        scratch_shapes=[
             pltpu.VMEM((ROWS, COLS, CHAN), BF16),
             pltpu.VMEM((CHAN, 4 * CHAN), BF16),
-            pltpu.VMEM(mask_rows.shape, jnp.int32),
+            pltpu.VMEM(mask.shape, jnp.int32),
             pltpu.VMEM(gain.shape, F32),
             pltpu.VMEM((4 * CHAN, CHAN), BF16),
-        ]
-        + PROJ_SCRATCH
-        + [pltpu.SemaphoreType.DMA((ROWS // CHUNK + 3,))],
-        vmem=56,
-    )
-    return call(place, mask, mask_rows, gain, cells, weight)
+            *PROJ_SCRATCH,
+            pltpu.VMEM(PAIRS.shape, BF16),
+            pltpu.VMEM(TURNED.shape, BF16),
+            pltpu.SemaphoreType.DMA((3 + 2 * (ROWS // CHUNK) + CHAN // SPAN,)),
+        ],
+        compiler_params=pltpu.CompilerParams(vmem_limit_bytes=56 * MIB),
+        name="project",
+    )(mask, gain, cells, weight)
 
 
 def gate_kernel(module, gain_ref, cells_ref, weight_ref, out_ref):
@@ -169,7 +197,8 @@
     return call(gain, cells, weight)
 
 
-def normed_hidden_rows(module, gain_ref, hidden_ref, scratch):
+def normed_hidden_rows(module, gain_ref, hidden_ref, gains, scratch):
+    gains[...] = channel_column(gain_ref, module)
     for first in range(0, ROWS, 16):
         rows = slice(first, first + 16)
         hidden = hidden_ref[:, rows].astype(F32)
@@ -178,7 +207,7 @@
         scale = lax.rsqrt(jnp.mean(centred * centred, axis=0) + EPSILON)
 
         def body(chan, carry):
-            values = (hidden_ref[chan, rows].astype(F32) - average) * scale * gain_ref[module, chan]
+            values = (hidden_ref[chan, rows].astype(F32) - average) * scale * gains[pl.ds(chan, 1), :]
             scratch[pl.ds(chan * ROW_PITCH + first, 16), :] = values
             return carry
 
@@ -199,8 +228,8 @@
     ]
 
 
-def finish_kernel(gain_ref, hidden_ref, cells_ref, gate_ref, weight_ref, out_hbm, scratch, out_ref, sems):
-    normed_hidden_rows(1, gain_ref, hidden_ref, scratch)
+def finish_kernel(gain_ref, hidden_ref, cells_ref, gate_ref, weight_ref, out_hbm, gains, scratch, out_ref, sems):
+    normed_hidden_rows(1, gain_ref, hidden_ref, gains, scratch)
     weight = jnp.transpose(weight_ref[1])
     copies = []
     for first in range(0, ROWS, SUB):
@@ -217,11 +246,11 @@
 def finish(gain, hidden, cells, gate, weight):
     return pl.pallas_call(
         finish_kernel,
-        in_specs=[SMEM, VMEM, VMEM, VMEM, VMEM],
+        in_specs=[VMEM] * 5,
         out_specs=HBM,
         out_shape=CELLS,
         scratch_shapes=[
-            HIDDEN_SCRATCH,
+            *HIDDEN_SCRATCH,
             pltpu.VMEM((ROWS, COLS, CHAN), BF16),
             pltpu.SemaphoreType.DMA((ROWS // CHUNK,)),
         ],
@@ -231,32 +260,33 @@
 
 
 def finish_project_kernel(
-    place_ref, row_mask_ref, col_mask_ref, in_gain_ref, out_gain_ref, hidden_ref, cells_ref, gate_ref,
-    weight_ref, proj_ref, cells_out, pairs_out, scratch, proj_turned, left, right,
+    mask_ref, in_gain_ref, out_gain_ref, hidden_ref, cells_ref, gate_ref, weight_ref, proj_ref,
+    cells_out, pairs_out, gains, scratch, proj_turned, row_masks, left, right,
 ):
-    gain_mask = masked_gain(place_ref, in_gain_ref, 1, col_mask_ref)
-    normed_hidden_rows(0, out_gain_ref, hidden_ref, scratch)
+    gain_mask = masked_gain(in_gain_ref, 1, mask_ref)
+    set_row_masks(mask_ref, row_masks)
+    normed_hidden_rows(0, out_gain_ref, hidden_ref, gains, scratch)
     weight = jnp.transpose(weight_ref[0])
     proj_turned[...] = jnp.transpose(proj_ref[1])
     for first in range(0, ROWS, SUB):
         rows = updated_rows(first, scratch, weight, cells_ref, gate_ref)
         for index, row in enumerate(rows):
             cells_out[first + index] = row
-        masks = [row_mask(place_ref, row_mask_ref, first + index) for index in range(SUB)]
+        masks = [row_mask(row_masks, first + index) for index in range(SUB)]
         rows = [row.astype(F32) for row in rows]
         project_rows(rows, masks, gain_mask, proj_turned, left, right, first)
     emit_projections(left, right, pairs_out)
 
 
-def finish_project(place, mask, mask_rows, in_gain, out_gain, hidden, cells, gate, weight, proj):
+def finish_project(mask, in_gain, out_gain, hidden, cells, gate, weight, proj):
     call = kernel_call(
         finish_project_kernel,
         "finish_project",
-        [SMEM, SMEM, VMEM, VMEM, SMEM] + [VMEM] * 5,
+        [VMEM] * 8,
         [TURNED, PAIRS],
-        [HIDDEN_SCRATCH, pltpu.VMEM((4 * CHAN, CHAN), BF16)] + PROJ_SCRATCH,
-    )
-    return call(place, mask, mask_rows, in_gain, out_gain, hidden, cells, gate, weight, proj)
+        HIDDEN_SCRATCH + [pltpu.VMEM((4 * CHAN, CHAN), BF16)] + PROJ_SCRATCH,
+    )
+    return call(mask, in_gain, out_gain, hidden, cells, gate, weight, proj)
 
 
 GROUPS = 16
@@ -270,8 +300,8 @@
     return slice(block * COLS, (block + 1) * COLS)
 
 
-def outgoing_kernel(place_ref, pairs_ref, other_ref, out_ref, left, right):
-    core = place_ref[2]
+def outgoing_kernel(pairs_ref, other_ref, out_ref, left, right):
+    core = lax.axis_index("c")
     for block in range(BLOCKS):
         left[:, :, block_lanes(block)] = pairs_ref[:, block, 0]
         right[:, core, :, block_lanes(block)] = pairs_ref[:, block, 1]
@@ -289,19 +319,19 @@
             out_ref[:, block + half] = product[:, block_lanes(half)].reshape(GROUPS, ROWS, COLS)
 
 
-def outgoing(place, pairs, other):
+def outgoing(pairs, other):
     call = kernel_call(
         outgoing_kernel,
         "outgoing",
-        [SMEM, VMEM, VMEM],
+        [VMEM, VMEM],
         PRODUCT,
         [pltpu.VMEM((GROUPS, ROWS, TOKENS), BF16), pltpu.VMEM((GROUPS, 2, ROWS, TOKENS), BF16)],
     )
-    return call(place, pairs, other)
-
-
-def incoming_send_kernel(place_ref, pairs_ref, send_ref, left_ref, right_ref, turned):
-    core = place_ref[2]
+    return call(pairs, other)
+
+
+def incoming_send_kernel(pairs_ref, send_ref, left_ref, right_ref, turned):
+    core = lax.axis_index("c")
     for block in range(BLOCKS):
         right_ref[:, block_lanes(block)] = pairs_ref[:, block, 1].reshape(HALF, COLS)
         left = pairs_ref[:, block, 0].reshape(HALF, COLS)
@@ -312,11 +342,11 @@
     ).astype(BF16)
 
 
-def incoming_send(place, pairs):
+def incoming_send(pairs):
     call = kernel_call(
         incoming_send_kernel,
         "incoming_send",
-        [SMEM, VMEM],
+        [VMEM],
         [
             jax.ShapeDtypeStruct((HALF, TOKENS), BF16),
             jax.ShapeDtypeStruct((HALF, HALF), BF16),
@@ -324,7 +354,7 @@
         ],
         [pltpu.VMEM((GROUPS, 2, ROWS, HALF), BF16)],
     )
-    return call(place, pairs)
+    return call(pairs)
 
 
 def incoming_kernel(left_ref, right_ref, other_ref, out_ref):
@@ -350,21 +380,18 @@
 
 
 def per_device(pair_input, token_mask, in_gain, proj_weight, gate_weight, out_gain, out_weight):
-    place = jnp.stack(
-        [lax.axis_index(("xh", "z", "c")) * ROWS, lax.axis_index(("xl", "y")), lax.axis_index("c")]
-    ).astype(jnp.int32)
-    masks = (place, token_mask, token_mask.reshape(BLOCKS, COLS))
-
-    pairs, cells = project(*masks, in_gain, pair_input, proj_weight)
+    mask = token_mask.reshape(BLOCKS, COLS)
+
+    pairs, cells = project(mask, in_gain, pair_input, proj_weight)
     pairs = exchange(pairs).reshape(GROUPS, BLOCKS, 2, ROWS, COLS)
     other = to_other_core(pairs[:, :, 1])
     gate = output_gate(0, in_gain, cells, gate_weight)
-    product, gate = lax.optimization_barrier((outgoing(place, pairs, other), gate))
+    product, gate = lax.optimization_barrier((outgoing(pairs, other), gate))
     hidden = exchange(product.reshape(CHAN, ROWS, COLS))
-    cells, pairs = finish_project(*masks, in_gain, out_gain, hidden, cells, gate, out_weight, proj_weight)
+    cells, pairs = finish_project(mask, in_gain, out_gain, hidden, cells, gate, out_weight, proj_weight)
 
     pairs = exchange(pairs).reshape(GROUPS, BLOCKS, 2, ROWS, COLS)
-    send, left, right = incoming_send(place, pairs)
+    send, left, right = incoming_send(pairs)
     other = to_other_core(send)
     gate = output_gate(1, in_gain, cells, gate_weight)
     product, gate = lax.optimization_barrier((incoming(left, right, other), gate))

time: 231 us -> 225 us (0.974)
  Pallas kernels: 21.7 us -> 16.2 us
    pallas_call x5, Pallas kernels: 18.9 us -> 13.4 us  [the longest x1 4.6 us: project(): pl.pallas_call(project_kernel, in_specs=[HBM, HBM, HBM, HBM], out_specs=[...]
where the time goes in v4:
time: 225 us
  blocking collectives  198 us (88%)
  Pallas kernels  16.2 us (7%)
  starting transfers between devices  7.31 us (3%)
  waiting for transfers between devices  2.42 us (1%)
    all_to_all x4, blocking collectives, exchange(): lax.all_to_all(values, PEERS, split_axis=0, concat_axis=0, tiled=True)  198 us
    ppermute x2, starting transfers between devices, to_other_core(): return lax.ppermute(values, 'c', [(0, 1), (1, 0)])  7.31 us
    pallas_call x1, Pallas kernels, project(): pl.pallas_call(project_kernel, in_specs=[HBM, HBM, HBM, HBM], out_specs=[...  4.6 us
  transfers between devices with their start and end apart: 2, of which 2 were waited for; matrix products, arithmetic and copies ran while one was open for 0% of the time, Pallas kernels for 1%

profile of v4, /device:TPU:1, one launch (start us, length us, event | category | flops | bytes accessed | tf_op | source)
XLA Modules:
  0.0 224.7 jit_solution(2359756028620132574)
XLA Ops:
  0.0 4.6 %project.1 = (bf16[128,2,32,128]{3,2,1,0:T(8,128)(2,1)}, bf16[32,128,128]{2,1,0:T(8,128)(2,1)}) custom-call(s32[8,128]{1,0:T(8,128)} %bitcast.12, f32[2,128]{1,0:T(2,128)} %gain_ref.4, bf16[32,128,128]{2,1,0:T(8,128)(2,1)} %cells_hbm.1, bf16[2,128,512]{2,1,0:T(8,128)(2,1)} %proj_ref.1), custom_call_target="tpu_custom_call" | custom-call | tf_op jit(solution)/shard_map/project/pallas_call | solution.py:156
  4.6 68.7 %all_to_all.20 = bf16[128,2,32,128]{3,2,1,0:T(8,128)(2,1)S(1)} all-to-all(bf16[128,2,32,128]{3,2,1,0:T(8,128)(2,1)} %get-tuple-element.16), channel_id=1, replica_groups=mesh['xh'=2,'z'=8,'c'=2,'xl'=2,'y'=4] {'xh','z','xl','y'}, dimensions={0} | all-to-all | bytes 4194304 | tf_op jit(solution)/shard_map/all_to_all | solution.py:375
  73.3 0.4 copy.8
  73.6 0.0 copy-start
  73.7 0.0 copy-start.3
  73.7 0.0 copy-start.5
  73.7 0.1 slice_bitcast_fusion
  73.8 3.0 %collective-permute-start = (bf16[16,8,32,128]{3,2,1,0:T(8,128)(2,1)S(1)}, bf16[16,8,32,128]{3,2,1,0:T(8,128)(2,1)S(1)}, u32[]{:S(2)}, u32[]{:S(2)}) collective-permute-start(bf16[16,8,32,128]{3,2,1,0:T(8,128)(2,1)S(1)} %slice_bitcast_fusion), channel_id=1, source_target_pairs={{0,8},{8,0},{1,9},{9,1},{2,10},{10,2},{3,11},{11,3},{4,12},{12,4},... | collective-permute-start | bytes 3145736 | tf_op jit(solution)/shard_map/ppermute | solution.py:379
  76.8 0.0 copy-done
  76.8 0.0 copy-done.3
  76.8 0.0 copy-done.5
  76.8 1.1 output_gate.2.gate_ref
  77.8 1.2 collective-permute-done.other_ref
  79.0 1.6 outgoing.1
  80.7 0.0 copy-start.1
  80.7 0.0 copy-start.2
  80.7 0.0 copy-start.4
  80.7 0.0 copy-start.6
  80.7 36.4 %all_to_all.21.hidden_ref = bf16[128,32,128]{2,1,0:T(8,128)(2,1)S(1)} all-to-all(bf16[128,32,128]{2,1,0:T(8,128)(2,1)S(1)} %bitcast.11), channel_id=1, replica_groups=mesh['xh'=2,'z'=8,'c'=2,'xl'=2,'y'=4] {'xh','z','xl','y'}, dimensions={0} | all-to-all | bytes 2097152 | tf_op jit(solution)/shard_map/all_to_all | solution.py:375
  117.1 0.0 copy-done.1
  117.1 0.0 copy-done.2
  117.1 0.0 copy-done.4
  117.1 0.0 copy-done.6
  117.1 3.6 %finish_project.1 = (bf16[32,128,128]{2,1,0:T(8,128)(2,1)S(1)}, bf16[128,2,32,128]{3,2,1,0:T(8,128)(2,1)S(1)}) custom-call(s32[8,128]{1,0:T(8,128)S(1)} %bitcast.13, f32[2,128]{1,0:T(2,128)S(1)} %copy-done.5, f32[2,128]{1,0:T(2,128)S(1)} %copy-done.6, bf16[128,32,128]{2,1,0:T(8,128)(2,1)S(1)} %all_to_all.21.hidden_ref, bf16[32,128,128]{2,1,0:T(8,128)(2,1)S(1)} %copy-done, ...), custom_call_target="tpu_custom_call" | custom-call | tf_op jit(solution)/shard_map/finish_project/pallas_call | solution.py:289
  120.7 56.8 %all_to_all.22 = bf16[128,2,32,128]{3,2,1,0:T(8,128)(2,1)S(1)} all-to-all(bf16[128,2,32,128]{3,2,1,0:T(8,128)(2,1)S(1)} %get-tuple-element.20), channel_id=1, replica_groups=mesh['xh'=2,'z'=8,'c'=2,'xl'=2,'y'=4] {'xh','z','xl','y'}, dimensions={0} | all-to-all | bytes 4194304 | tf_op jit(solution)/shard_map/all_to_all | solution.py:375
  177.4 1.1 incoming_send.1
  178.5 4.3 %collective-permute-start.1 = (bf16[512,1024]{1,0:T(8,128)(2,1)S(1)}, bf16[512,1024]{1,0:T(8,128)(2,1)S(1)}, u32[]{:S(2)}, u32[]{:S(2)}) collective-permute-start(bf16[512,1024]{1,0:T(8,128)(2,1)S(1)} %get-tuple-element.23), channel_id=1, source_target_pairs={{0,8},{8,0},{1,9},{9,1},{2,10},{10,2},{3,11},{11,3},{4,12},{12,4},... | collective-permute-start | bytes 3145736 | tf_op jit(solution)/shard_map/ppermute | solution.py:379
  182.9 1.1 output_gate.3.gate_ref
  183.9 1.2 collective-permute-done.1.other_ref
  185.1 0.7 incoming.1
  185.9 36.1 %all_to_all.23.hidden_ref = bf16[128,32,128]{2,1,0:T(8,128)(2,1)S(1)} all-to-all(bf16[128,32,128]{2,1,0:T(8,128)(2,1)S(1)} %bitcast.10), channel_id=1, replica_groups=mesh['xh'=2,'z'=8,'c'=2,'xl'=2,'y'=4] {'xh','z','xl','y'}, dimensions={0} | all-to-all | bytes 2097152 | tf_op jit(solution)/shard_map/all_to_all | solution.py:375
  222.0 2.5 %finish.1 = bf16[32,128,128]{2,1,0:T(8,128)(2,1)} custom-call(f32[2,128]{1,0:T(2,128)S(1)} %copy-done.6, bf16[128,32,128]{2,1,0:T(8,128)(2,1)S(1)} %all_to_all.23.hidden_ref, bf16[32,128,128]{2,1,0:T(8,128)(2,1)S(1)} %get-tuple-element.24.cells_ref, f32[32,128,128]{2,1,0:T(8,128)S(1)} %output_gate.3.gate_ref, bf16[2,128,128]{2,1,0:T(8,128)(2,1)S(1)} %copy-done.2), custom_call_target="tpu_custom_call" | custom-call | tf_op jit(solution)/shard_map/finish/pallas_call | solution.py:247
Async XLA Ops:
  73.6 3.1 %copy-start = (bf16[32,128,128]{2,1,0:T(8,128)(2,1)S(1)}, bf16[32,128,128]{2,1,0:T(8,128)(2,1)}, u32[]{:S(2)}) copy-start(bf16[32,128,128]{2,1,0:T(8,128)(2,1)} %get-tuple-element.17.cells_ref) | copy-start | bytes 3145732
  73.7 3.1 %copy-start.3 = (bf16[2,128,128]{2,1,0:T(8,128)(2,1)S(1)}, bf16[2,128,128]{2,1,0:T(8,128)(2,1)}, u32[]{:S(2)}) copy-start(bf16[2,128,128]{2,1,0:T(8,128)(2,1)} %weight_ref.6) | copy-start | bytes 196612
  73.7 3.1 %copy-start.5 = (f32[2,128]{1,0:T(2,128)S(1)}, f32[2,128]{1,0:T(2,128)}, u32[]{:S(2)}) copy-start(f32[2,128]{1,0:T(2,128)} %gain_ref.4) | copy-start | bytes 3076
  73.8 5.3 %collective-permute-start = (bf16[16,8,32,128]{3,2,1,0:T(8,128)(2,1)S(1)}, bf16[16,8,32,128]{3,2,1,0:T(8,128)(2,1)S(1)}, u32[]{:S(2)}, u32[]{:S(2)}) collective-permute-start(bf16[16,8,32,128]{3,2,1,0:T(8,128)(2,1)S(1)} %slice_bitcast_fusion), channel_id=1, source_target_pairs={{0,8},{8,0},{1,9},{9,1},{2,10},{10,2},{3,11},{11,3},{4,12},{12,4},... | collective-permute-start | bytes 3145736 | tf_op jit(solution)/shard_map/ppermute | solution.py:379
  80.7 36.4 %copy-start.1 = (bf16[2,128,512]{2,1,0:T(8,128)(2,1)S(1)}, bf16[2,128,512]{2,1,0:T(8,128)(2,1)}, u32[]{:S(2)}) copy-start(bf16[2,128,512]{2,1,0:T(8,128)(2,1)} %proj_ref.1) | copy-start | bytes 786436
  80.7 36.4 %copy-start.2 = (bf16[2,128,128]{2,1,0:T(8,128)(2,1)S(1)}, bf16[2,128,128]{2,1,0:T(8,128)(2,1)}, u32[]{:S(2)}) copy-start(bf16[2,128,128]{2,1,0:T(8,128)(2,1)} %weight_ref.7) | copy-start | bytes 196612
  80.7 36.4 %copy-start.4 = (s32[1024]{0:T(1024)S(1)}, s32[1024]{0:T(1024)}, u32[]{:S(2)}) copy-start(s32[1024]{0:T(1024)} %param.8) | copy-start | bytes 12292
  80.7 36.4 %copy-start.6 = (f32[2,128]{1,0:T(2,128)S(1)}, f32[2,128]{1,0:T(2,128)}, u32[]{:S(2)}) copy-start(f32[2,128]{1,0:T(2,128)} %gain_ref.5) | copy-start | bytes 3076
  178.5 6.6 %collective-permute-start.1 = (bf16[512,1024]{1,0:T(8,128)(2,1)S(1)}, bf16[512,1024]{1,0:T(8,128)(2,1)S(1)}, u32[]{:S(2)}, u32[]{:S(2)}) collective-permute-start(bf16[512,1024]{1,0:T(8,128)(2,1)S(1)} %get-tuple-element.23), channel_id=1, source_target_pairs={{0,8},{8,0},{1,9},{9,1},{2,10},{10,2},{3,11},{11,3},{4,12},{12,4},... | collective-permute-start | bytes 3145736 | tf_op jit(solution)/shard_map/ppermute | solution.py:379

commit v5 on v4

--- a/solution.py
+++ b/solution.py
@@ -13,10 +13,13 @@
 COLS = 128
 SUB = 16
 CHUNK = 16
-SPAN = 32
+SPAN = 4
 CHAN_PITCH = CHAN + 1
 ROW_PITCH = ROWS + 1
-PEERS = ("xh", "z", "xl", "y")
+DEVICES = ("xh", "z", "c", "xl", "y")
+PLACES = 16
+BLOCKS = 8
+PART = 16
 F32 = jnp.float32
 BF16 = jnp.bfloat16
 MIB = 1024 * 1024
@@ -45,7 +48,7 @@
 HBM = pl.BlockSpec(memory_space=pltpu.HBM)
 PROJ_SCRATCH = [pltpu.VMEM((COLS, COLS), F32)] + [pltpu.VMEM((ROWS * CHAN_PITCH, COLS), F32)] * 2
 HIDDEN_SCRATCH = [pltpu.VMEM((CHAN, COLS), F32), pltpu.VMEM((CHAN * ROW_PITCH, COLS), F32)]
-PAIRS = jax.ShapeDtypeStruct((CHAN, 2, ROWS, COLS), BF16)
+PAIRS = jax.ShapeDtypeStruct((PLACES, 2, BLOCKS, 2, PART, COLS), BF16)
 CELLS = jax.ShapeDtypeStruct((ROWS, COLS, CHAN), BF16)
 TURNED = jax.ShapeDtypeStruct((ROWS, CHAN, COLS), BF16)
 GATE = jax.ShapeDtypeStruct((ROWS, CHAN, COLS), F32)
@@ -90,14 +93,16 @@
         right_scratch[place, :] = right[:, lanes]
 
 
-def emit_projections(left_scratch, right_scratch, out_ref, first=0, count=CHAN):
-    def body(chan, carry):
-        place = pl.ds(chan, ROWS, stride=CHAN_PITCH)
-        out_ref[chan, 0] = left_scratch[place, :].astype(BF16)
-        out_ref[chan, 1] = right_scratch[place, :].astype(BF16)
+def emit_projections(left_scratch, right_scratch, out_ref, first=0, count=PLACES):
+    def body(place, carry):
+        for block in range(BLOCKS):
+            for core in range(2):
+                rows = pl.ds(core * PART * CHAN_PITCH + place * BLOCKS + block, PART, stride=CHAN_PITCH)
+                out_ref[place, core, block, 0] = left_scratch[rows, :].astype(BF16)
+                out_ref[place, core, block, 1] = right_scratch[rows, :].astype(BF16)
         return carry
 
-    lax.fori_loop(first, first + count, body, 0, unroll=8)
+    lax.fori_loop(first, first + count, body, 0)
 
 
 def project_kernel(
@@ -139,7 +144,7 @@
         masks = [row_mask(row_masks, first + index) for index in range(SUB)]
         project_rows(rows, masks, gain_mask, weight_turned, left, right, first)
     pair_copies = []
-    for first in range(0, CHAN, SPAN):
+    for first in range(0, PLACES, SPAN):
         emit_projections(left, right, pairs_ref, first, SPAN)
         span = pl.ds(first, SPAN)
         pair_copies.append(
@@ -167,7 +172,7 @@
             *PROJ_SCRATCH,
             pltpu.VMEM(PAIRS.shape, BF16),
             pltpu.VMEM(TURNED.shape, BF16),
-            pltpu.SemaphoreType.DMA((3 + 2 * (ROWS // CHUNK) + CHAN // SPAN,)),
+            pltpu.SemaphoreType.DMA((3 + 2 * (ROWS // CHUNK) + PLACES // SPAN,)),
         ],
         compiler_params=pltpu.CompilerParams(vmem_limit_bytes=56 * MIB),
         name="project",
@@ -199,19 +204,20 @@
 
 def normed_hidden_rows(module, gain_ref, hidden_ref, gains, scratch):
     gains[...] = channel_column(gain_ref, module)
-    for first in range(0, ROWS, 16):
-        rows = slice(first, first + 16)
-        hidden = hidden_ref[:, rows].astype(F32)
+    for core in range(2):
+        hidden = hidden_ref[:, core].astype(F32).reshape(CHAN, PART, COLS)
         average = jnp.mean(hidden, axis=0)
         centred = hidden - average[None]
         scale = lax.rsqrt(jnp.mean(centred * centred, axis=0) + EPSILON)
 
-        def body(chan, carry):
-            values = (hidden_ref[chan, rows].astype(F32) - average) * scale * gains[pl.ds(chan, 1), :]
-            scratch[pl.ds(chan * ROW_PITCH + first, 16), :] = values
+        def body(place, carry):
+            for block in range(BLOCKS):
+                chan = place * BLOCKS + block
+                values = (hidden_ref[place, core, block].astype(F32) - average) * scale * gains[pl.ds(chan, 1), :]
+                scratch[pl.ds(chan * ROW_PITCH + core * PART, PART), :] = values
             return carry
 
-        lax.fori_loop(0, CHAN, body, 0, unroll=8)
+        lax.fori_loop(0, PLACES, body, 0)
 
 
 def updated_rows(first, scratch, weight, cells_ref, gate_ref):
@@ -289,11 +295,10 @@
     return call(mask, in_gain, out_gain, hidden, cells, gate, weight, proj)
 
 
-GROUPS = 16
-BLOCKS = 8
+GROUPS = 32
 TOKENS = BLOCKS * COLS
-HALF = GROUPS * ROWS
-PRODUCT = jax.ShapeDtypeStruct((GROUPS, BLOCKS, ROWS, COLS), BF16)
+HALF = GROUPS * PART
+PRODUCT = jax.ShapeDtypeStruct((GROUPS, BLOCKS, PART, COLS), BF16)
 
 
 def block_lanes(block):
@@ -308,7 +313,7 @@
         right[:, 1 - core, :, block_lanes(block)] = other_ref[:, block]
     left_rows = left[...].reshape(HALF, TOKENS)
     for block in range(0, BLOCKS, 2):
-        groups = slice(block * 2, block * 2 + 4)
+        groups = slice(block * 4, block * 4 + 8)
         product = lax.dot_general(
             left_rows,
             right[groups].reshape(2 * COLS, TOKENS),
@@ -316,7 +321,7 @@
             preferred_element_type=F32,
         ).astype(BF16)
         for half in range(2):
-            out_ref[:, block + half] = product[:, block_lanes(half)].reshape(GROUPS, ROWS, COLS)
+            out_ref[:, block + half] = product[:, block_lanes(half)].reshape(GROUPS, PART, COLS)
 
 
 def outgoing(pairs, other):
@@ -325,7 +330,7 @@
         "outgoing",
         [VMEM, VMEM],
         PRODUCT,
-        [pltpu.VMEM((GROUPS, ROWS, TOKENS), BF16), pltpu.VMEM((GROUPS, 2, ROWS, TOKENS), BF16)],
+        [pltpu.VMEM((GROUPS, PART, TOKENS), BF16), pltpu.VMEM((GROUPS, 2, PART, TOKENS), BF16)],
     )
     return call(pairs, other)
 
@@ -335,7 +340,7 @@
     for block in range(BLOCKS):
         right_ref[:, block_lanes(block)] = pairs_ref[:, block, 1].reshape(HALF, COLS)
         left = pairs_ref[:, block, 0].reshape(HALF, COLS)
-        turned[2 * block : 2 * block + 2] = jnp.transpose(left).reshape(2, 2, ROWS, HALF)
+        turned[4 * block : 4 * block + 4] = jnp.transpose(left).reshape(4, 2, PART, HALF)
     left_ref[...] = turned[:, core].reshape(HALF, HALF)
     send_ref[...] = jnp.dot(
         turned[:, 1 - core].reshape(HALF, HALF), right_ref[...], preferred_element_type=F32
@@ -352,7 +357,7 @@
             jax.ShapeDtypeStruct((HALF, HALF), BF16),
             jax.ShapeDtypeStruct((HALF, TOKENS), BF16),
         ],
-        [pltpu.VMEM((GROUPS, 2, ROWS, HALF), BF16)],
+        [pltpu.VMEM((GROUPS, 2, PART, HALF), BF16)],
     )
     return call(pairs)
 
@@ -364,7 +369,7 @@
         total = jnp.dot(left, right_ref[:, lanes], preferred_element_type=F32)
         product = (total + other_ref[:, lanes].astype(F32)).astype(BF16)
         for half in range(2):
-            out_ref[:, block + half] = product[:, block_lanes(half)].reshape(GROUPS, ROWS, COLS)
+            out_ref[:, block + half] = product[:, block_lanes(half)].reshape(GROUPS, PART, COLS)
 
 
 def incoming(left, right, other):
@@ -372,7 +377,16 @@
 
 
 def exchange(values):
-    return lax.all_to_all(values, PEERS, split_axis=0, concat_axis=0, tiled=True)
+    return lax.all_to_all(values, DEVICES, split_axis=0, concat_axis=0, tiled=True)
+
+
+def exchange_pairs(pairs):
+    received = exchange(pairs.reshape(2 * CHAN, 2, PART, COLS))
+    return received.reshape(GROUPS, BLOCKS, 2, PART, COLS)
+
+
+def exchange_product(product):
+    return exchange(product.reshape(2 * CHAN, PART, COLS)).reshape(PLACES, 2, BLOCKS, PART, COLS)
 
 
 def to_other_core(values):
@@ -383,19 +397,19 @@
     mask = token_mask.reshape(BLOCKS, COLS)
 
     pairs, cells = project(mask, in_gain, pair_input, proj_weight)
-    pairs = exchange(pairs).reshape(GROUPS, BLOCKS, 2, ROWS, COLS)
+    pairs = exchange_pairs(pairs)
     other = to_other_core(pairs[:, :, 1])
     gate = output_gate(0, in_gain, cells, gate_weight)
     product, gate = lax.optimization_barrier((outgoing(pairs, other), gate))
-    hidden = exchange(product.reshape(CHAN, ROWS, COLS))
+    hidden = exchange_product(product)
     cells, pairs = finish_project(mask, in_gain, out_gain, hidden, cells, gate, out_weight, proj_weight)
 
-    pairs = exchange(pairs).reshape(GROUPS, BLOCKS, 2, ROWS, COLS)
+    pairs = exchange_pairs(pairs)
     send, left, right = incoming_send(pairs)
     other = to_other_core(send)
     gate = output_gate(1, in_gain, cells, gate_weight)
     product, gate = lax.optimization_barrier((incoming(left, right, other), gate))
-    hidden = exchange(product.reshape(CHAN, ROWS, COLS))
+    hidden = exchange_product(product)
     return finish(out_gain, hidden, cells, gate, out_weight)
 
 

time: 225 us -> 223 us (level)
  starting transfers between devices: 7.31 us -> 2.67 us
    ppermute x2, starting transfers between devices: 7.31 us -> 2.67 us  [to_other_core(): return lax.ppermute(values, 'c', [(0, 1), (1, 0)])]
where the time goes in v5:
time: 223 us; the launch traced here: 222 us
  blocking collectives  200 us (90%)
  Pallas kernels  16.2 us (7%)
  starting transfers between devices  2.67 us (1%)
  waiting for transfers between devices  2.42 us (1%)
    all_to_all x4, blocking collectives, exchange(): lax.all_to_all(values, DEVICES, split_axis=0, concat_axis=0, tiled=True)  200 us
    pallas_call x1, Pallas kernels, project(): pl.pallas_call(project_kernel, in_specs=[HBM, HBM, HBM, HBM], out_specs=[...  4.6 us
  transfers between devices with their start and end apart: 2, of which 2 were waited for; matrix products, arithmetic and copies ran while one was open for 0% of the time, Pallas kernels for 1%

profile of v5, /device:TPU:1, one launch (start us, length us, event | category | flops | bytes accessed | tf_op | source)
XLA Modules:
  0.0 222.2 jit_solution(10073426001916521977)
XLA Ops:
  0.0 4.6 %project.1 = (bf16[16,2,8,2,16,128]{5,4,3,2,1,0:T(8,128)(2,1)}, bf16[32,128,128]{2,1,0:T(8,128)(2,1)}) custom-call(s32[8,128]{1,0:T(8,128)} %bitcast.19, f32[2,128]{1,0:T(2,128)} %gain_ref.4, bf16[32,128,128]{2,1,0:T(8,128)(2,1)} %cells_hbm.1, bf16[2,128,512]{2,1,0:T(8,128)(2,1)} %proj_ref.1), custom_call_target="tpu_custom_call" | custom-call | tf_op jit(solution)/shard_map/project/pallas_call | solution.py:161
  4.6 68.9 %all_to_all.20 = bf16[256,2,16,128]{3,2,1,0:T(8,128)(2,1)S(1)} all-to-all(bf16[256,2,16,128]{3,2,1,0:T(8,128)(2,1)} %bitcast.22), channel_id=1, replica_groups=mesh['xh'=2,'z'=8,'c'=2,'xl'=2,'y'=4] {'xh','z','c','xl','y'}, dimensions={0} | all-to-all | bytes 4194304 | tf_op jit(solution)/shard_map/all_to_all | solution.py:380
  73.5 0.4 copy.10
  73.9 0.0 copy-start
  73.9 0.0 copy-start.3
  73.9 0.0 copy-start.5
  73.9 0.2 slice_bitcast_fusion
  74.1 1.3 collective-permute-start
  75.5 0.0 copy-done
  75.5 0.0 copy-done.3
  75.5 0.0 copy-done.5
  75.5 1.1 output_gate.2.gate_ref
  76.5 1.2 collective-permute-done.other_ref
  77.8 1.6 outgoing.1
  79.3 0.0 copy-start.1
  79.3 0.0 copy-start.2
  79.3 0.0 copy-start.4
  79.4 0.0 copy-start.6
  79.4 35.4 %all_to_all.21 = bf16[256,16,128]{2,1,0:T(8,128)(2,1)S(1)} all-to-all(bf16[256,16,128]{2,1,0:T(8,128)(2,1)S(1)} %bitcast.17), channel_id=1, replica_groups=mesh['xh'=2,'z'=8,'c'=2,'xl'=2,'y'=4] {'xh','z','c','xl','y'}, dimensions={0} | all-to-all | bytes 2097152 | tf_op jit(solution)/shard_map/all_to_all | solution.py:380
  114.7 0.0 copy-done.1
  114.7 0.0 copy-done.2
  114.7 0.0 copy-done.4
  114.8 0.0 copy-done.6
  114.8 3.5 %finish_project.1 = (bf16[32,128,128]{2,1,0:T(8,128)(2,1)S(1)}, bf16[16,2,8,2,16,128]{5,4,3,2,1,0:T(8,128)(2,1)S(1)}) custom-call(s32[8,128]{1,0:T(8,128)S(1)} %bitcast.20, f32[2,128]{1,0:T(2,128)S(1)} %copy-done.5, f32[2,128]{1,0:T(2,128)S(1)} %copy-done.6, bf16[16,2,8,16,128]{4,3,2,1,0:T(8,128)(2,1)S(1)} %bitcast.14, bf16[32,128,128]{2,1,0:T(8,128)(2,1)S(1)} %copy-done, ...), custom_call_target="tpu_custom_call" | custom-call | tf_op jit(solution)/shard_map/finish_project/pallas_call | solution.py:295
  118.3 60.3 %all_to_all.22 = bf16[256,2,16,128]{3,2,1,0:T(8,128)(2,1)S(1)} all-to-all(bf16[256,2,16,128]{3,2,1,0:T(8,128)(2,1)S(1)} %bitcast.18), channel_id=1, replica_groups=mesh['xh'=2,'z'=8,'c'=2,'xl'=2,'y'=4] {'xh','z','c','xl','y'}, dimensions={0} | all-to-all | bytes 4194304 | tf_op jit(solution)/shard_map/all_to_all | solution.py:380
  178.7 1.1 incoming_send.1
  179.8 1.3 collective-permute-start.1
  181.1 1.1 output_gate.3.gate_ref
  182.2 1.2 collective-permute-done.1.other_ref
  183.4 0.7 incoming.1
  184.2 35.4 %all_to_all.23 = bf16[256,16,128]{2,1,0:T(8,128)(2,1)S(1)} all-to-all(bf16[256,16,128]{2,1,0:T(8,128)(2,1)S(1)} %bitcast.15), channel_id=1, replica_groups=mesh['xh'=2,'z'=8,'c'=2,'xl'=2,'y'=4] {'xh','z','c','xl','y'}, dimensions={0} | all-to-all | bytes 2097152 | tf_op jit(solution)/shard_map/all_to_all | solution.py:380
  219.5 2.5 %finish.1 = bf16[32,128,128]{2,1,0:T(8,128)(2,1)} custom-call(f32[2,128]{1,0:T(2,128)S(1)} %copy-done.6, bf16[16,2,8,16,128]{4,3,2,1,0:T(8,128)(2,1)S(1)} %bitcast.16, bf16[32,128,128]{2,1,0:T(8,128)(2,1)S(1)} %get-tuple-element.24.cells_ref, f32[32,128,128]{2,1,0:T(8,128)S(1)} %output_gate.3.gate_ref, bf16[2,128,128]{2,1,0:T(8,128)(2,1)S(1)} %copy-done.2), custom_call_target="tpu_custom_call" | custom-call | tf_op jit(solution)/shard_map/finish/pallas_call | solution.py:253
Async XLA Ops:
  73.9 1.6 copy-start
  73.9 1.6 copy-start.3
  73.9 1.6 copy-start.5
  74.1 3.6 %collective-permute-start = (bf16[32,8,16,128]{3,2,1,0:T(8,128)(2,1)S(1)}, bf16[32,8,16,128]{3,2,1,0:T(8,128)(2,1)S(1)}, u32[]{:S(2)}, u32[]{:S(2)}) collective-permute-start(bf16[32,8,16,128]{3,2,1,0:T(8,128)(2,1)S(1)} %slice_bitcast_fusion), channel_id=1, source_target_pairs={{0,8},{8,0},{1,9},{9,1},{2,10},{10,2},{3,11},{11,3},{4,12},{12,4},... | collective-permute-start | bytes 3145736 | tf_op jit(solution)/shard_map/ppermute | solution.py:393
  79.3 35.4 %copy-start.1 = (bf16[2,128,512]{2,1,0:T(8,128)(2,1)S(1)}, bf16[2,128,512]{2,1,0:T(8,128)(2,1)}, u32[]{:S(2)}) copy-start(bf16[2,128,512]{2,1,0:T(8,128)(2,1)} %proj_ref.1) | copy-start | bytes 786436
  79.3 35.4 %copy-start.2 = (bf16[2,128,128]{2,1,0:T(8,128)(2,1)S(1)}, bf16[2,128,128]{2,1,0:T(8,128)(2,1)}, u32[]{:S(2)}) copy-start(bf16[2,128,128]{2,1,0:T(8,128)(2,1)} %weight_ref.7) | copy-start | bytes 196612
  79.3 35.4 %copy-start.4 = (s32[1024]{0:T(1024)S(1)}, s32[1024]{0:T(1024)}, u32[]{:S(2)}) copy-start(s32[1024]{0:T(1024)} %param.8) | copy-start | bytes 12292
  79.4 35.4 %copy-start.6 = (f32[2,128]{1,0:T(2,128)S(1)}, f32[2,128]{1,0:T(2,128)}, u32[]{:S(2)}) copy-start(f32[2,128]{1,0:T(2,128)} %gain_ref.5) | copy-start | bytes 3076
  179.8 3.6 %collective-permute-start.1 = (bf16[512,1024]{1,0:T(8,128)(2,1)S(1)}, bf16[512,1024]{1,0:T(8,128)(2,1)S(1)}, u32[]{:S(2)}, u32[]{:S(2)}) collective-permute-start(bf16[512,1024]{1,0:T(8,128)(2,1)S(1)} %get-tuple-element.23), channel_id=1, source_target_pairs={{0,8},{8,0},{1,9},{9,1},{2,10},{10,2},{3,11},{11,3},{4,12},{12,4},... | collective-permute-start | bytes 3145736 | tf_op jit(solution)/shard_map/ppermute | solution.py:393

commit v6 on v5

--- a/solution.py
+++ b/solution.py
@@ -46,8 +46,8 @@
 
 
 HBM = pl.BlockSpec(memory_space=pltpu.HBM)
-PROJ_SCRATCH = [pltpu.VMEM((COLS, COLS), F32)] + [pltpu.VMEM((ROWS * CHAN_PITCH, COLS), F32)] * 2
-HIDDEN_SCRATCH = [pltpu.VMEM((CHAN, COLS), F32), pltpu.VMEM((CHAN * ROW_PITCH, COLS), F32)]
+PROJ_SCRATCH = [pltpu.VMEM((COLS, COLS), F32)] + [pltpu.VMEM((ROWS * CHAN_PITCH + CHAN, COLS), F32)] * 2
+HIDDEN_SCRATCH = [pltpu.VMEM((CHAN, COLS), F32), pltpu.VMEM((CHAN * ROW_PITCH + ROWS, COLS), F32)]
 PAIRS = jax.ShapeDtypeStruct((PLACES, 2, BLOCKS, 2, PART, COLS), BF16)
 CELLS = jax.ShapeDtypeStruct((ROWS, COLS, CHAN), BF16)
 TURNED = jax.ShapeDtypeStruct((ROWS, CHAN, COLS), BF16)
@@ -61,13 +61,24 @@
     return centred * lax.rsqrt(variance + EPSILON) * factor
 
 
+def by_part(columns):
+    starts = [group * ROWS + core * PART for core in range(2) for group in range(COLS // ROWS)]
+    return jnp.concatenate([columns[start : start + PART] for start in starts], axis=0)
+
+
+def natural(columns):
+    starts = [core * (COLS // 2) + group * PART for group in range(COLS // ROWS) for core in range(2)]
+    return jnp.concatenate([columns[start : start + PART] for start in starts], axis=0)
+
+
 def channel_column(gain_ref, module):
     return jnp.transpose(jnp.broadcast_to(gain_ref[module : module + 1, :], (COLS, CHAN)))
 
 
 def masked_gain(gain_ref, module, col_mask_ref):
     block = lax.axis_index(("xl", "y"))
-    return channel_column(gain_ref, module) * col_mask_ref[pl.ds(block, 1), :].astype(F32)
+    tokens = jnp.broadcast_to(col_mask_ref[pl.ds(block, 1), :].astype(F32), (COLS, COLS))
+    return channel_column(gain_ref, module) * jnp.transpose(by_part(jnp.transpose(tokens)))
 
 
 def set_row_masks(mask_ref, scratch):
@@ -136,7 +147,7 @@
             cell_copies[first // CHUNK].wait()
         rows = []
         for index in range(first, first + SUB):
-            row = jnp.transpose(cells_ref[index])
+            row = jnp.transpose(by_part(cells_ref[index]))
             turned_ref[index] = row
             rows.append(row.astype(F32))
         if (first + SUB) % CHUNK == 0:
@@ -240,7 +251,7 @@
     copies = []
     for first in range(0, ROWS, SUB):
         for index, row in enumerate(updated_rows(first, scratch, weight, cells_ref, gate_ref)):
-            out_ref[first + index] = jnp.transpose(row)
+            out_ref[first + index] = natural(jnp.transpose(row))
         if (first + SUB) % CHUNK == 0:
             rows = pl.ds(first + SUB - CHUNK, CHUNK)
             copies.append(pltpu.make_async_copy(out_ref.at[rows], out_hbm.at[rows], sems.at[first // CHUNK]))
@@ -305,34 +316,61 @@
     return slice(block * COLS, (block + 1) * COLS)
 
 
-def outgoing_kernel(pairs_ref, other_ref, out_ref, left, right):
-    core = lax.axis_index("c")
+def take_right_kernel(pairs_ref, out_ref):
+    out_ref[...] = pairs_ref[:, :, 1]
+
+
+def take_right(pairs):
+    shape = jax.ShapeDtypeStruct((GROUPS, BLOCKS, PART, COLS), BF16)
+    return kernel_call(take_right_kernel, "take_right", [VMEM], shape)(pairs)
+
+
+def product_half(left_ref, right, block):
+    rows = right[block * (COLS // 2) : (block + 2) * (COLS // 2)]
+    return lax.dot_general(left_ref[...], rows, (((1,), (1,)), ((), ())), preferred_element_type=F32)
+
+
+def outgoing_own_kernel(pairs_ref, left_ref, own_ref, right):
     for block in range(BLOCKS):
-        left[:, :, block_lanes(block)] = pairs_ref[:, block, 0]
-        right[:, core, :, block_lanes(block)] = pairs_ref[:, block, 1]
-        right[:, 1 - core, :, block_lanes(block)] = other_ref[:, block]
-    left_rows = left[...].reshape(HALF, TOKENS)
-    for block in range(0, BLOCKS, 2):
-        groups = slice(block * 4, block * 4 + 8)
-        product = lax.dot_general(
-            left_rows,
-            right[groups].reshape(2 * COLS, TOKENS),
-            (((1,), (1,)), ((), ())),
-            preferred_element_type=F32,
-        ).astype(BF16)
-        for half in range(2):
-            out_ref[:, block + half] = product[:, block_lanes(half)].reshape(GROUPS, PART, COLS)
-
-
-def outgoing(pairs, other):
+        left_ref[:, block_lanes(block)] = pairs_ref[:, block, 0].reshape(HALF, COLS)
+        right[:, block_lanes(block)] = pairs_ref[:, block, 1].reshape(HALF, COLS)
+    for pair in range(BLOCKS // 2):
+        own_ref[:, block_lanes(pair)] = product_half(left_ref, right, 2 * pair)
+
+
+def outgoing_own(pairs):
     call = kernel_call(
-        outgoing_kernel,
-        "outgoing",
-        [VMEM, VMEM],
-        PRODUCT,
-        [pltpu.VMEM((GROUPS, PART, TOKENS), BF16), pltpu.VMEM((GROUPS, 2, PART, TOKENS), BF16)],
-    )
-    return call(pairs, other)
+        outgoing_own_kernel,
+        "outgoing_own",
+        [VMEM],
+        [jax.ShapeDtypeStruct((HALF, TOKENS), BF16), jax.ShapeDtypeStruct((HALF, HALF), F32)],
+        [pltpu.VMEM((HALF, TOKENS), BF16)],
+        cost=pl.CostEstimate(flops=2 * HALF * HALF * TOKENS, bytes_accessed=4 << 20, transcendentals=0),
+    )
+    return call(pairs)
+
+
+def outgoing_kernel(left_ref, own_ref, other_ref, out_ref, right):
+    own_first = lax.axis_index("c") == 0
+    lower = lax.broadcasted_iota(jnp.int32, (HALF, COLS), 1) < COLS // 2
+    for block in range(BLOCKS):
+        right[:, block_lanes(block)] = other_ref[:, block].reshape(HALF, COLS)
+    for pair in range(BLOCKS // 2):
+        own = own_ref[:, block_lanes(pair)]
+        other = product_half(left_ref, right, 2 * pair)
+        first = jnp.where(own_first, own, other)
+        second = jnp.where(own_first, other, own)
+        even = jnp.where(lower, first, pltpu.roll(second, COLS // 2, 1)).astype(BF16)
+        odd = jnp.where(lower, pltpu.roll(first, COLS // 2, 1), second).astype(BF16)
+        out_ref[:, 2 * pair] = even.reshape(GROUPS, PART, COLS)
+        out_ref[:, 2 * pair + 1] = odd.reshape(GROUPS, PART, COLS)
+
+
+def outgoing(left, own, other):
+    call = kernel_call(
+        outgoing_kernel, "outgoing", [VMEM, VMEM, VMEM], PRODUCT, [pltpu.VMEM((HALF, TOKENS), BF16)]
+    )
+    return call(left, own, other)
 
 
 def incoming_send_kernel(pairs_ref, send_ref, left_ref, right_ref, turned):
@@ -340,10 +378,10 @@
     for block in range(BLOCKS):
         right_ref[:, block_lanes(block)] = pairs_ref[:, block, 1].reshape(HALF, COLS)
         left = pairs_ref[:, block, 0].reshape(HALF, COLS)
-        turned[4 * block : 4 * block + 4] = jnp.transpose(left).reshape(4, 2, PART, HALF)
-    left_ref[...] = turned[:, core].reshape(HALF, HALF)
+        turned[:, block] = jnp.transpose(left).reshape(2, COLS // 2, HALF)
+    left_ref[...] = turned[core].reshape(HALF, HALF)
     send_ref[...] = jnp.dot(
-        turned[:, 1 - core].reshape(HALF, HALF), right_ref[...], preferred_element_type=F32
+        turned[1 - core].reshape(HALF, HALF), right_ref[...], preferred_element_type=F32
     ).astype(BF16)
 
 
@@ -357,7 +395,7 @@
             jax.ShapeDtypeStruct((HALF, HALF), BF16),
             jax.ShapeDtypeStruct((HALF, TOKENS), BF16),
         ],
-        [pltpu.VMEM((GROUPS, 2, PART, HALF), BF16)],
+        [pltpu.VMEM((2, BLOCKS, COLS // 2, HALF), BF16)],
     )
     return call(pairs)
 
@@ -398,9 +436,10 @@
 
     pairs, cells = project(mask, in_gain, pair_input, proj_weight)
     pairs = exchange_pairs(pairs)
-    other = to_other_core(pairs[:, :, 1])
+    other = to_other_core(take_right(pairs))
+    left, own = outgoing_own(pairs)
     gate = output_gate(0, in_gain, cells, gate_weight)
-    product, gate = lax.optimization_barrier((outgoing(pairs, other), gate))
+    product, gate = lax.optimization_barrier((outgoing(left, own, other), gate))
     hidden = exchange_product(product)
     cells, pairs = finish_project(mask, in_gain, out_gain, hidden, cells, gate, out_weight, proj_weight)
 

time: 223 us -> 223 us (level)
  transfers between devices with their start and end apart: 2 -> 2, of which waited for: 2 -> 1; matrix products, arithmetic and copies ran while one was open for 0% -> 0% of each run, Pallas kernels for 1% -> 2%
where the time goes in v6:
time: 223 us; the launch traced here: 222 us
  blocking collectives  201 us (90%)
  Pallas kernels  17.5 us (8%)
  starting transfers between devices  2.66 us (1%)
    all_to_all x4, blocking collectives, exchange(): lax.all_to_all(values, DEVICES, split_axis=0, concat_axis=0, tiled=True)  201 us
    pallas_call x1, Pallas kernels, project(): pl.pallas_call(project_kernel, in_specs=[HBM, HBM, HBM, HBM], out_specs=[...  4.6 us
  transfers between devices with their start and end apart: 2, of which 1 were waited for; matrix products, arithmetic and copies ran while one was open for 0% of the time, Pallas kernels for 2%

profile of v6, /device:TPU:1, one launch (start us, length us, event | category | flops | bytes accessed | tf_op | source)
XLA Modules:
  0.0 222.4 jit_solution(5110941331859380982)
XLA Ops:
  0.0 4.6 %project.1 = (bf16[16,2,8,2,16,128]{5,4,3,2,1,0:T(8,128)(2,1)}, bf16[32,128,128]{2,1,0:T(8,128)(2,1)}) custom-call(s32[8,128]{1,0:T(8,128)} %bitcast.17, f32[2,128]{1,0:T(2,128)} %gain_ref.4, bf16[32,128,128]{2,1,0:T(8,128)(2,1)} %cells_hbm.1, bf16[2,128,512]{2,1,0:T(8,128)(2,1)} %proj_ref.1), custom_call_target="tpu_custom_call" | custom-call | tf_op jit(solution)/shard_map/project/pallas_call | solution.py:172
  4.6 68.9 %all_to_all.20 = bf16[256,2,16,128]{3,2,1,0:T(8,128)(2,1)S(1)} all-to-all(bf16[256,2,16,128]{3,2,1,0:T(8,128)(2,1)} %bitcast.19), channel_id=1, replica_groups=mesh['xh'=2,'z'=8,'c'=2,'xl'=2,'y'=4] {'xh','z','c','xl','y'}, dimensions={0} | all-to-all | bytes 4194304 | tf_op jit(solution)/shard_map/all_to_all | solution.py:418
  73.6 0.0 copy-start
  73.6 0.0 copy-start.3
  73.6 0.0 copy-start.5
  73.6 0.1 take_right.1
  73.6 1.3 collective-permute-start
  75.0 0.0 copy-done
  75.0 0.0 copy-done.3
  75.0 0.0 copy-done.5
  75.0 1.1 output_gate.2.gate_ref
  76.1 1.4 outgoing_own.1
  77.4 0.0 collective-permute-done.other_ref
  77.4 1.4 outgoing.1
  78.9 0.0 copy-start.1
  78.9 0.0 copy-start.2
  78.9 0.0 copy-start.4
  78.9 0.0 copy-start.6
  78.9 36.1 %all_to_all.21 = bf16[256,16,128]{2,1,0:T(8,128)(2,1)S(1)} all-to-all(bf16[256,16,128]{2,1,0:T(8,128)(2,1)S(1)} %bitcast.14), channel_id=1, replica_groups=mesh['xh'=2,'z'=8,'c'=2,'xl'=2,'y'=4] {'xh','z','c','xl','y'}, dimensions={0} | all-to-all | bytes 2097152 | tf_op jit(solution)/shard_map/all_to_all | solution.py:418
  115.0 0.0 copy-done.1
  115.0 0.0 copy-done.2
  115.0 0.0 copy-done.4
  115.0 0.0 copy-done.6
  115.0 3.6 %finish_project.1 = (bf16[32,128,128]{2,1,0:T(8,128)(2,1)S(1)}, bf16[16,2,8,2,16,128]{5,4,3,2,1,0:T(8,128)(2,1)S(1)}) custom-call(s32[8,128]{1,0:T(8,128)S(1)} %bitcast.18, f32[2,128]{1,0:T(2,128)S(1)} %copy-done.5, f32[2,128]{1,0:T(2,128)S(1)} %copy-done.6, bf16[16,2,8,16,128]{4,3,2,1,0:T(8,128)(2,1)S(1)} %bitcast.12, bf16[32,128,128]{2,1,0:T(8,128)(2,1)S(1)} %copy-done, ...), custom_call_target="tpu_custom_call" | custom-call | tf_op jit(solution)/shard_map/finish_project/pallas_call | solution.py:306
  118.6 60.3 %all_to_all.22 = bf16[256,2,16,128]{3,2,1,0:T(8,128)(2,1)S(1)} all-to-all(bf16[256,2,16,128]{3,2,1,0:T(8,128)(2,1)S(1)} %bitcast.16), channel_id=1, replica_groups=mesh['xh'=2,'z'=8,'c'=2,'xl'=2,'y'=4] {'xh','z','c','xl','y'}, dimensions={0} | all-to-all | bytes 4194304 | tf_op jit(solution)/shard_map/all_to_all | solution.py:418
  178.9 1.1 incoming_send.1
  180.0 1.3 collective-permute-start.1
  181.4 1.1 output_gate.3.gate_ref
  182.4 1.2 collective-permute-done.1.other_ref
  183.6 0.7 incoming.1
  184.4 35.4 %all_to_all.23 = bf16[256,16,128]{2,1,0:T(8,128)(2,1)S(1)} all-to-all(bf16[256,16,128]{2,1,0:T(8,128)(2,1)S(1)} %bitcast.13), channel_id=1, replica_groups=mesh['xh'=2,'z'=8,'c'=2,'xl'=2,'y'=4] {'xh','z','c','xl','y'}, dimensions={0} | all-to-all | bytes 2097152 | tf_op jit(solution)/shard_map/all_to_all | solution.py:418
  219.8 2.5 %finish.1 = bf16[32,128,128]{2,1,0:T(8,128)(2,1)} custom-call(f32[2,128]{1,0:T(2,128)S(1)} %copy-done.6, bf16[16,2,8,16,128]{4,3,2,1,0:T(8,128)(2,1)S(1)} %bitcast.15, bf16[32,128,128]{2,1,0:T(8,128)(2,1)S(1)} %get-tuple-element.28.cells_ref, f32[32,128,128]{2,1,0:T(8,128)S(1)} %output_gate.3.gate_ref, bf16[2,128,128]{2,1,0:T(8,128)(2,1)S(1)} %copy-done.2), custom_call_target="tpu_custom_call" | custom-call | tf_op jit(solution)/shard_map/finish/pallas_call | solution.py:264
Async XLA Ops:
  73.6 1.4 copy-start
  73.6 1.4 copy-start.3
  73.6 1.4 copy-start.5
  73.6 3.8 %collective-permute-start = (bf16[32,8,16,128]{3,2,1,0:T(8,128)(2,1)S(1)}, bf16[32,8,16,128]{3,2,1,0:T(8,128)(2,1)S(1)}, u32[]{:S(2)}, u32[]{:S(2)}) collective-permute-start(bf16[32,8,16,128]{3,2,1,0:T(8,128)(2,1)S(1)} %take_right.1), channel_id=1, source_target_pairs={{0,8},{8,0},{1,9},{9,1},{2,10},{10,2},{3,11},{11,3},{4,12},{12,4},... | collective-permute-start | bytes 3145736 | tf_op jit(solution)/shard_map/ppermute | solution.py:431
  78.9 36.1 %copy-start.1 = (bf16[2,128,512]{2,1,0:T(8,128)(2,1)S(1)}, bf16[2,128,512]{2,1,0:T(8,128)(2,1)}, u32[]{:S(2)}) copy-start(bf16[2,128,512]{2,1,0:T(8,128)(2,1)} %proj_ref.1) | copy-start | bytes 786436
  78.9 36.1 %copy-start.2 = (bf16[2,128,128]{2,1,0:T(8,128)(2,1)S(1)}, bf16[2,128,128]{2,1,0:T(8,128)(2,1)}, u32[]{:S(2)}) copy-start(bf16[2,128,128]{2,1,0:T(8,128)(2,1)} %weight_ref.7) | copy-start | bytes 196612
  78.9 36.1 %copy-start.4 = (s32[1024]{0:T(1024)S(1)}, s32[1024]{0:T(1024)}, u32[]{:S(2)}) copy-start(s32[1024]{0:T(1024)} %param.8) | copy-start | bytes 12292
  78.9 36.1 %copy-start.6 = (f32[2,128]{1,0:T(2,128)S(1)}, f32[2,128]{1,0:T(2,128)}, u32[]{:S(2)}) copy-start(f32[2,128]{1,0:T(2,128)} %gain_ref.5) | copy-start | bytes 3076
  180.0 3.6 %collective-permute-start.1 = (bf16[512,1024]{1,0:T(8,128)(2,1)S(1)}, bf16[512,1024]{1,0:T(8,128)(2,1)S(1)}, u32[]{:S(2)}, u32[]{:S(2)}) collective-permute-start(bf16[512,1024]{1,0:T(8,128)(2,1)S(1)} %get-tuple-element.27), channel_id=1, source_target_pairs={{0,8},{8,0},{1,9},{9,1},{2,10},{10,2},{3,11},{11,3},{4,12},{12,4},... | collective-permute-start | bytes 3145736 | tf_op jit(solution)/shard_map/ppermute | solution.py:431

commit v7 on v5

--- a/solution.py
+++ b/solution.py
@@ -46,8 +46,8 @@
 
 
 HBM = pl.BlockSpec(memory_space=pltpu.HBM)
-PROJ_SCRATCH = [pltpu.VMEM((COLS, COLS), F32)] + [pltpu.VMEM((ROWS * CHAN_PITCH, COLS), F32)] * 2
-HIDDEN_SCRATCH = [pltpu.VMEM((CHAN, COLS), F32), pltpu.VMEM((CHAN * ROW_PITCH, COLS), F32)]
+PROJ_SCRATCH = [pltpu.VMEM((COLS, COLS), F32)] + [pltpu.VMEM((ROWS * CHAN_PITCH + CHAN, COLS), F32)] * 2
+HIDDEN_SCRATCH = [pltpu.VMEM((CHAN, COLS), F32), pltpu.VMEM((CHAN * ROW_PITCH + ROWS, COLS), F32)]
 PAIRS = jax.ShapeDtypeStruct((PLACES, 2, BLOCKS, 2, PART, COLS), BF16)
 CELLS = jax.ShapeDtypeStruct((ROWS, COLS, CHAN), BF16)
 TURNED = jax.ShapeDtypeStruct((ROWS, CHAN, COLS), BF16)
@@ -305,6 +305,15 @@
     return slice(block * COLS, (block + 1) * COLS)
 
 
+def take_right_kernel(pairs_ref, out_ref):
+    out_ref[...] = pairs_ref[:, :, 1]
+
+
+def take_right(pairs):
+    shape = jax.ShapeDtypeStruct((GROUPS, BLOCKS, PART, COLS), BF16)
+    return kernel_call(take_right_kernel, "take_right", [VMEM], shape)(pairs)
+
+
 def outgoing_kernel(pairs_ref, other_ref, out_ref, left, right):
     core = lax.axis_index("c")
     for block in range(BLOCKS):
@@ -398,7 +407,7 @@
 
     pairs, cells = project(mask, in_gain, pair_input, proj_weight)
     pairs = exchange_pairs(pairs)
-    other = to_other_core(pairs[:, :, 1])
+    other = to_other_core(take_right(pairs))
     gate = output_gate(0, in_gain, cells, gate_weight)
     product, gate = lax.optimization_barrier((outgoing(pairs, other), gate))
     hidden = exchange_product(product)

time: 223 us -> 222 us (level)
  no operation moved by 1% of the time
where the time goes in v7:
time: 222 us
  blocking collectives  200 us (90%)
  Pallas kernels  16.2 us (7%)
  starting transfers between devices  2.67 us (1%)
  waiting for transfers between devices  2.42 us (1%)
    all_to_all x4, blocking collectives, exchange(): lax.all_to_all(values, DEVICES, split_axis=0, concat_axis=0, tiled=True)  200 us
    pallas_call x1, Pallas kernels, project(): pl.pallas_call(project_kernel, in_specs=[HBM, HBM, HBM, HBM], out_specs=[...  4.6 us
  transfers between devices with their start and end apart: 2, of which 2 were waited for; matrix products, arithmetic and copies ran while one was open for 0% of the time, Pallas kernels for 1%

profile of v7, /device:TPU:1, one launch (start us, length us, event | category | flops | bytes accessed | tf_op | source)
XLA Modules:
  0.0 221.7 jit_solution(9442038138704575169)
XLA Ops:
  0.0 4.6 %project.1 = (bf16[16,2,8,2,16,128]{5,4,3,2,1,0:T(8,128)(2,1)}, bf16[32,128,128]{2,1,0:T(8,128)(2,1)}) custom-call(s32[8,128]{1,0:T(8,128)} %bitcast.17, f32[2,128]{1,0:T(2,128)} %gain_ref.4, bf16[32,128,128]{2,1,0:T(8,128)(2,1)} %cells_hbm.1, bf16[2,128,512]{2,1,0:T(8,128)(2,1)} %proj_ref.1), custom_call_target="tpu_custom_call" | custom-call | tf_op jit(solution)/shard_map/project/pallas_call | solution.py:161
  4.6 68.9 %all_to_all.20 = bf16[256,2,16,128]{3,2,1,0:T(8,128)(2,1)S(1)} all-to-all(bf16[256,2,16,128]{3,2,1,0:T(8,128)(2,1)} %bitcast.19), channel_id=1, replica_groups=mesh['xh'=2,'z'=8,'c'=2,'xl'=2,'y'=4] {'xh','z','c','xl','y'}, dimensions={0} | all-to-all | bytes 4194304 | tf_op jit(solution)/shard_map/all_to_all | solution.py:389
  73.5 0.0 copy-start
  73.5 0.0 copy-start.3
  73.5 0.0 copy-start.5
  73.5 0.1 take_right.1
  73.6 1.3 collective-permute-start
  74.9 0.0 copy-done
  74.9 0.0 copy-done.3
  74.9 0.0 copy-done.5
  75.0 1.1 output_gate.2.gate_ref
  76.0 1.2 collective-permute-done.other_ref
  77.2 1.6 outgoing.1
  78.8 0.0 copy-start.1
  78.8 0.0 copy-start.2
  78.8 0.0 copy-start.4
  78.8 0.0 copy-start.6
  78.8 35.4 %all_to_all.21 = bf16[256,16,128]{2,1,0:T(8,128)(2,1)S(1)} all-to-all(bf16[256,16,128]{2,1,0:T(8,128)(2,1)S(1)} %bitcast.15), channel_id=1, replica_groups=mesh['xh'=2,'z'=8,'c'=2,'xl'=2,'y'=4] {'xh','z','c','xl','y'}, dimensions={0} | all-to-all | bytes 2097152 | tf_op jit(solution)/shard_map/all_to_all | solution.py:389
  114.2 0.0 copy-done.1
  114.2 0.0 copy-done.2
  114.2 0.0 copy-done.4
  114.2 0.0 copy-done.6
  114.2 3.5 %finish_project.1 = (bf16[32,128,128]{2,1,0:T(8,128)(2,1)S(1)}, bf16[16,2,8,2,16,128]{5,4,3,2,1,0:T(8,128)(2,1)S(1)}) custom-call(s32[8,128]{1,0:T(8,128)S(1)} %bitcast.18, f32[2,128]{1,0:T(2,128)S(1)} %copy-done.5, f32[2,128]{1,0:T(2,128)S(1)} %copy-done.6, bf16[16,2,8,16,128]{4,3,2,1,0:T(8,128)(2,1)S(1)} %bitcast.12, bf16[32,128,128]{2,1,0:T(8,128)(2,1)S(1)} %copy-done, ...), custom_call_target="tpu_custom_call" | custom-call | tf_op jit(solution)/shard_map/finish_project/pallas_call | solution.py:295
  117.8 60.3 %all_to_all.22 = bf16[256,2,16,128]{3,2,1,0:T(8,128)(2,1)S(1)} all-to-all(bf16[256,2,16,128]{3,2,1,0:T(8,128)(2,1)S(1)} %bitcast.16), channel_id=1, replica_groups=mesh['xh'=2,'z'=8,'c'=2,'xl'=2,'y'=4] {'xh','z','c','xl','y'}, dimensions={0} | all-to-all | bytes 4194304 | tf_op jit(solution)/shard_map/all_to_all | solution.py:389
  178.1 1.1 incoming_send.1
  179.3 1.3 collective-permute-start.1
  180.6 1.1 output_gate.3.gate_ref
  181.7 1.2 collective-permute-done.1.other_ref
  182.9 0.7 incoming.1
  183.6 35.4 %all_to_all.23 = bf16[256,16,128]{2,1,0:T(8,128)(2,1)S(1)} all-to-all(bf16[256,16,128]{2,1,0:T(8,128)(2,1)S(1)} %bitcast.13), channel_id=1, replica_groups=mesh['xh'=2,'z'=8,'c'=2,'xl'=2,'y'=4] {'xh','z','c','xl','y'}, dimensions={0} | all-to-all | bytes 2097152 | tf_op jit(solution)/shard_map/all_to_all | solution.py:389
  219.0 2.5 %finish.1 = bf16[32,128,128]{2,1,0:T(8,128)(2,1)} custom-call(f32[2,128]{1,0:T(2,128)S(1)} %copy-done.6, bf16[16,2,8,16,128]{4,3,2,1,0:T(8,128)(2,1)S(1)} %bitcast.14, bf16[32,128,128]{2,1,0:T(8,128)(2,1)S(1)} %get-tuple-element.24.cells_ref, f32[32,128,128]{2,1,0:T(8,128)S(1)} %output_gate.3.gate_ref, bf16[2,128,128]{2,1,0:T(8,128)(2,1)S(1)} %copy-done.2), custom_call_target="tpu_custom_call" | custom-call | tf_op jit(solution)/shard_map/finish/pallas_call | solution.py:253
Async XLA Ops:
  73.5 1.4 copy-start
  73.5 1.4 copy-start.3
  73.5 1.4 copy-start.5
  73.6 3.6 %collective-permute-start = (bf16[32,8,16,128]{3,2,1,0:T(8,128)(2,1)S(1)}, bf16[32,8,16,128]{3,2,1,0:T(8,128)(2,1)S(1)}, u32[]{:S(2)}, u32[]{:S(2)}) collective-permute-start(bf16[32,8,16,128]{3,2,1,0:T(8,128)(2,1)S(1)} %take_right.1), channel_id=1, source_target_pairs={{0,8},{8,0},{1,9},{9,1},{2,10},{10,2},{3,11},{11,3},{4,12},{12,4},... | collective-permute-start | bytes 3145736 | tf_op jit(solution)/shard_map/ppermute | solution.py:402
  78.8 35.4 %copy-start.1 = (bf16[2,128,512]{2,1,0:T(8,128)(2,1)S(1)}, bf16[2,128,512]{2,1,0:T(8,128)(2,1)}, u32[]{:S(2)}) copy-start(bf16[2,128,512]{2,1,0:T(8,128)(2,1)} %proj_ref.1) | copy-start | bytes 786436
  78.8 35.4 %copy-start.2 = (bf16[2,128,128]{2,1,0:T(8,128)(2,1)S(1)}, bf16[2,128,128]{2,1,0:T(8,128)(2,1)}, u32[]{:S(2)}) copy-start(bf16[2,128,128]{2,1,0:T(8,128)(2,1)} %weight_ref.7) | copy-start | bytes 196612
  78.8 35.4 %copy-start.4 = (s32[1024]{0:T(1024)S(1)}, s32[1024]{0:T(1024)}, u32[]{:S(2)}) copy-start(s32[1024]{0:T(1024)} %param.8) | copy-start | bytes 12292
  78.8 35.4 %copy-start.6 = (f32[2,128]{1,0:T(2,128)S(1)}, f32[2,128]{1,0:T(2,128)}, u32[]{:S(2)}) copy-start(f32[2,128]{1,0:T(2,128)} %gain_ref.5) | copy-start | bytes 3076
  179.3 3.6 %collective-permute-start.1 = (bf16[512,1024]{1,0:T(8,128)(2,1)S(1)}, bf16[512,1024]{1,0:T(8,128)(2,1)S(1)}, u32[]{:S(2)}, u32[]{:S(2)}) collective-permute-start(bf16[512,1024]{1,0:T(8,128)(2,1)S(1)} %get-tuple-element.23), channel_id=1, source_target_pairs={{0,8},{8,0},{1,9},{9,1},{2,10},{10,2},{3,11},{11,3},{4,12},{12,4},... | collective-permute-start | bytes 3145736 | tf_op jit(solution)/shard_map/ppermute | solution.py:402

commit v8 on v4

--- a/solution.py
+++ b/solution.py
@@ -11,12 +11,16 @@
 CHAN = 128
 ROWS = 32
 COLS = 128
+GROUPS = 16
+DEPTH = 8
+BLOCKS = 8
 SUB = 16
 CHUNK = 16
 SPAN = 32
 CHAN_PITCH = CHAN + 1
 ROW_PITCH = ROWS + 1
 PEERS = ("xh", "z", "xl", "y")
+PLANE = ("xh", "xl", "y")
 F32 = jnp.float32
 BF16 = jnp.bfloat16
 MIB = 1024 * 1024
@@ -43,8 +47,8 @@
 
 
 HBM = pl.BlockSpec(memory_space=pltpu.HBM)
-PROJ_SCRATCH = [pltpu.VMEM((COLS, COLS), F32)] + [pltpu.VMEM((ROWS * CHAN_PITCH, COLS), F32)] * 2
-HIDDEN_SCRATCH = [pltpu.VMEM((CHAN, COLS), F32), pltpu.VMEM((CHAN * ROW_PITCH, COLS), F32)]
+PROJ_SCRATCH = [pltpu.VMEM((COLS, COLS), F32)] + [pltpu.VMEM((ROWS * CHAN_PITCH + CHAN, COLS), F32)] * 2
+HIDDEN_SCRATCH = [pltpu.VMEM((CHAN, COLS), F32), pltpu.VMEM((CHAN * ROW_PITCH + ROWS, COLS), F32)]
 PAIRS = jax.ShapeDtypeStruct((CHAN, 2, ROWS, COLS), BF16)
 CELLS = jax.ShapeDtypeStruct((ROWS, COLS, CHAN), BF16)
 TURNED = jax.ShapeDtypeStruct((ROWS, CHAN, COLS), BF16)
@@ -206,12 +210,14 @@
         centred = hidden - average[None]
         scale = lax.rsqrt(jnp.mean(centred * centred, axis=0) + EPSILON)
 
-        def body(chan, carry):
-            values = (hidden_ref[chan, rows].astype(F32) - average) * scale * gains[pl.ds(chan, 1), :]
-            scratch[pl.ds(chan * ROW_PITCH + first, 16), :] = values
+        def body(place, carry):
+            for block in range(BLOCKS):
+                chan = place % DEPTH * 2 * BLOCKS + place // DEPTH * BLOCKS + block
+                values = (hidden_ref[place * BLOCKS + block, rows].astype(F32) - average) * scale
+                scratch[pl.ds(chan * ROW_PITCH + first, 16), :] = values * gains[pl.ds(chan, 1), :]
             return carry
 
-        lax.fori_loop(0, CHAN, body, 0, unroll=8)
+        lax.fori_loop(0, GROUPS, body, 0)
 
 
 def updated_rows(first, scratch, weight, cells_ref, gate_ref):
@@ -289,8 +295,6 @@
     return call(mask, in_gain, out_gain, hidden, cells, gate, weight, proj)
 
 
-GROUPS = 16
-BLOCKS = 8
 TOKENS = BLOCKS * COLS
 HALF = GROUPS * ROWS
 PRODUCT = jax.ShapeDtypeStruct((GROUPS, BLOCKS, ROWS, COLS), BF16)
@@ -300,11 +304,24 @@
     return slice(block * COLS, (block + 1) * COLS)
 
 
+def side(pairs_ref, block, which):
+    return pairs_ref[:, block, :, which].reshape(GROUPS, ROWS, COLS)
+
+
+def take_right_kernel(pairs_ref, out_ref):
+    for block in range(BLOCKS):
+        out_ref[:, block] = side(pairs_ref, block, 1)
+
+
+def take_right(pairs):
+    return kernel_call(take_right_kernel, "take_right", [VMEM], PRODUCT)(pairs)
+
+
 def outgoing_kernel(pairs_ref, other_ref, out_ref, left, right):
     core = lax.axis_index("c")
     for block in range(BLOCKS):
-        left[:, :, block_lanes(block)] = pairs_ref[:, block, 0]
-        right[:, core, :, block_lanes(block)] = pairs_ref[:, block, 1]
+        left[:, :, block_lanes(block)] = side(pairs_ref, block, 0)
+        right[:, core, :, block_lanes(block)] = side(pairs_ref, block, 1)
         right[:, 1 - core, :, block_lanes(block)] = other_ref[:, block]
     left_rows = left[...].reshape(HALF, TOKENS)
     for block in range(0, BLOCKS, 2):
@@ -333,8 +350,8 @@
 def incoming_send_kernel(pairs_ref, send_ref, left_ref, right_ref, turned):
     core = lax.axis_index("c")
     for block in range(BLOCKS):
-        right_ref[:, block_lanes(block)] = pairs_ref[:, block, 1].reshape(HALF, COLS)
-        left = pairs_ref[:, block, 0].reshape(HALF, COLS)
+        right_ref[:, block_lanes(block)] = side(pairs_ref, block, 1).reshape(HALF, COLS)
+        left = side(pairs_ref, block, 0).reshape(HALF, COLS)
         turned[2 * block : 2 * block + 2] = jnp.transpose(left).reshape(2, 2, ROWS, HALF)
     left_ref[...] = turned[:, core].reshape(HALF, HALF)
     send_ref[...] = jnp.dot(
@@ -375,6 +392,23 @@
     return lax.all_to_all(values, PEERS, split_axis=0, concat_axis=0, tiled=True)
 
 
+def planes_first(pairs):
+    pairs = jnp.swapaxes(lax.all_to_all(pairs, "z", split_axis=0, concat_axis=0, tiled=True), 0, 1)
+    return lax.all_to_all(pairs, PLANE, split_axis=0, concat_axis=0, tiled=True)
+
+
+def planes_last(pairs):
+    pairs = jnp.swapaxes(pairs, 0, 1)
+    pairs = jnp.swapaxes(lax.all_to_all(pairs, PLANE, split_axis=0, concat_axis=0, tiled=True), 0, 1)
+    return jnp.swapaxes(lax.all_to_all(pairs, "z", split_axis=0, concat_axis=0, tiled=True), 0, 1)
+
+
+def exchange_pairs(pairs):
+    pairs = pairs.reshape(DEPTH, 2 * BLOCKS, 2 * ROWS, COLS)
+    pairs = lax.cond(lax.axis_index("c") == 0, planes_first, planes_last, pairs)
+    return pairs.reshape(2, BLOCKS, DEPTH, 2, ROWS, COLS)
+
+
 def to_other_core(values):
     return lax.ppermute(values, "c", [(0, 1), (1, 0)])
 
@@ -383,14 +417,14 @@
     mask = token_mask.reshape(BLOCKS, COLS)
 
     pairs, cells = project(mask, in_gain, pair_input, proj_weight)
-    pairs = exchange(pairs).reshape(GROUPS, BLOCKS, 2, ROWS, COLS)
-    other = to_other_core(pairs[:, :, 1])
+    pairs = exchange_pairs(pairs)
+    other = to_other_core(take_right(pairs))
     gate = output_gate(0, in_gain, cells, gate_weight)
     product, gate = lax.optimization_barrier((outgoing(pairs, other), gate))
     hidden = exchange(product.reshape(CHAN, ROWS, COLS))
     cells, pairs = finish_project(mask, in_gain, out_gain, hidden, cells, gate, out_weight, proj_weight)
 
-    pairs = exchange(pairs).reshape(GROUPS, BLOCKS, 2, ROWS, COLS)
+    pairs = exchange_pairs(pairs)
     send, left, right = incoming_send(pairs)
     other = to_other_core(send)
     gate = output_gate(1, in_gain, cells, gate_weight)

time: 225 us -> 224 us (level)
  blocking collectives: 198 us -> 195 us
    all_to_all x4 -> x2, blocking collectives: 198 us -> 75.6 us  [exchange(): lax.all_to_all(values, PEERS, split_axis=0, concat_axis=0, tiled=True)]
    all_to_all x0 -> x4, blocking collectives: none -> 119 us  [the longest x2 73.8 us: planes_last(): lax.all_to_all(pairs, 'z', split_axis=0, concat_axis=0, tiled=True)]
where the time goes in v8:
time: 224 us; the launch traced here: 223 us
  blocking collectives  195 us (87%)
  Pallas kernels  15.6 us (7%)
  starting transfers between devices  8.85 us (4%)
  waiting for transfers between devices  2.44 us (1%)
    all_to_all x2, blocking collectives, exchange(): lax.all_to_all(values, PEERS, split_axis=0, concat_axis=0, tiled=True)  75.6 us
    all_to_all x2, blocking collectives, planes_last(): lax.all_to_all(pairs, 'z', split_axis=0, concat_axis=0, tiled=True)  73.8 us
    all_to_all x2, blocking collectives, planes_last(): lax.all_to_all(pairs, PLANE, split_axis=0, concat_axis=0, tiled=True)  45 us
    ppermute x2, starting transfers between devices, to_other_core(): return lax.ppermute(values, 'c', [(0, 1), (1, 0)])  8.85 us
  transfers between devices with their start and end apart: 2, of which 2 were waited for; matrix products, arithmetic and copies ran while one was open for 0% of the time, Pallas kernels for 1%

profile of v8, /device:TPU:1, one launch (start us, length us, event | category | flops | bytes accessed | tf_op | source)
XLA Modules:
  0.0 223.3 jit_solution(9686101834887277267)
XLA Ops:
  0.0 3.7 %project.1 = (bf16[128,2,32,128]{3,2,1,0:T(8,128)(2,1)S(1)}, bf16[32,128,128]{2,1,0:T(8,128)(2,1)}) custom-call(s32[8,128]{1,0:T(8,128)} %bitcast.24, f32[2,128]{1,0:T(2,128)} %gain_ref.4, bf16[32,128,128]{2,1,0:T(8,128)(2,1)} %cells_hbm.1, bf16[2,128,512]{2,1,0:T(8,128)(2,1)} %proj_ref.1), custom_call_target="tpu_custom_call" | custom-call | tf_op jit(solution)/shard_map/project/pallas_call | solution.py:160
  3.7 62.9 %conditional.2 = (bf16[2,8,8,2,32,128]{5,4,3,2,1,0:T(8,128)(2,1)S(1)}) conditional(s32[]{:T(128)} %convert_element_type.4, bf16[8,16,64,128]{3,2,1,0:T(8,128)(2,1)S(1)} %bitcast.29, bf16[8,16,64,128]{3,2,1,0:T(8,128)(2,1)S(1)} %bitcast.30), branch_computations={%region_0.0_spmd, %region_1.0_spmd} | conditional | bytes 20971528 | solution.py:408
  3.7 0.2 copy.30
  3.9 24.9 %all_to_all.42 = bf16[16,8,64,128]{3,2,1,0:T(8,128)(2,1)S(1)} all-to-all(bf16[16,8,64,128]{3,2,1,0:T(8,128)(2,1)S(1)} %bitcast.35), channel_id=1, replica_groups=mesh['xh'=2,'z'=8,'c'=2,'xl'=2,'y'=4] {'xh','xl','y'}, dimensions={0} | all-to-all | bytes 4194304 | tf_op jit(solution)/shard_map/cond/branch_0_fun/all_to_all | solution.py:402
  28.8 0.2 copy.15
  29.0 37.2 %all_to_all.43 = bf16[8,16,64,128]{3,2,1,0:T(8,128)(2,1)S(1)} all-to-all(bf16[8,16,64,128]{3,2,1,0:T(8,128)(2,1)S(1)} %copy.15), channel_id=1, replica_groups=mesh['xh'=2,'z'=8,'c'=2,'xl'=2,'y'=4] {'z'}, dimensions={0} | all-to-all | bytes 4194304 | tf_op jit(solution)/shard_map/cond/branch_0_fun/all_to_all | solution.py:403
  66.2 0.4 copy.26
  66.6 0.0 copy-start
  66.6 0.0 copy-start.3
  66.6 0.0 copy-start.5
  66.6 0.1 take_right.1
  66.7 5.1 %collective-permute-start = (bf16[16,8,32,128]{3,2,1,0:T(8,128)(2,1)S(1)}, bf16[16,8,32,128]{3,2,1,0:T(8,128)(2,1)S(1)}, u32[]{:S(2)}, u32[]{:S(2)}) collective-permute-start(bf16[16,8,32,128]{3,2,1,0:T(8,128)(2,1)S(1)} %take_right.1), channel_id=1, source_target_pairs={{0,8},{8,0},{1,9},{9,1},{2,10},{10,2},{3,11},{11,3},{4,12},{12,4},... | collective-permute-start | bytes 3145736 | tf_op jit(solution)/shard_map/ppermute | solution.py:413
  71.8 0.0 copy-done
  71.8 0.0 copy-done.3
  71.8 0.0 copy-done.5
  71.8 1.1 output_gate.2.gate_ref
  72.9 1.2 collective-permute-done.other_ref
  74.1 1.6 outgoing.1
  75.7 0.0 copy-start.1
  75.7 0.0 copy-start.2
  75.8 0.0 copy-start.4
  75.8 0.0 copy-start.6
  75.8 37.6 %all_to_all.50.hidden_ref = bf16[128,32,128]{2,1,0:T(8,128)(2,1)S(1)} all-to-all(bf16[128,32,128]{2,1,0:T(8,128)(2,1)S(1)} %bitcast.23), channel_id=1, replica_groups=mesh['xh'=2,'z'=8,'c'=2,'xl'=2,'y'=4] {'xh','z','xl','y'}, dimensions={0} | all-to-all | bytes 2097152 | tf_op jit(solution)/shard_map/all_to_all | solution.py:392
  113.3 0.0 copy-done.1
  113.3 0.0 copy-done.2
  113.3 0.0 copy-done.4
  113.3 0.0 copy-done.6
  113.4 3.7 %finish_project.1 = (bf16[32,128,128]{2,1,0:T(8,128)(2,1)S(1)}, bf16[128,2,32,128]{3,2,1,0:T(8,128)(2,1)S(1)}) custom-call(s32[8,128]{1,0:T(8,128)S(1)} %bitcast.25, f32[2,128]{1,0:T(2,128)S(1)} %copy-done.5, f32[2,128]{1,0:T(2,128)S(1)} %copy-done.6, bf16[128,32,128]{2,1,0:T(8,128)(2,1)S(1)} %all_to_all.50.hidden_ref, bf16[32,128,128]{2,1,0:T(8,128)(2,1)S(1)} %copy-done, ...), custom_call_target="tpu_custom_call" | custom-call | tf_op jit(solution)/shard_map/finish_project/pallas_call | solution.py:295
  117.1 57.3 %conditional.3 = (bf16[16,8,64,128]{3,2,0,1:T(8,128)(2,1)S(1)}) conditional(s32[]{:T(128)} %convert_element_type.4, bf16[8,16,64,128]{3,2,1,0:T(8,128)(2,1)S(1)} %bitcast.27, bf16[8,16,64,128]{3,2,1,0:T(8,128)(2,1)S(1)} %bitcast.28), branch_computations={%region_2.0_spmd, %region_3.0_spmd} | conditional | bytes 16777224 | solution.py:408
  117.1 0.2 copy.31
  117.3 20.1 %all_to_all.46 = bf16[16,8,64,128]{3,2,1,0:T(8,128)(2,1)S(1)} all-to-all(bf16[16,8,64,128]{3,2,1,0:T(8,128)(2,1)S(1)} %bitcast.37), channel_id=1, replica_groups=mesh['xh'=2,'z'=8,'c'=2,'xl'=2,'y'=4] {'xh','xl','y'}, dimensions={0} | all-to-all | bytes 4194304 | tf_op jit(solution)/shard_map/cond/branch_0_fun/all_to_all | solution.py:402
  137.5 0.2 copy.18
  137.7 36.7 %all_to_all.47 = bf16[8,16,64,128]{3,2,1,0:T(8,128)(2,1)S(1)} all-to-all(bf16[8,16,64,128]{3,2,1,0:T(8,128)(2,1)S(1)} %copy.18), channel_id=1, replica_groups=mesh['xh'=2,'z'=8,'c'=2,'xl'=2,'y'=4] {'z'}, dimensions={0} | all-to-all | bytes 4194304 | tf_op jit(solution)/shard_map/cond/branch_0_fun/all_to_all | solution.py:403
  174.4 0.2 copy.25
  174.6 1.1 incoming_send.1
  175.7 3.8 %collective-permute-start.1 = (bf16[512,1024]{1,0:T(8,128)(2,1)S(1)}, bf16[512,1024]{1,0:T(8,128)(2,1)S(1)}, u32[]{:S(2)}, u32[]{:S(2)}) collective-permute-start(bf16[512,1024]{1,0:T(8,128)(2,1)S(1)} %get-tuple-element.36), channel_id=1, source_target_pairs={{0,8},{8,0},{1,9},{9,1},{2,10},{10,2},{3,11},{11,3},{4,12},{12,4},... | collective-permute-start | bytes 3145736 | tf_op jit(solution)/shard_map/ppermute | solution.py:413
  179.4 1.1 output_gate.3.gate_ref
  180.5 1.2 collective-permute-done.1.other_ref
  181.7 0.7 incoming.1
  182.4 38.1 %all_to_all.51.hidden_ref = bf16[128,32,128]{2,1,0:T(8,128)(2,1)S(1)} all-to-all(bf16[128,32,128]{2,1,0:T(8,128)(2,1)S(1)} %bitcast.22), channel_id=1, replica_groups=mesh['xh'=2,'z'=8,'c'=2,'xl'=2,'y'=4] {'xh','z','xl','y'}, dimensions={0} | all-to-all | bytes 2097152 | tf_op jit(solution)/shard_map/all_to_all | solution.py:392
  220.5 2.6 %finish.1 = bf16[32,128,128]{2,1,0:T(8,128)(2,1)} custom-call(f32[2,128]{1,0:T(2,128)S(1)} %copy-done.6, bf16[128,32,128]{2,1,0:T(8,128)(2,1)S(1)} %all_to_all.51.hidden_ref, bf16[32,128,128]{2,1,0:T(8,128)(2,1)S(1)} %get-tuple-element.37.cells_ref, f32[32,128,128]{2,1,0:T(8,128)S(1)} %output_gate.3.gate_ref, bf16[2,128,128]{2,1,0:T(8,128)(2,1)S(1)} %copy-done.2), custom_call_target="tpu_custom_call" | custom-call | tf_op jit(solution)/shard_map/finish/pallas_call | solution.py:253
Async XLA Ops:
  66.6 5.2 %copy-start = (bf16[32,128,128]{2,1,0:T(8,128)(2,1)S(1)}, bf16[32,128,128]{2,1,0:T(8,128)(2,1)}, u32[]{:S(2)}) copy-start(bf16[32,128,128]{2,1,0:T(8,128)(2,1)} %get-tuple-element.30.cells_ref) | copy-start | bytes 3145732
  66.6 5.2 %copy-start.3 = (bf16[2,128,128]{2,1,0:T(8,128)(2,1)S(1)}, bf16[2,128,128]{2,1,0:T(8,128)(2,1)}, u32[]{:S(2)}) copy-start(bf16[2,128,128]{2,1,0:T(8,128)(2,1)} %weight_ref.6) | copy-start | bytes 196612
  66.6 5.2 %copy-start.5 = (f32[2,128]{1,0:T(2,128)S(1)}, f32[2,128]{1,0:T(2,128)}, u32[]{:S(2)}) copy-start(f32[2,128]{1,0:T(2,128)} %gain_ref.4) | copy-start | bytes 3076
  66.7 7.4 %collective-permute-start = (bf16[16,8,32,128]{3,2,1,0:T(8,128)(2,1)S(1)}, bf16[16,8,32,128]{3,2,1,0:T(8,128)(2,1)S(1)}, u32[]{:S(2)}, u32[]{:S(2)}) collective-permute-start(bf16[16,8,32,128]{3,2,1,0:T(8,128)(2,1)S(1)} %take_right.1), channel_id=1, source_target_pairs={{0,8},{8,0},{1,9},{9,1},{2,10},{10,2},{3,11},{11,3},{4,12},{12,4},... | collective-permute-start | bytes 3145736 | tf_op jit(solution)/shard_map/ppermute | solution.py:413
  75.7 37.6 %copy-start.1 = (bf16[2,128,512]{2,1,0:T(8,128)(2,1)S(1)}, bf16[2,128,512]{2,1,0:T(8,128)(2,1)}, u32[]{:S(2)}) copy-start(bf16[2,128,512]{2,1,0:T(8,128)(2,1)} %proj_ref.1) | copy-start | bytes 786436
  75.7 37.6 %copy-start.2 = (bf16[2,128,128]{2,1,0:T(8,128)(2,1)S(1)}, bf16[2,128,128]{2,1,0:T(8,128)(2,1)}, u32[]{:S(2)}) copy-start(bf16[2,128,128]{2,1,0:T(8,128)(2,1)} %weight_ref.7) | copy-start | bytes 196612
  75.8 37.6 %copy-start.4 = (s32[1024]{0:T(1024)S(1)}, s32[1024]{0:T(1024)}, u32[]{:S(2)}) copy-start(s32[1024]{0:T(1024)} %param.12) | copy-start | bytes 12292
  75.8 37.6 %copy-start.6 = (f32[2,128]{1,0:T(2,128)S(1)}, f32[2,128]{1,0:T(2,128)}, u32[]{:S(2)}) copy-start(f32[2,128]{1,0:T(2,128)} %gain_ref.5) | copy-start | bytes 3076
  175.7 6.0 %collective-permute-start.1 = (bf16[512,1024]{1,0:T(8,128)(2,1)S(1)}, bf16[512,1024]{1,0:T(8,128)(2,1)S(1)}, u32[]{:S(2)}, u32[]{:S(2)}) collective-permute-start(bf16[512,1024]{1,0:T(8,128)(2,1)S(1)} %get-tuple-element.36), channel_id=1, source_target_pairs={{0,8},{8,0},{1,9},{9,1},{2,10},{10,2},{3,11},{11,3},{4,12},{12,4},... | collective-permute-start | bytes 3145736 | tf_op jit(solution)/shard_map/ppermute | solution.py:413

commit v9 on v8

--- a/solution.py
+++ b/solution.py
@@ -13,13 +13,13 @@
 COLS = 128
 GROUPS = 16
 DEPTH = 8
+CHIPS = 16
 BLOCKS = 8
 SUB = 16
 CHUNK = 16
 SPAN = 32
 CHAN_PITCH = CHAN + 1
 ROW_PITCH = ROWS + 1
-PEERS = ("xh", "z", "xl", "y")
 PLANE = ("xh", "xl", "y")
 F32 = jnp.float32
 BF16 = jnp.bfloat16
@@ -205,19 +205,19 @@
     gains[...] = channel_column(gain_ref, module)
     for first in range(0, ROWS, 16):
         rows = slice(first, first + 16)
-        hidden = hidden_ref[:, rows].astype(F32)
+        hidden = hidden_ref[:, :, rows].astype(F32).reshape(CHAN, 16, COLS)
         average = jnp.mean(hidden, axis=0)
         centred = hidden - average[None]
         scale = lax.rsqrt(jnp.mean(centred * centred, axis=0) + EPSILON)
 
-        def body(place, carry):
-            for block in range(BLOCKS):
-                chan = place % DEPTH * 2 * BLOCKS + place // DEPTH * BLOCKS + block
-                values = (hidden_ref[place * BLOCKS + block, rows].astype(F32) - average) * scale
+        def body(chip, carry):
+            for plane in range(DEPTH):
+                chan = plane * CHIPS + chip
+                values = (hidden_ref[chip, plane, rows].astype(F32) - average) * scale
                 scratch[pl.ds(chan * ROW_PITCH + first, 16), :] = values * gains[pl.ds(chan, 1), :]
             return carry
 
-        lax.fori_loop(0, GROUPS, body, 0)
+        lax.fori_loop(0, CHIPS, body, 0)
 
 
 def updated_rows(first, scratch, weight, cells_ref, gate_ref):
@@ -297,7 +297,7 @@
 
 TOKENS = BLOCKS * COLS
 HALF = GROUPS * ROWS
-PRODUCT = jax.ShapeDtypeStruct((GROUPS, BLOCKS, ROWS, COLS), BF16)
+PRODUCT = jax.ShapeDtypeStruct((DEPTH, 2, BLOCKS, ROWS, COLS), BF16)
 
 
 def block_lanes(block):
@@ -314,7 +314,15 @@
 
 
 def take_right(pairs):
-    return kernel_call(take_right_kernel, "take_right", [VMEM], PRODUCT)(pairs)
+    shape = jax.ShapeDtypeStruct((GROUPS, BLOCKS, ROWS, COLS), BF16)
+    return kernel_call(take_right_kernel, "take_right", [VMEM], shape)(pairs)
+
+
+def store_product(product, out_ref, block):
+    for half in range(2):
+        columns = product[:, block_lanes(half)].reshape(2, DEPTH, ROWS, COLS)
+        for side_x in range(2):
+            out_ref[:, side_x, block + half] = columns[side_x]
 
 
 def outgoing_kernel(pairs_ref, other_ref, out_ref, left, right):
@@ -332,8 +340,7 @@
             (((1,), (1,)), ((), ())),
             preferred_element_type=F32,
         ).astype(BF16)
-        for half in range(2):
-            out_ref[:, block + half] = product[:, block_lanes(half)].reshape(GROUPS, ROWS, COLS)
+        store_product(product, out_ref, block)
 
 
 def outgoing(pairs, other):
@@ -380,16 +387,11 @@
         lanes = slice(block * COLS, (block + 2) * COLS)
         total = jnp.dot(left, right_ref[:, lanes], preferred_element_type=F32)
         product = (total + other_ref[:, lanes].astype(F32)).astype(BF16)
-        for half in range(2):
-            out_ref[:, block + half] = product[:, block_lanes(half)].reshape(GROUPS, ROWS, COLS)
+        store_product(product, out_ref, block)
 
 
 def incoming(left, right, other):
     return kernel_call(incoming_kernel, "incoming", [VMEM, VMEM, VMEM], PRODUCT)(left, right, other)
-
-
-def exchange(values):
-    return lax.all_to_all(values, PEERS, split_axis=0, concat_axis=0, tiled=True)
 
 
 def planes_first(pairs):
@@ -403,10 +405,17 @@
     return jnp.swapaxes(lax.all_to_all(pairs, "z", split_axis=0, concat_axis=0, tiled=True), 0, 1)
 
 
-def exchange_pairs(pairs):
-    pairs = pairs.reshape(DEPTH, 2 * BLOCKS, 2 * ROWS, COLS)
-    pairs = lax.cond(lax.axis_index("c") == 0, planes_first, planes_last, pairs)
+def exchange(values, first_core):
+    return lax.cond(lax.axis_index("c") == first_core, planes_first, planes_last, values)
+
+
+def exchange_pairs(pairs, first_core):
+    pairs = exchange(pairs.reshape(DEPTH, CHIPS, 2 * ROWS, COLS), first_core)
     return pairs.reshape(2, BLOCKS, DEPTH, 2, ROWS, COLS)
+
+
+def exchange_product(product, first_core):
+    return exchange(product.reshape(DEPTH, CHIPS, ROWS, COLS), first_core)
 
 
 def to_other_core(values):
@@ -417,19 +426,19 @@
     mask = token_mask.reshape(BLOCKS, COLS)
 
     pairs, cells = project(mask, in_gain, pair_input, proj_weight)
-    pairs = exchange_pairs(pairs)
+    pairs = exchange_pairs(pairs, 0)
     other = to_other_core(take_right(pairs))
     gate = output_gate(0, in_gain, cells, gate_weight)
     product, gate = lax.optimization_barrier((outgoing(pairs, other), gate))
-    hidden = exchange(product.reshape(CHAN, ROWS, COLS))
+    hidden = exchange_product(product, 0)
     cells, pairs = finish_project(mask, in_gain, out_gain, hidden, cells, gate, out_weight, proj_weight)
 
-    pairs = exchange_pairs(pairs)
+    pairs = exchange_pairs(pairs, 1)
     send, left, right = incoming_send(pairs)
     other = to_other_core(send)
     gate = output_gate(1, in_gain, cells, gate_weight)
     product, gate = lax.optimization_barrier((incoming(left, right, other), gate))
-    hidden = exchange(product.reshape(CHAN, ROWS, COLS))
+    hidden = exchange_product(product, 0)
     return finish(out_gain, hidden, cells, gate, out_weight)
 
 

time: 224 us -> 220 us (0.982)
  blocking collectives: 195 us -> 185 us
    all_to_all x2, blocking collectives: 75.6 us -> 52 us  [the longest x1 31.4 us: planes_first(): lax.all_to_all(pairs, 'z', split_axis=0, concat_axis=0, tiled=True)]
    all_to_all x2 -> x3, blocking collectives: 45 us -> 54.4 us  [planes_last(): lax.all_to_all(pairs, PLANE, split_axis=0, concat_axis=0, tiled=True)]
    all_to_all x2 -> x3, blocking collectives: 73.8 us -> 78.8 us  [planes_last(): lax.all_to_all(pairs, 'z', split_axis=0, concat_axis=0, tiled=True)]
where the time goes in v9:
time: 220 us
  blocking collectives  185 us (84%)
  Pallas kernels  17.4 us (8%)
  starting transfers between devices  10.4 us (5%)
  local copies, waits for them, and re-layouts  3.11 us (1%)
  waiting for transfers between devices  2.78 us (1%)
    all_to_all x3, blocking collectives, planes_last(): lax.all_to_all(pairs, 'z', split_axis=0, concat_axis=0, tiled=True)  78.8 us
    all_to_all x3, blocking collectives, planes_last(): lax.all_to_all(pairs, PLANE, split_axis=0, concat_axis=0, tiled=True)  54.4 us
    all_to_all x1, blocking collectives, planes_first(): lax.all_to_all(pairs, 'z', split_axis=0, concat_axis=0, tiled=True)  31.4 us
    all_to_all x1, blocking collectives, planes_first(): return lax.all_to_all(pairs, PLANE, split_axis=0, concat_axis=0, tiled=True)  20.6 us
    ppermute x2, starting transfers between devices, to_other_core(): return lax.ppermute(values, 'c', [(0, 1), (1, 0)])  10.4 us
  transfers between devices with their start and end apart: 2, of which 2 were waited for; matrix products, arithmetic and copies ran while one was open for 0% of the time, Pallas kernels for 1%

profile of v9, /device:TPU:1, one launch (start us, length us, event | category | flops | bytes accessed | tf_op | source)
XLA Modules:
  0.0 219.5 jit_solution(2571472651367660190)
XLA Ops:
  0.0 3.7 %project.1 = (bf16[128,2,32,128]{3,2,1,0:T(8,128)(2,1)S(1)}, bf16[32,128,128]{2,1,0:T(8,128)(2,1)}) custom-call(s32[8,128]{1,0:T(8,128)} %bitcast.34, f32[2,128]{1,0:T(2,128)} %gain_ref.4, bf16[32,128,128]{2,1,0:T(8,128)(2,1)} %cells_hbm.1, bf16[2,128,512]{2,1,0:T(8,128)(2,1)} %proj_ref.1), custom_call_target="tpu_custom_call" | custom-call | tf_op jit(solution)/shard_map/project/pallas_call | solution.py:160
  3.7 63.0 %conditional.4 = (bf16[2,8,8,2,32,128]{5,4,3,2,1,0:T(8,128)(2,1)S(1)}) conditional(s32[]{:T(128)} %convert_element_type.8, bf16[8,16,64,128]{3,2,1,0:T(8,128)(2,1)S(1)} %bitcast.43, bf16[8,16,64,128]{3,2,1,0:T(8,128)(2,1)S(1)} %bitcast.44), branch_computations={%region_0.0_spmd, %region_1.0_spmd} | conditional | bytes 20971528 | solution.py:409
  3.7 0.2 copy.52
  3.9 24.9 %all_to_all.64 = bf16[16,8,64,128]{3,2,1,0:T(8,128)(2,1)S(1)} all-to-all(bf16[16,8,64,128]{3,2,1,0:T(8,128)(2,1)S(1)} %bitcast.49), channel_id=1, replica_groups=mesh['xh'=2,'z'=8,'c'=2,'xl'=2,'y'=4] {'xh','xl','y'}, dimensions={0} | all-to-all | bytes 4194304 | tf_op jit(solution)/shard_map/cond/branch_0_fun/all_to_all | solution.py:404
  28.8 0.2 copy.21
  29.0 37.2 %all_to_all.65 = bf16[8,16,64,128]{3,2,1,0:T(8,128)(2,1)S(1)} all-to-all(bf16[8,16,64,128]{3,2,1,0:T(8,128)(2,1)S(1)} %copy.21), channel_id=1, replica_groups=mesh['xh'=2,'z'=8,'c'=2,'xl'=2,'y'=4] {'z'}, dimensions={0} | all-to-all | bytes 4194304 | tf_op jit(solution)/shard_map/cond/branch_0_fun/all_to_all | solution.py:405
  66.2 0.4 copy.42
  66.6 0.0 copy-start.9
  66.6 0.0 copy-start
  66.7 0.0 copy-start.5
  66.7 0.0 copy-start.7
  66.7 1.1 take_right.1
  67.7 5.0 %collective-permute-start = (bf16[16,8,32,128]{3,2,1,0:T(8,128)(2,1)}, bf16[16,8,32,128]{3,2,1,0:T(8,128)(2,1)}, u32[]{:S(2)}, u32[]{:S(2)}) collective-permute-start(bf16[16,8,32,128]{3,2,1,0:T(8,128)(2,1)} %take_right.1), channel_id=1, source_target_pairs={{0,8},{8,0},{1,9},{9,1},{2,10},{10,2},{3,11},{11,3},{4,12},{12,4},... | collective-permute-start | bytes 3145736 | tf_op jit(solution)/shard_map/ppermute | solution.py:422
  72.7 0.0 copy-done.9
  72.7 0.0 copy-done
  72.7 0.0 copy-done.5
  72.7 0.0 copy-done.7
  72.7 0.0 copy-start.10
  72.7 1.0 output_gate.2.gate_ref
  73.8 1.5 collective-permute-done.other_ref
  75.4 0.0 copy-done.10
  75.4 2.8 %outgoing.1 = bf16[8,2,8,32,128]{4,3,2,1,0:T(8,128)(2,1)S(1)} custom-call(bf16[2,8,8,2,32,128]{5,4,3,2,1,0:T(8,128)(2,1)S(1)} %copy-done.10, bf16[16,8,32,128]{3,2,1,0:T(8,128)(2,1)} %collective-permute-done.other_ref), custom_call_target="tpu_custom_call" | custom-call | tf_op jit(solution)/shard_map/outgoing/pallas_call | solution.py:354
  78.2 0.0 copy-start.3
  78.2 0.0 copy-start.4
  78.2 0.0 copy-start.6
  78.2 0.0 copy-start.8
  78.2 36.3 %conditional.5 = (bf16[16,8,32,128]{3,2,1,0:T(8,128)(2,1)S(1)}) conditional(s32[]{:T(128)} %convert_element_type.8, bf16[8,16,32,128]{3,2,1,0:T(8,128)(2,1)S(1)} %bitcast.39, bf16[8,16,32,128]{3,2,1,0:T(8,128)(2,1)S(1)} %bitcast.40), branch_computations={%region_2.0_spmd, %region_3.0_spmd} | conditional | bytes 10485768 | solution.py:409
  78.3 0.1 copy.53
  78.4 14.7 %all_to_all.68 = bf16[16,8,32,128]{3,2,1,0:T(8,128)(2,1)S(1)} all-to-all(bf16[16,8,32,128]{3,2,1,0:T(8,128)(2,1)S(1)} %bitcast.57), channel_id=1, replica_groups=mesh['xh'=2,'z'=8,'c'=2,'xl'=2,'y'=4] {'xh','xl','y'}, dimensions={0} | all-to-all | bytes 2097152 | tf_op jit(solution)/shard_map/cond/branch_0_fun/all_to_all | solution.py:404
  93.1 0.1 copy.24
  93.2 21.2 %all_to_all.69 = bf16[8,16,32,128]{3,2,1,0:T(8,128)(2,1)S(1)} all-to-all(bf16[8,16,32,128]{3,2,1,0:T(8,128)(2,1)S(1)} %copy.24), channel_id=1, replica_groups=mesh['xh'=2,'z'=8,'c'=2,'xl'=2,'y'=4] {'z'}, dimensions={0} | all-to-all | bytes 2097152 | tf_op jit(solution)/shard_map/cond/branch_0_fun/all_to_all | solution.py:405
  114.4 0.1 copy.44
  114.5 0.0 copy-done.3
  114.5 0.0 copy-done.4
  114.5 0.0 copy-done.6
  114.5 0.0 copy-done.8
  114.6 3.5 %finish_project.1 = (bf16[32,128,128]{2,1,0:T(8,128)(2,1)S(1)}, bf16[128,2,32,128]{3,2,1,0:T(8,128)(2,1)S(1)}) custom-call(s32[8,128]{1,0:T(8,128)S(1)} %bitcast.35, f32[2,128]{1,0:T(2,128)S(1)} %copy-done.7, f32[2,128]{1,0:T(2,128)S(1)} %copy-done.8, bf16[16,8,32,128]{3,2,1,0:T(8,128)(2,1)S(1)} %get-tuple-element.51.hidden_ref, ...), custom_call_target="tpu_custom_call" | custom-call | tf_op jit(solution)/shard_map/finish_project/pallas_call | solution.py:295
  118.1 0.0 copy-start.1
  118.1 1.0 copy-done.1
  119.0 52.6 %conditional.6 = (bf16[16,8,64,128]{3,2,0,1:T(8,128)(2,1)S(1)}) conditional(s32[]{:T(128)} %convert_element_type.9, bf16[8,16,64,128]{3,2,1,0:T(8,128)(2,1)S(1)} %bitcast.41, bf16[8,16,64,128]{3,2,1,0:T(8,128)(2,1)S(1)} %bitcast.42), branch_computations={%region_4.0_spmd, %region_5.0_spmd} | conditional | bytes 16777224 | solution.py:409
  119.0 31.4 %all_to_all.74 = bf16[8,16,64,128]{3,2,1,0:T(8,128)(2,1)S(1)} all-to-all(bf16[8,16,64,128]{3,2,1,0:T(8,128)(2,1)S(1)} %param.5), channel_id=1, replica_groups=mesh['xh'=2,'z'=8,'c'=2,'xl'=2,'y'=4] {'z'}, dimensions={0} | all-to-all | bytes 4194304 | tf_op jit(solution)/shard_map/cond/branch_1_fun/all_to_all | solution.py:398
  150.5 0.2 copy.28
  150.7 20.6 %all_to_all.75 = bf16[16,8,64,128]{3,2,1,0:T(8,128)(2,1)S(1)} all-to-all(bf16[16,8,64,128]{3,2,1,0:T(8,128)(2,1)S(1)} %copy.28), channel_id=1, replica_groups=mesh['xh'=2,'z'=8,'c'=2,'xl'=2,'y'=4] {'xh','xl','y'}, dimensions={0} | all-to-all | bytes 4194304 | tf_op jit(solution)/shard_map/cond/branch_1_fun/all_to_all | solution.py:399
  171.3 0.2 copy.29
  171.6 0.2 copy.39
  171.9 0.0 copy-start.2
  171.9 1.1 incoming_send.1
  173.0 5.4 %collective-permute-start.1 = (bf16[512,1024]{1,0:T(8,128)(2,1)S(1)}, bf16[512,1024]{1,0:T(8,128)(2,1)S(1)}, u32[]{:S(2)}, u32[]{:S(2)}) collective-permute-start(bf16[512,1024]{1,0:T(8,128)(2,1)S(1)} %get-tuple-element.46), channel_id=1, source_target_pairs={{0,8},{8,0},{1,9},{9,1},{2,10},{10,2},{3,11},{11,3},{4,12},{12,4},... | collective-permute-start | bytes 3145736 | tf_op jit(solution)/shard_map/ppermute | solution.py:422
  178.4 0.0 copy-done.2
  178.4 1.0 output_gate.3.gate_ref
  179.4 1.2 collective-permute-done.1.other_ref
  180.7 0.7 incoming.1
  181.4 35.5 %conditional.7 = (bf16[16,8,32,128]{3,2,1,0:T(8,128)(2,1)S(1)}) conditional(s32[]{:T(128)} %convert_element_type.8, bf16[8,16,32,128]{3,2,1,0:T(8,128)(2,1)S(1)} %bitcast.37, bf16[8,16,32,128]{3,2,1,0:T(8,128)(2,1)S(1)} %bitcast.38), branch_computations={%region_6.0_spmd, %region_7.0_spmd} | conditional | bytes 10485768 | solution.py:409
  181.4 0.1 copy.55
  181.5 14.7 %all_to_all.76 = bf16[16,8,32,128]{3,2,1,0:T(8,128)(2,1)S(1)} all-to-all(bf16[16,8,32,128]{3,2,1,0:T(8,128)(2,1)S(1)} %bitcast.59), channel_id=1, replica_groups=mesh['xh'=2,'z'=8,'c'=2,'xl'=2,'y'=4] {'xh','xl','y'}, dimensions={0} | all-to-all | bytes 2097152 | tf_op jit(solution)/shard_map/cond/branch_0_fun/all_to_all | solution.py:404
  196.2 0.1 copy.30
  196.3 20.5 %all_to_all.77 = bf16[8,16,32,128]{3,2,1,0:T(8,128)(2,1)S(1)} all-to-all(bf16[8,16,32,128]{3,2,1,0:T(8,128)(2,1)S(1)} %copy.30), channel_id=1, replica_groups=mesh['xh'=2,'z'=8,'c'=2,'xl'=2,'y'=4] {'z'}, dimensions={0} | all-to-all | bytes 2097152 | tf_op jit(solution)/shard_map/cond/branch_0_fun/all_to_all | solution.py:405
  216.8 0.1 copy.46
  216.9 2.4 %finish.1 = bf16[32,128,128]{2,1,0:T(8,128)(2,1)} custom-call(f32[2,128]{1,0:T(2,128)S(1)} %copy-done.8, bf16[16,8,32,128]{3,2,1,0:T(8,128)(2,1)S(1)} %get-tuple-element.52.hidden_ref, bf16[32,128,128]{2,1,0:T(8,128)(2,1)S(1)} %copy-done.2, f32[32,128,128]{2,1,0:T(8,128)S(1)} %output_gate.3.gate_ref, bf16[2,128,128]{2,1,0:T(8,128)(2,1)S(1)} %copy-done.4), custom_call_target="tpu_custom_call" | custom-call | tf_op jit(solution)/shard_map/finish/pallas_call | solution.py:253
Async XLA Ops:
  66.6 6.1 %copy-start.9 = (bf16[2,8,8,2,32,128]{5,4,3,2,1,0:T(8,128)(2,1)}, bf16[2,8,8,2,32,128]{5,4,3,2,1,0:T(8,128)(2,1)S(1)}, u32[]{:S(2)}) copy-start(bf16[2,8,8,2,32,128]{5,4,3,2,1,0:T(8,128)(2,1)S(1)} %get-tuple-element.50.pairs_ref) | copy-start | bytes 6291460
  66.6 6.1 %copy-start = (bf16[32,128,128]{2,1,0:T(8,128)(2,1)S(1)}, bf16[32,128,128]{2,1,0:T(8,128)(2,1)}, u32[]{:S(2)}) copy-start(bf16[32,128,128]{2,1,0:T(8,128)(2,1)} %get-tuple-element.40.cells_ref) | copy-start | bytes 3145732
  66.7 6.1 %copy-start.5 = (bf16[2,128,128]{2,1,0:T(8,128)(2,1)S(1)}, bf16[2,128,128]{2,1,0:T(8,128)(2,1)}, u32[]{:S(2)}) copy-start(bf16[2,128,128]{2,1,0:T(8,128)(2,1)} %weight_ref.6) | copy-start | bytes 196612
  66.7 6.1 %copy-start.7 = (f32[2,128]{1,0:T(2,128)S(1)}, f32[2,128]{1,0:T(2,128)}, u32[]{:S(2)}) copy-start(f32[2,128]{1,0:T(2,128)} %gain_ref.4) | copy-start | bytes 3076
  67.7 7.6 %collective-permute-start = (bf16[16,8,32,128]{3,2,1,0:T(8,128)(2,1)}, bf16[16,8,32,128]{3,2,1,0:T(8,128)(2,1)}, u32[]{:S(2)}, u32[]{:S(2)}) collective-permute-start(bf16[16,8,32,128]{3,2,1,0:T(8,128)(2,1)} %take_right.1), channel_id=1, source_target_pairs={{0,8},{8,0},{1,9},{9,1},{2,10},{10,2},{3,11},{11,3},{4,12},{12,4},... | collective-permute-start | bytes 3145736 | tf_op jit(solution)/shard_map/ppermute | solution.py:422
  72.7 2.6 %copy-start.10 = (bf16[2,8,8,2,32,128]{5,4,3,2,1,0:T(8,128)(2,1)S(1)}, bf16[2,8,8,2,32,128]{5,4,3,2,1,0:T(8,128)(2,1)}, u32[]{:S(2)}) copy-start(bf16[2,8,8,2,32,128]{5,4,3,2,1,0:T(8,128)(2,1)} %copy-done.9) | copy-start | bytes 6291460
  78.2 36.3 %copy-start.3 = (bf16[2,128,512]{2,1,0:T(8,128)(2,1)S(1)}, bf16[2,128,512]{2,1,0:T(8,128)(2,1)}, u32[]{:S(2)}) copy-start(bf16[2,128,512]{2,1,0:T(8,128)(2,1)} %proj_ref.1) | copy-start | bytes 786436
  78.2 36.3 %copy-start.4 = (bf16[2,128,128]{2,1,0:T(8,128)(2,1)S(1)}, bf16[2,128,128]{2,1,0:T(8,128)(2,1)}, u32[]{:S(2)}) copy-start(bf16[2,128,128]{2,1,0:T(8,128)(2,1)} %weight_ref.7) | copy-start | bytes 196612
  78.2 36.3 %copy-start.6 = (s32[1024]{0:T(1024)S(1)}, s32[1024]{0:T(1024)}, u32[]{:S(2)}) copy-start(s32[1024]{0:T(1024)} %param.16) | copy-start | bytes 12292
  78.2 36.3 %copy-start.8 = (f32[2,128]{1,0:T(2,128)S(1)}, f32[2,128]{1,0:T(2,128)}, u32[]{:S(2)}) copy-start(f32[2,128]{1,0:T(2,128)} %gain_ref.5) | copy-start | bytes 3076
  118.1 1.0 copy-start.1
  171.9 6.5 %copy-start.2 = (bf16[32,128,128]{2,1,0:T(8,128)(2,1)S(1)}, bf16[32,128,128]{2,1,0:T(8,128)(2,1)}, u32[]{:S(2)}) copy-start(bf16[32,128,128]{2,1,0:T(8,128)(2,1)} %copy-done.1) | copy-start | bytes 3145732
  173.0 7.7 %collective-permute-start.1 = (bf16[512,1024]{1,0:T(8,128)(2,1)S(1)}, bf16[512,1024]{1,0:T(8,128)(2,1)S(1)}, u32[]{:S(2)}, u32[]{:S(2)}) collective-permute-start(bf16[512,1024]{1,0:T(8,128)(2,1)S(1)} %get-tuple-element.46), channel_id=1, source_target_pairs={{0,8},{8,0},{1,9},{9,1},{2,10},{10,2},{3,11},{11,3},{4,12},{12,4},... | collective-permute-start | bytes 3145736 | tf_op jit(solution)/shard_map/ppermute | solution.py:422

commit v10 on v9

--- a/solution.py
+++ b/solution.py
@@ -213,7 +213,8 @@
         def body(chip, carry):
             for plane in range(DEPTH):
                 chan = plane * CHIPS + chip
-                values = (hidden_ref[chip, plane, rows].astype(F32) - average) * scale
+                place = (plane, chip) if module == 0 else (chip, plane)
+                values = (hidden_ref[place + (rows,)].astype(F32) - average) * scale
                 scratch[pl.ds(chan * ROW_PITCH + first, 16), :] = values * gains[pl.ds(chan, 1), :]
             return carry
 
@@ -418,6 +419,12 @@
     return exchange(product.reshape(DEPTH, CHIPS, ROWS, COLS), first_core)
 
 
+def exchange_at_once(product):
+    flat = product.reshape(CHAN, ROWS, COLS)
+    flat = lax.all_to_all(flat, ("z",) + PLANE, split_axis=0, concat_axis=0, tiled=True)
+    return flat.reshape(DEPTH, CHIPS, ROWS, COLS)
+
+
 def to_other_core(values):
     return lax.ppermute(values, "c", [(0, 1), (1, 0)])
 
@@ -430,7 +437,7 @@
     other = to_other_core(take_right(pairs))
     gate = output_gate(0, in_gain, cells, gate_weight)
     product, gate = lax.optimization_barrier((outgoing(pairs, other), gate))
-    hidden = exchange_product(product, 0)
+    hidden = exchange_at_once(product)
     cells, pairs = finish_project(mask, in_gain, out_gain, hidden, cells, gate, out_weight, proj_weight)
 
     pairs = exchange_pairs(pairs, 1)

time: 220 us -> 220 us (level)
  blocking collectives: 185 us -> 151 us
  waiting for transfers between devices: 2.78 us -> 30.2 us
  starting transfers between devices: 10.4 us -> 17.4 us
    all_to_all x0 -> x1, waiting for transfers between devices: none -> 27.8 us  [exchange_at_once(): lax.all_to_all(flat, ('z',) + PLANE, split_axis=0, concat_axis=0, tiled=T...]
    all_to_all x3 -> x2, blocking collectives: 78.8 us -> 57.6 us  [planes_last(): lax.all_to_all(pairs, 'z', split_axis=0, concat_axis=0, tiled=True)]
    all_to_all x3 -> x2, blocking collectives: 54.4 us -> 39.6 us  [planes_last(): lax.all_to_all(pairs, PLANE, split_axis=0, concat_axis=0, tiled=True)]
    all_to_all x0 -> x1, starting transfers between devices: none -> 7.98 us  [exchange_at_once(): lax.all_to_all(flat, ('z',) + PLANE, split_axis=0, concat_axis=0, tiled=T...]
  transfers between devices with their start and end apart: 2 -> 3, of which waited for: 2 -> 3; matrix products, arithmetic and copies ran while one was open for 0% -> 0% of each run, Pallas kernels for 1% -> 1%
where the time goes in v10:
time: 220 us; the launch traced here: 219 us
  blocking collectives  151 us (69%)
  waiting for transfers between devices  30.2 us (14%)
  starting transfers between devices  17.4 us (8%)
  Pallas kernels  16.4 us (7%)
  local copies, waits for them, and re-layouts  3.77 us (2%)
    all_to_all x2, blocking collectives, planes_last(): lax.all_to_all(pairs, 'z', split_axis=0, concat_axis=0, tiled=True)  57.6 us
    all_to_all x2, blocking collectives, planes_last(): lax.all_to_all(pairs, PLANE, split_axis=0, concat_axis=0, tiled=True)  39.6 us
    all_to_all x1, blocking collectives, planes_first(): lax.all_to_all(pairs, 'z', split_axis=0, concat_axis=0, tiled=True)  32.5 us
    all_to_all x1, waiting for transfers between devices, exchange_at_once(): lax.all_to_all(flat, ('z',) + PLANE, split_axis=0, concat_axis=0, tiled=T...  27.8 us
    all_to_all x1, blocking collectives, planes_first(): return lax.all_to_all(pairs, PLANE, split_axis=0, concat_axis=0, tiled=True)  21.3 us
    ppermute x2, starting transfers between devices, to_other_core(): return lax.ppermute(values, 'c', [(0, 1), (1, 0)])  9.41 us
    all_to_all x1, starting transfers between devices, exchange_at_once(): lax.all_to_all(flat, ('z',) + PLANE, split_axis=0, concat_axis=0, tiled=T...  7.98 us
    pallas_call x1, Pallas kernels, finish_project(): return call(mask, in_gain, out_gain, hidden, cells, gate, weight, proj)  4.72 us
  transfers between devices with their start and end apart: 3, of which 3 were waited for; matrix products, arithmetic and copies ran while one was open for 0% of the time, Pallas kernels for 1%

profile of v10, /device:TPU:1, one launch (start us, length us, event | category | flops | bytes accessed | tf_op | source)
XLA Modules:
  0.0 219.3 jit_solution(12052005803780183541)
XLA Ops:
  0.0 3.7 %project.1 = (bf16[128,2,32,128]{3,2,1,0:T(8,128)(2,1)S(1)}, bf16[32,128,128]{2,1,0:T(8,128)(2,1)}) custom-call(s32[8,128]{1,0:T(8,128)} %bitcast.30, f32[2,128]{1,0:T(2,128)} %gain_ref.4, bf16[32,128,128]{2,1,0:T(8,128)(2,1)} %cells_hbm.1, bf16[2,128,512]{2,1,0:T(8,128)(2,1)} %proj_ref.1), custom_call_target="tpu_custom_call" | custom-call | tf_op jit(solution)/shard_map/project/pallas_call | solution.py:160
  3.7 63.0 %conditional.3 = (bf16[2,8,8,2,32,128]{5,4,3,2,1,0:T(8,128)(2,1)S(1)}) conditional(s32[]{:T(128)} %convert_element_type.7, bf16[8,16,64,128]{3,2,1,0:T(8,128)(2,1)S(1)} %bitcast.37, bf16[8,16,64,128]{3,2,1,0:T(8,128)(2,1)S(1)} %bitcast.38), branch_computations={%region_0.0_spmd, %region_1.0_spmd} | conditional | bytes 20971528 | solution.py:410
  3.7 0.2 copy.41
  3.9 24.9 %all_to_all.53 = bf16[16,8,64,128]{3,2,1,0:T(8,128)(2,1)S(1)} all-to-all(bf16[16,8,64,128]{3,2,1,0:T(8,128)(2,1)S(1)} %bitcast.43), channel_id=1, replica_groups=mesh['xh'=2,'z'=8,'c'=2,'xl'=2,'y'=4] {'xh','xl','y'}, dimensions={0} | all-to-all | bytes 4194304 | tf_op jit(solution)/shard_map/cond/branch_0_fun/all_to_all | solution.py:405
  28.8 0.2 copy.18
  29.0 37.2 %all_to_all.54 = bf16[8,16,64,128]{3,2,1,0:T(8,128)(2,1)S(1)} all-to-all(bf16[8,16,64,128]{3,2,1,0:T(8,128)(2,1)S(1)} %copy.18), channel_id=1, replica_groups=mesh['xh'=2,'z'=8,'c'=2,'xl'=2,'y'=4] {'z'}, dimensions={0} | all-to-all | bytes 4194304 | tf_op jit(solution)/shard_map/cond/branch_0_fun/all_to_all | solution.py:406
  66.2 0.4 copy.34
  66.6 0.0 copy-start.10
  66.6 0.0 copy-start
  66.7 0.0 copy-start.6
  66.7 0.0 copy-start.8
  66.7 0.1 take_right.1
  66.8 5.1 %collective-permute-start = (bf16[16,8,32,128]{3,2,1,0:T(8,128)(2,1)S(1)}, bf16[16,8,32,128]{3,2,1,0:T(8,128)(2,1)S(1)}, u32[]{:S(2)}, u32[]{:S(2)}) collective-permute-start(bf16[16,8,32,128]{3,2,1,0:T(8,128)(2,1)S(1)} %take_right.1), channel_id=1, source_target_pairs={{0,8},{8,0},{1,9},{9,1},{2,10},{10,2},{3,11},{11,3},{4,12},{12,4},... | collective-permute-start | bytes 3145736 | tf_op jit(solution)/shard_map/ppermute | solution.py:429
  71.8 0.0 copy-done.10
  71.8 0.0 copy-done
  71.8 0.0 copy-done.6
  71.8 0.0 copy-done.8
  71.8 0.0 copy-start.11
  71.8 1.1 output_gate.2.gate_ref
  72.9 1.2 collective-permute-done.other_ref
  74.1 0.0 copy-done.11
  74.1 1.6 outgoing.1
  75.7 0.0 copy-start.3
  75.7 1.0 copy-done.3
  76.7 0.0 copy-start.4
  76.7 0.0 copy-start.5
  76.7 0.0 copy-start.7
  76.7 0.0 copy-start.9
  76.7 8.0 %all-to-all-start.12 = ((bf16[128,32,128]{2,1,0:T(8,128)(2,1)}), bf16[128,32,128]{2,1,0:T(8,128)(2,1)}, u32[]{:S(2)}, u32[]{:S(2)}) async-start(bf16[128,32,128]{2,1,0:T(8,128)(2,1)} %bitcast.29), calls=%async_computation.12 | async-start | bytes 2097152 | tf_op jit(solution)/shard_map/all_to_all | solution.py:424
  84.7 27.8 %all-to-all-done.12 = bf16[128,32,128]{2,1,0:T(8,128)(2,1)} async-done(((bf16[128,32,128]{2,1,0:T(8,128)(2,1)}), bf16[128,32,128]{2,1,0:T(8,128)(2,1)}, u32[]{:S(2)}, u32[]{:S(2)}) %all-to-all-start.12) | async-done | bytes 1048608 | tf_op jit(solution)/shard_map/all_to_all | solution.py:424
  112.5 0.0 copy-done.4
  112.5 0.0 copy-done.5
  112.5 0.0 copy-done.7
  112.5 0.0 copy-done.9
  112.5 4.7 %finish_project.1 = (bf16[32,128,128]{2,1,0:T(8,128)(2,1)S(1)}, bf16[128,2,32,128]{3,2,1,0:T(8,128)(2,1)S(1)}) custom-call(s32[8,128]{1,0:T(8,128)S(1)} %bitcast.31, f32[2,128]{1,0:T(2,128)S(1)} %copy-done.8, f32[2,128]{1,0:T(2,128)S(1)} %copy-done.9, bf16[8,16,32,128]{3,2,1,0:T(8,128)(2,1)} %bitcast.18.hidden_ref, bf16[32,128,128]{2,1,0:T(8,128)(2,1)S(1)} %copy-done, ...), custom_call_target="tpu_custom_call" | custom-call | tf_op jit(solution)/shard_map/finish_project/pallas_call | solution.py:296
  117.2 0.0 copy-start.1
  117.2 1.0 copy-done.1
  118.2 54.2 %conditional.4 = (bf16[16,8,64,128]{3,2,0,1:T(8,128)(2,1)S(1)}) conditional(s32[]{:T(128)} %convert_element_type.8, bf16[8,16,64,128]{3,2,1,0:T(8,128)(2,1)S(1)} %bitcast.35, bf16[8,16,64,128]{3,2,1,0:T(8,128)(2,1)S(1)} %bitcast.36), branch_computations={%region_2.0_spmd, %region_3.0_spmd} | conditional | bytes 16777224 | solution.py:410
  118.2 32.5 %all_to_all.59 = bf16[8,16,64,128]{3,2,1,0:T(8,128)(2,1)S(1)} all-to-all(bf16[8,16,64,128]{3,2,1,0:T(8,128)(2,1)S(1)} %param.3), channel_id=1, replica_groups=mesh['xh'=2,'z'=8,'c'=2,'xl'=2,'y'=4] {'z'}, dimensions={0} | all-to-all | bytes 4194304 | tf_op jit(solution)/shard_map/cond/branch_1_fun/all_to_all | solution.py:399
  150.7 0.2 copy.22
  150.9 21.3 %all_to_all.60 = bf16[16,8,64,128]{3,2,1,0:T(8,128)(2,1)S(1)} all-to-all(bf16[16,8,64,128]{3,2,1,0:T(8,128)(2,1)S(1)} %copy.22), channel_id=1, replica_groups=mesh['xh'=2,'z'=8,'c'=2,'xl'=2,'y'=4] {'xh','xl','y'}, dimensions={0} | all-to-all | bytes 4194304 | tf_op jit(solution)/shard_map/cond/branch_1_fun/all_to_all | solution.py:400
  172.2 0.2 copy.23
  172.4 0.2 copy.31
  172.7 0.0 copy-start.2
  172.7 1.1 incoming_send.1
  173.8 4.4 %collective-permute-start.1 = (bf16[512,1024]{1,0:T(8,128)(2,1)S(1)}, bf16[512,1024]{1,0:T(8,128)(2,1)S(1)}, u32[]{:S(2)}, u32[]{:S(2)}) collective-permute-start(bf16[512,1024]{1,0:T(8,128)(2,1)S(1)} %get-tuple-element.41), channel_id=1, source_target_pairs={{0,8},{8,0},{1,9},{9,1},{2,10},{10,2},{3,11},{11,3},{4,12},{12,4},... | collective-permute-start | bytes 3145736 | tf_op jit(solution)/shard_map/ppermute | solution.py:429
  178.1 0.0 copy-done.2
  178.1 1.1 output_gate.3.gate_ref
  179.2 1.2 collective-permute-done.1.other_ref
  180.4 0.7 incoming.1
  181.1 35.5 %conditional.5 = (bf16[16,8,32,128]{3,2,1,0:T(8,128)(2,1)S(1)}) conditional(s32[]{:T(128)} %convert_element_type.7, bf16[8,16,32,128]{3,2,1,0:T(8,128)(2,1)S(1)} %bitcast.33, bf16[8,16,32,128]{3,2,1,0:T(8,128)(2,1)S(1)} %bitcast.34), branch_computations={%region_4.0_spmd, %region_5.0_spmd} | conditional | bytes 10485768 | solution.py:410
  181.1 0.1 copy.43
  181.3 14.7 %all_to_all.61 = bf16[16,8,32,128]{3,2,1,0:T(8,128)(2,1)S(1)} all-to-all(bf16[16,8,32,128]{3,2,1,0:T(8,128)(2,1)S(1)} %bitcast.49), channel_id=1, replica_groups=mesh['xh'=2,'z'=8,'c'=2,'xl'=2,'y'=4] {'xh','xl','y'}, dimensions={0} | all-to-all | bytes 2097152 | tf_op jit(solution)/shard_map/cond/branch_0_fun/all_to_all | solution.py:405
  196.0 0.1 copy.24
  196.1 20.5 %all_to_all.62 = bf16[8,16,32,128]{3,2,1,0:T(8,128)(2,1)S(1)} all-to-all(bf16[8,16,32,128]{3,2,1,0:T(8,128)(2,1)S(1)} %copy.24), channel_id=1, replica_groups=mesh['xh'=2,'z'=8,'c'=2,'xl'=2,'y'=4] {'z'}, dimensions={0} | all-to-all | bytes 2097152 | tf_op jit(solution)/shard_map/cond/branch_0_fun/all_to_all | solution.py:406
  216.5 0.1 copy.36
  216.7 2.4 %finish.1 = bf16[32,128,128]{2,1,0:T(8,128)(2,1)} custom-call(f32[2,128]{1,0:T(2,128)S(1)} %copy-done.9, bf16[16,8,32,128]{3,2,1,0:T(8,128)(2,1)S(1)} %get-tuple-element.46.hidden_ref, bf16[32,128,128]{2,1,0:T(8,128)(2,1)S(1)} %copy-done.2, f32[32,128,128]{2,1,0:T(8,128)S(1)} %output_gate.3.gate_ref, bf16[2,128,128]{2,1,0:T(8,128)(2,1)S(1)} %copy-done.5), custom_call_target="tpu_custom_call" | custom-call | tf_op jit(solution)/shard_map/finish/pallas_call | solution.py:254
Async XLA Ops:
  66.6 5.2 %copy-start.10 = (bf16[2,8,8,2,32,128]{5,4,3,2,1,0:T(8,128)(2,1)}, bf16[2,8,8,2,32,128]{5,4,3,2,1,0:T(8,128)(2,1)S(1)}, u32[]{:S(2)}) copy-start(bf16[2,8,8,2,32,128]{5,4,3,2,1,0:T(8,128)(2,1)S(1)} %get-tuple-element.45.pairs_ref) | copy-start | bytes 6291460
  66.6 5.2 %copy-start = (bf16[32,128,128]{2,1,0:T(8,128)(2,1)S(1)}, bf16[32,128,128]{2,1,0:T(8,128)(2,1)}, u32[]{:S(2)}) copy-start(bf16[32,128,128]{2,1,0:T(8,128)(2,1)} %get-tuple-element.35.cells_ref) | copy-start | bytes 3145732
  66.7 5.2 %copy-start.6 = (bf16[2,128,128]{2,1,0:T(8,128)(2,1)S(1)}, bf16[2,128,128]{2,1,0:T(8,128)(2,1)}, u32[]{:S(2)}) copy-start(bf16[2,128,128]{2,1,0:T(8,128)(2,1)} %weight_ref.6) | copy-start | bytes 196612
  66.7 5.2 %copy-start.8 = (f32[2,128]{1,0:T(2,128)S(1)}, f32[2,128]{1,0:T(2,128)}, u32[]{:S(2)}) copy-start(f32[2,128]{1,0:T(2,128)} %gain_ref.4) | copy-start | bytes 3076
  66.8 7.3 %collective-permute-start = (bf16[16,8,32,128]{3,2,1,0:T(8,128)(2,1)S(1)}, bf16[16,8,32,128]{3,2,1,0:T(8,128)(2,1)S(1)}, u32[]{:S(2)}, u32[]{:S(2)}) collective-permute-start(bf16[16,8,32,128]{3,2,1,0:T(8,128)(2,1)S(1)} %take_right.1), channel_id=1, source_target_pairs={{0,8},{8,0},{1,9},{9,1},{2,10},{10,2},{3,11},{11,3},{4,12},{12,4},... | collective-permute-start | bytes 3145736 | tf_op jit(solution)/shard_map/ppermute | solution.py:429
  71.8 2.3 %copy-start.11 = (bf16[2,8,8,2,32,128]{5,4,3,2,1,0:T(8,128)(2,1)S(1)}, bf16[2,8,8,2,32,128]{5,4,3,2,1,0:T(8,128)(2,1)}, u32[]{:S(2)}) copy-start(bf16[2,8,8,2,32,128]{5,4,3,2,1,0:T(8,128)(2,1)} %copy-done.10) | copy-start | bytes 6291460
  75.7 1.0 copy-start.3
  76.7 35.8 %copy-start.4 = (bf16[2,128,512]{2,1,0:T(8,128)(2,1)S(1)}, bf16[2,128,512]{2,1,0:T(8,128)(2,1)}, u32[]{:S(2)}) copy-start(bf16[2,128,512]{2,1,0:T(8,128)(2,1)} %proj_ref.1) | copy-start | bytes 786436
  76.7 35.8 %copy-start.5 = (bf16[2,128,128]{2,1,0:T(8,128)(2,1)S(1)}, bf16[2,128,128]{2,1,0:T(8,128)(2,1)}, u32[]{:S(2)}) copy-start(bf16[2,128,128]{2,1,0:T(8,128)(2,1)} %weight_ref.7) | copy-start | bytes 196612
  76.7 35.8 %copy-start.7 = (s32[1024]{0:T(1024)S(1)}, s32[1024]{0:T(1024)}, u32[]{:S(2)}) copy-start(s32[1024]{0:T(1024)} %param.14) | copy-start | bytes 12292
  76.7 35.8 %copy-start.9 = (f32[2,128]{1,0:T(2,128)S(1)}, f32[2,128]{1,0:T(2,128)}, u32[]{:S(2)}) copy-start(f32[2,128]{1,0:T(2,128)} %gain_ref.5) | copy-start | bytes 3076
  76.7 35.8 %all-to-all-start.12 = ((bf16[128,32,128]{2,1,0:T(8,128)(2,1)}), bf16[128,32,128]{2,1,0:T(8,128)(2,1)}, u32[]{:S(2)}, u32[]{:S(2)}) async-start(bf16[128,32,128]{2,1,0:T(8,128)(2,1)} %bitcast.29), calls=%async_computation.12 | async-start | bytes 2097152 | tf_op jit(solution)/shard_map/all_to_all | solution.py:424
  117.2 1.0 copy-start.1
  172.7 5.5 %copy-start.2 = (bf16[32,128,128]{2,1,0:T(8,128)(2,1)S(1)}, bf16[32,128,128]{2,1,0:T(8,128)(2,1)}, u32[]{:S(2)}) copy-start(bf16[32,128,128]{2,1,0:T(8,128)(2,1)} %copy-done.1) | copy-start | bytes 3145732
  173.8 6.6 %collective-permute-start.1 = (bf16[512,1024]{1,0:T(8,128)(2,1)S(1)}, bf16[512,1024]{1,0:T(8,128)(2,1)S(1)}, u32[]{:S(2)}, u32[]{:S(2)}) collective-permute-start(bf16[512,1024]{1,0:T(8,128)(2,1)S(1)} %get-tuple-element.41), channel_id=1, source_target_pairs={{0,8},{8,0},{1,9},{9,1},{2,10},{10,2},{3,11},{11,3},{4,12},{12,4},... | collective-permute-start | bytes 3145736 | tf_op jit(solution)/shard_map/ppermute | solution.py:429

commit v11 on v10

--- a/solution.py
+++ b/solution.py
@@ -436,7 +436,7 @@
     pairs = exchange_pairs(pairs, 0)
     other = to_other_core(take_right(pairs))
     gate = output_gate(0, in_gain, cells, gate_weight)
-    product, gate = lax.optimization_barrier((outgoing(pairs, other), gate))
+    product = outgoing(pairs, other)
     hidden = exchange_at_once(product)
     cells, pairs = finish_project(mask, in_gain, out_gain, hidden, cells, gate, out_weight, proj_weight)
 
@@ -444,7 +444,7 @@
     send, left, right = incoming_send(pairs)
     other = to_other_core(send)
     gate = output_gate(1, in_gain, cells, gate_weight)
-    product, gate = lax.optimization_barrier((incoming(left, right, other), gate))
+    product = incoming(left, right, other)
     hidden = exchange_product(product, 0)
     return finish(out_gain, hidden, cells, gate, out_weight)
 

time: 220 us -> 220 us (level)
  no operation moved by 1% of the time
where the time goes in v11:
time: 220 us; the launch traced here: 219 us
  blocking collectives  150 us (68%)
  waiting for transfers between devices  31.1 us (14%)
  Pallas kernels  17.4 us (8%)
  starting transfers between devices  17.3 us (8%)
  local copies, waits for them, and re-layouts  2.8 us (1%)
    all_to_all x2, blocking collectives, planes_last(): lax.all_to_all(pairs, 'z', split_axis=0, concat_axis=0, tiled=True)  57.6 us
    all_to_all x2, blocking collectives, planes_last(): lax.all_to_all(pairs, PLANE, split_axis=0, concat_axis=0, tiled=True)  39.6 us
    all_to_all x1, blocking collectives, planes_first(): lax.all_to_all(pairs, 'z', split_axis=0, concat_axis=0, tiled=True)  32.4 us
    all_to_all x1, waiting for transfers between devices, exchange_at_once(): lax.all_to_all(flat, ('z',) + PLANE, split_axis=0, concat_axis=0, tiled=T...  27.6 us
    all_to_all x1, blocking collectives, planes_first(): return lax.all_to_all(pairs, PLANE, split_axis=0, concat_axis=0, tiled=True)  20.7 us
    ppermute x2, starting transfers between devices, to_other_core(): return lax.ppermute(values, 'c', [(0, 1), (1, 0)])  9.29 us
    all_to_all x1, starting transfers between devices, exchange_at_once(): lax.all_to_all(flat, ('z',) + PLANE, split_axis=0, concat_axis=0, tiled=T...  7.97 us
    pallas_call x1, Pallas kernels, finish_project(): return call(mask, in_gain, out_gain, hidden, cells, gate, weight, proj)  4.72 us
  transfers between devices with their start and end apart: 3, of which 3 were waited for; matrix products, arithmetic and copies ran while one was open for 0% of the time, Pallas kernels for 1%

profile of v11, /device:TPU:1, one launch (start us, length us, event | category | flops | bytes accessed | tf_op | source)
XLA Modules:
  0.0 219.3 jit_solution(13132170450180614544)
XLA Ops:
  0.0 3.7 %project.1 = (bf16[128,2,32,128]{3,2,1,0:T(8,128)(2,1)S(1)}, bf16[32,128,128]{2,1,0:T(8,128)(2,1)}) custom-call(s32[8,128]{1,0:T(8,128)} %bitcast.30, f32[2,128]{1,0:T(2,128)} %gain_ref.4, bf16[32,128,128]{2,1,0:T(8,128)(2,1)} %cells_hbm.1, bf16[2,128,512]{2,1,0:T(8,128)(2,1)} %proj_ref.1), custom_call_target="tpu_custom_call" | custom-call | tf_op jit(solution)/shard_map/project/pallas_call | solution.py:160
  3.7 63.0 %conditional.3 = (bf16[2,8,8,2,32,128]{5,4,3,2,1,0:T(8,128)(2,1)S(1)}) conditional(s32[]{:T(128)} %convert_element_type.7, bf16[8,16,64,128]{3,2,1,0:T(8,128)(2,1)S(1)} %bitcast.37, bf16[8,16,64,128]{3,2,1,0:T(8,128)(2,1)S(1)} %bitcast.38), branch_computations={%region_0.0_spmd, %region_1.0_spmd} | conditional | bytes 20971528 | solution.py:410
  3.7 0.2 copy.41
  3.9 24.9 %all_to_all.53 = bf16[16,8,64,128]{3,2,1,0:T(8,128)(2,1)S(1)} all-to-all(bf16[16,8,64,128]{3,2,1,0:T(8,128)(2,1)S(1)} %bitcast.43), channel_id=1, replica_groups=mesh['xh'=2,'z'=8,'c'=2,'xl'=2,'y'=4] {'xh','xl','y'}, dimensions={0} | all-to-all | bytes 4194304 | tf_op jit(solution)/shard_map/cond/branch_0_fun/all_to_all | solution.py:405
  28.8 0.2 copy.18
  29.0 37.2 %all_to_all.54 = bf16[8,16,64,128]{3,2,1,0:T(8,128)(2,1)S(1)} all-to-all(bf16[8,16,64,128]{3,2,1,0:T(8,128)(2,1)S(1)} %copy.18), channel_id=1, replica_groups=mesh['xh'=2,'z'=8,'c'=2,'xl'=2,'y'=4] {'z'}, dimensions={0} | all-to-all | bytes 4194304 | tf_op jit(solution)/shard_map/cond/branch_0_fun/all_to_all | solution.py:406
  66.2 0.4 copy.34
  66.6 0.1 take_right.1
  66.7 5.1 %collective-permute-start = (bf16[16,8,32,128]{3,2,1,0:T(8,128)(2,1)S(1)}, bf16[16,8,32,128]{3,2,1,0:T(8,128)(2,1)S(1)}, u32[]{:S(2)}, u32[]{:S(2)}) collective-permute-start(bf16[16,8,32,128]{3,2,1,0:T(8,128)(2,1)S(1)} %take_right.1), channel_id=1, source_target_pairs={{0,8},{8,0},{1,9},{9,1},{2,10},{10,2},{3,11},{11,3},{4,12},{12,4},... | collective-permute-start | bytes 3145736 | tf_op jit(solution)/shard_map/ppermute | solution.py:429
  71.8 2.3 %collective-permute-done.other_ref = bf16[16,8,32,128]{3,2,1,0:T(8,128)(2,1)S(1)} collective-permute-done((bf16[16,8,32,128]{3,2,1,0:T(8,128)(2,1)S(1)}, bf16[16,8,32,128]{3,2,1,0:T(8,128)(2,1)S(1)}, u32[]{:S(2)}, u32[]{:S(2)}) %collective-permute-start) | collective-permute-done | bytes 1048608 | tf_op jit(solution)/shard_map/ppermute | solution.py:429
  74.1 2.6 %outgoing.1 = bf16[8,2,8,32,128]{4,3,2,1,0:T(8,128)(2,1)} custom-call(bf16[2,8,8,2,32,128]{5,4,3,2,1,0:T(8,128)(2,1)S(1)} %get-tuple-element.37.pairs_ref, bf16[16,8,32,128]{3,2,1,0:T(8,128)(2,1)S(1)} %collective-permute-done.other_ref), custom_call_target="tpu_custom_call" | custom-call | tf_op jit(solution)/shard_map/outgoing/pallas_call | solution.py:355
  76.7 0.0 copy-start
  76.7 0.0 copy-start.5
  76.7 0.0 copy-start.7
  76.7 8.0 %all-to-all-start.12 = ((bf16[128,32,128]{2,1,0:T(8,128)(2,1)}), bf16[128,32,128]{2,1,0:T(8,128)(2,1)}, u32[]{:S(2)}, u32[]{:S(2)}) async-start(bf16[128,32,128]{2,1,0:T(8,128)(2,1)} %bitcast.19), calls=%async_computation.12 | async-start | bytes 2097152 | tf_op jit(solution)/shard_map/all_to_all | solution.py:424
  84.7 0.0 copy-start.3
  84.7 0.0 copy-start.4
  84.7 0.0 copy-start.6
  84.7 0.0 copy-start.8
  84.7 0.0 copy-done
  84.8 0.0 copy-done.5
  84.8 0.0 copy-done.7
  84.8 1.1 output_gate.2.gate_ref
  85.8 27.6 %all-to-all-done.12 = bf16[128,32,128]{2,1,0:T(8,128)(2,1)} async-done(((bf16[128,32,128]{2,1,0:T(8,128)(2,1)}), bf16[128,32,128]{2,1,0:T(8,128)(2,1)}, u32[]{:S(2)}, u32[]{:S(2)}) %all-to-all-start.12) | async-done | bytes 1048608 | tf_op jit(solution)/shard_map/all_to_all | solution.py:424
  113.4 0.0 copy-done.3
  113.4 0.0 copy-done.4
  113.4 0.0 copy-done.6
  113.4 0.0 copy-done.8
  113.4 4.7 %finish_project.1 = (bf16[32,128,128]{2,1,0:T(8,128)(2,1)S(1)}, bf16[128,2,32,128]{3,2,1,0:T(8,128)(2,1)S(1)}) custom-call(s32[8,128]{1,0:T(8,128)S(1)} %bitcast.31, f32[2,128]{1,0:T(2,128)S(1)} %copy-done.7, f32[2,128]{1,0:T(2,128)S(1)} %copy-done.8, bf16[8,16,32,128]{3,2,1,0:T(8,128)(2,1)} %bitcast.20.hidden_ref, bf16[32,128,128]{2,1,0:T(8,128)(2,1)S(1)} %copy-done, ...), custom_call_target="tpu_custom_call" | custom-call | tf_op jit(solution)/shard_map/finish_project/pallas_call | solution.py:296
  118.1 0.0 copy-start.1
  118.1 1.0 copy-done.1
  119.1 53.5 %conditional.4 = (bf16[16,8,64,128]{3,2,0,1:T(8,128)(2,1)S(1)}) conditional(s32[]{:T(128)} %convert_element_type.8, bf16[8,16,64,128]{3,2,1,0:T(8,128)(2,1)S(1)} %bitcast.35, bf16[8,16,64,128]{3,2,1,0:T(8,128)(2,1)S(1)} %bitcast.36), branch_computations={%region_2.0_spmd, %region_3.0_spmd} | conditional | bytes 16777224 | solution.py:410
  119.1 32.4 %all_to_all.59 = bf16[8,16,64,128]{3,2,1,0:T(8,128)(2,1)S(1)} all-to-all(bf16[8,16,64,128]{3,2,1,0:T(8,128)(2,1)S(1)} %param.3), channel_id=1, replica_groups=mesh['xh'=2,'z'=8,'c'=2,'xl'=2,'y'=4] {'z'}, dimensions={0} | all-to-all | bytes 4194304 | tf_op jit(solution)/shard_map/cond/branch_1_fun/all_to_all | solution.py:399
  151.5 0.2 copy.22
  151.8 20.7 %all_to_all.60 = bf16[16,8,64,128]{3,2,1,0:T(8,128)(2,1)S(1)} all-to-all(bf16[16,8,64,128]{3,2,1,0:T(8,128)(2,1)S(1)} %copy.22), channel_id=1, replica_groups=mesh['xh'=2,'z'=8,'c'=2,'xl'=2,'y'=4] {'xh','xl','y'}, dimensions={0} | all-to-all | bytes 4194304 | tf_op jit(solution)/shard_map/cond/branch_1_fun/all_to_all | solution.py:400
  172.5 0.2 copy.23
  172.7 0.2 copy.31
  172.9 0.0 copy-start.2
  172.9 1.1 incoming_send.1
  174.0 4.2 %collective-permute-start.1 = (bf16[512,1024]{1,0:T(8,128)(2,1)S(1)}, bf16[512,1024]{1,0:T(8,128)(2,1)S(1)}, u32[]{:S(2)}, u32[]{:S(2)}) collective-permute-start(bf16[512,1024]{1,0:T(8,128)(2,1)S(1)} %get-tuple-element.35), channel_id=1, source_target_pairs={{0,8},{8,0},{1,9},{9,1},{2,10},{10,2},{3,11},{11,3},{4,12},{12,4},... | collective-permute-start | bytes 3145736 | tf_op jit(solution)/shard_map/ppermute | solution.py:429
  178.2 0.0 copy-done.2
  178.2 1.1 output_gate.3.gate_ref
  179.3 1.2 collective-permute-done.1.other_ref
  180.5 0.7 incoming.1
  181.2 35.5 %conditional.5 = (bf16[16,8,32,128]{3,2,1,0:T(8,128)(2,1)S(1)}) conditional(s32[]{:T(128)} %convert_element_type.7, (bf16[8,2,8,32,128]{4,3,2,1,0:T(8,128)(2,1)S(1)}) %tuple.34, (bf16[8,2,8,32,128]{4,3,2,1,0:T(8,128)(2,1)S(1)}) %tuple.34), branch_computations={%region_4.0_spmd, %region_5.0_spmd} | conditional | bytes 10485768 | solution.py:410
  181.2 0.1 copy.43
  181.3 14.7 %all_to_all.61 = bf16[16,8,32,128]{3,2,1,0:T(8,128)(2,1)S(1)} all-to-all(bf16[16,8,32,128]{3,2,1,0:T(8,128)(2,1)S(1)} %bitcast.49), channel_id=1, replica_groups=mesh['xh'=2,'z'=8,'c'=2,'xl'=2,'y'=4] {'xh','xl','y'}, dimensions={0} | all-to-all | bytes 2097152 | tf_op jit(solution)/shard_map/cond/branch_0_fun/all_to_all | solution.py:405
  196.1 0.1 copy.24
  196.2 20.5 %all_to_all.62 = bf16[8,16,32,128]{3,2,1,0:T(8,128)(2,1)S(1)} all-to-all(bf16[8,16,32,128]{3,2,1,0:T(8,128)(2,1)S(1)} %copy.24), channel_id=1, replica_groups=mesh['xh'=2,'z'=8,'c'=2,'xl'=2,'y'=4] {'z'}, dimensions={0} | all-to-all | bytes 2097152 | tf_op jit(solution)/shard_map/cond/branch_0_fun/all_to_all | solution.py:406
  216.6 0.1 copy.36
  216.7 2.4 %finish.1 = bf16[32,128,128]{2,1,0:T(8,128)(2,1)} custom-call(f32[2,128]{1,0:T(2,128)S(1)} %copy-done.8, bf16[16,8,32,128]{3,2,1,0:T(8,128)(2,1)S(1)} %get-tuple-element.38.hidden_ref, bf16[32,128,128]{2,1,0:T(8,128)(2,1)S(1)} %copy-done.2, f32[32,128,128]{2,1,0:T(8,128)S(1)} %output_gate.3.gate_ref, bf16[2,128,128]{2,1,0:T(8,128)(2,1)S(1)} %copy-done.4), custom_call_target="tpu_custom_call" | custom-call | tf_op jit(solution)/shard_map/finish/pallas_call | solution.py:254
Async XLA Ops:
  66.7 7.4 %collective-permute-start = (bf16[16,8,32,128]{3,2,1,0:T(8,128)(2,1)S(1)}, bf16[16,8,32,128]{3,2,1,0:T(8,128)(2,1)S(1)}, u32[]{:S(2)}, u32[]{:S(2)}) collective-permute-start(bf16[16,8,32,128]{3,2,1,0:T(8,128)(2,1)S(1)} %take_right.1), channel_id=1, source_target_pairs={{0,8},{8,0},{1,9},{9,1},{2,10},{10,2},{3,11},{11,3},{4,12},{12,4},... | collective-permute-start | bytes 3145736 | tf_op jit(solution)/shard_map/ppermute | solution.py:429
  76.7 8.0 %copy-start = (bf16[32,128,128]{2,1,0:T(8,128)(2,1)S(1)}, bf16[32,128,128]{2,1,0:T(8,128)(2,1)}, u32[]{:S(2)}) copy-start(bf16[32,128,128]{2,1,0:T(8,128)(2,1)} %get-tuple-element.31.cells_ref) | copy-start | bytes 3145732
  76.7 8.0 %copy-start.5 = (bf16[2,128,128]{2,1,0:T(8,128)(2,1)S(1)}, bf16[2,128,128]{2,1,0:T(8,128)(2,1)}, u32[]{:S(2)}) copy-start(bf16[2,128,128]{2,1,0:T(8,128)(2,1)} %weight_ref.6) | copy-start | bytes 196612
  76.7 8.1 %copy-start.7 = (f32[2,128]{1,0:T(2,128)S(1)}, f32[2,128]{1,0:T(2,128)}, u32[]{:S(2)}) copy-start(f32[2,128]{1,0:T(2,128)} %gain_ref.4) | copy-start | bytes 3076
  76.7 36.7 %all-to-all-start.12 = ((bf16[128,32,128]{2,1,0:T(8,128)(2,1)}), bf16[128,32,128]{2,1,0:T(8,128)(2,1)}, u32[]{:S(2)}, u32[]{:S(2)}) async-start(bf16[128,32,128]{2,1,0:T(8,128)(2,1)} %bitcast.19), calls=%async_computation.12 | async-start | bytes 2097152 | tf_op jit(solution)/shard_map/all_to_all | solution.py:424
  84.7 28.7 %copy-start.3 = (bf16[2,128,512]{2,1,0:T(8,128)(2,1)S(1)}, bf16[2,128,512]{2,1,0:T(8,128)(2,1)}, u32[]{:S(2)}) copy-start(bf16[2,128,512]{2,1,0:T(8,128)(2,1)} %proj_ref.1) | copy-start | bytes 786436
  84.7 28.7 %copy-start.4 = (bf16[2,128,128]{2,1,0:T(8,128)(2,1)S(1)}, bf16[2,128,128]{2,1,0:T(8,128)(2,1)}, u32[]{:S(2)}) copy-start(bf16[2,128,128]{2,1,0:T(8,128)(2,1)} %weight_ref.7) | copy-start | bytes 196612
  84.7 28.7 %copy-start.6 = (s32[1024]{0:T(1024)S(1)}, s32[1024]{0:T(1024)}, u32[]{:S(2)}) copy-start(s32[1024]{0:T(1024)} %param.14) | copy-start | bytes 12292
  84.7 28.7 %copy-start.8 = (f32[2,128]{1,0:T(2,128)S(1)}, f32[2,128]{1,0:T(2,128)}, u32[]{:S(2)}) copy-start(f32[2,128]{1,0:T(2,128)} %gain_ref.5) | copy-start | bytes 3076
  118.1 1.0 copy-start.1
  172.9 5.3 %copy-start.2 = (bf16[32,128,128]{2,1,0:T(8,128)(2,1)S(1)}, bf16[32,128,128]{2,1,0:T(8,128)(2,1)}, u32[]{:S(2)}) copy-start(bf16[32,128,128]{2,1,0:T(8,128)(2,1)} %copy-done.1) | copy-start | bytes 3145732
  174.0 6.5 %collective-permute-start.1 = (bf16[512,1024]{1,0:T(8,128)(2,1)S(1)}, bf16[512,1024]{1,0:T(8,128)(2,1)S(1)}, u32[]{:S(2)}, u32[]{:S(2)}) collective-permute-start(bf16[512,1024]{1,0:T(8,128)(2,1)S(1)} %get-tuple-element.35), channel_id=1, source_target_pairs={{0,8},{8,0},{1,9},{9,1},{2,10},{10,2},{3,11},{11,3},{4,12},{12,4},... | collective-permute-start | bytes 3145736 | tf_op jit(solution)/shard_map/ppermute | solution.py:429

commit v12 on v11

--- a/solution.py
+++ b/solution.py
@@ -267,7 +267,7 @@
 
 
 def finish_project_kernel(
-    mask_ref, in_gain_ref, out_gain_ref, hidden_ref, cells_ref, gate_ref, weight_ref, proj_ref,
+    mask_ref, in_gain_ref, out_gain_ref, hidden_ref, cells_ref, gate_weight_ref, weight_ref, proj_ref,
     cells_out, pairs_out, gains, scratch, proj_turned, row_masks, left, right,
 ):
     gain_mask = masked_gain(in_gain_ref, 1, mask_ref)
@@ -275,8 +275,15 @@
     normed_hidden_rows(0, out_gain_ref, hidden_ref, gains, scratch)
     weight = jnp.transpose(weight_ref[0])
     proj_turned[...] = jnp.transpose(proj_ref[1])
+    gate_gain = channel_column(in_gain_ref, 0)
+    gate_weight = jnp.transpose(gate_weight_ref[0])
     for first in range(0, ROWS, SUB):
-        rows = updated_rows(first, scratch, weight, cells_ref, gate_ref)
+        normed = [
+            layer_norm(cells_ref[first + index].astype(F32), gate_gain).astype(BF16) for index in range(SUB)
+        ]
+        gates = sigmoid(jnp.dot(gate_weight, jnp.concatenate(normed, axis=1), preferred_element_type=F32))
+        gate = {first + index: gates[:, index * COLS : (index + 1) * COLS] for index in range(SUB)}
+        rows = updated_rows(first, scratch, weight, cells_ref, gate)
         for index, row in enumerate(rows):
             cells_out[first + index] = row
         masks = [row_mask(row_masks, first + index) for index in range(SUB)]
@@ -435,10 +442,9 @@
     pairs, cells = project(mask, in_gain, pair_input, proj_weight)
     pairs = exchange_pairs(pairs, 0)
     other = to_other_core(take_right(pairs))
-    gate = output_gate(0, in_gain, cells, gate_weight)
     product = outgoing(pairs, other)
     hidden = exchange_at_once(product)
-    cells, pairs = finish_project(mask, in_gain, out_gain, hidden, cells, gate, out_weight, proj_weight)
+    cells, pairs = finish_project(mask, in_gain, out_gain, hidden, cells, gate_weight, out_weight, proj_weight)
 
     pairs = exchange_pairs(pairs, 1)
     send, left, right = incoming_send(pairs)

time: 220 us -> 218 us (level)
  transfers between devices with their start and end apart: 3 -> 3, of which waited for: 3 -> 3; matrix products, arithmetic and copies ran while one was open for 0% -> 0% of each run, Pallas kernels for 1% -> 0%
where the time goes in v12:
time: 218 us
  blocking collectives  150 us (69%)
  waiting for transfers between devices  32.6 us (15%)
  starting transfers between devices  16.5 us (8%)
  Pallas kernels  16 us (7%)
    all_to_all x2, blocking collectives, planes_last(): lax.all_to_all(pairs, 'z', split_axis=0, concat_axis=0, tiled=True)  57.6 us
    all_to_all x2, blocking collectives, planes_last(): lax.all_to_all(pairs, PLANE, split_axis=0, concat_axis=0, tiled=True)  39.6 us
    all_to_all x1, blocking collectives, planes_first(): lax.all_to_all(pairs, 'z', split_axis=0, concat_axis=0, tiled=True)  32.4 us
    all_to_all x1, waiting for transfers between devices, exchange_at_once(): lax.all_to_all(flat, ('z',) + PLANE, split_axis=0, concat_axis=0, tiled=T...  29.1 us
    all_to_all x1, blocking collectives, planes_first(): return lax.all_to_all(pairs, PLANE, split_axis=0, concat_axis=0, tiled=True)  20.8 us
    ppermute x2, starting transfers between devices, to_other_core(): return lax.ppermute(values, 'c', [(0, 1), (1, 0)])  9.05 us
    all_to_all x1, starting transfers between devices, exchange_at_once(): lax.all_to_all(flat, ('z',) + PLANE, split_axis=0, concat_axis=0, tiled=T...  7.45 us
  transfers between devices with their start and end apart: 3, of which 3 were waited for; matrix products, arithmetic and copies ran while one was open for 0% of the time, Pallas kernels for 0%

profile of v12, /device:TPU:1, one launch (start us, length us, event | category | flops | bytes accessed | tf_op | source)
XLA Modules:
  0.0 217.9 jit_solution(5760614282648914883)
XLA Ops:
  0.0 3.7 %project.1 = (bf16[128,2,32,128]{3,2,1,0:T(8,128)(2,1)S(1)}, bf16[32,128,128]{2,1,0:T(8,128)(2,1)}) custom-call(s32[8,128]{1,0:T(8,128)} %bitcast.31, f32[2,128]{1,0:T(2,128)} %gain_ref.2, bf16[32,128,128]{2,1,0:T(8,128)(2,1)} %cells_hbm.1, bf16[2,128,512]{2,1,0:T(8,128)(2,1)} %proj_ref.1), custom_call_target="tpu_custom_call" | custom-call | tf_op jit(solution)/shard_map/project/pallas_call | solution.py:160
  3.7 63.0 %conditional.3 = (bf16[2,8,8,2,32,128]{5,4,3,2,1,0:T(8,128)(2,1)S(1)}) conditional(s32[]{:T(128)} %convert_element_type.7, bf16[8,16,64,128]{3,2,1,0:T(8,128)(2,1)S(1)} %bitcast.38, bf16[8,16,64,128]{3,2,1,0:T(8,128)(2,1)S(1)} %bitcast.39), branch_computations={%region_0.0_spmd, %region_1.0_spmd} | conditional | bytes 20971528 | solution.py:417
  3.7 0.2 copy.41
  3.9 24.9 %all_to_all.53 = bf16[16,8,64,128]{3,2,1,0:T(8,128)(2,1)S(1)} all-to-all(bf16[16,8,64,128]{3,2,1,0:T(8,128)(2,1)S(1)} %bitcast.44), channel_id=1, replica_groups=mesh['xh'=2,'z'=8,'c'=2,'xl'=2,'y'=4] {'xh','xl','y'}, dimensions={0} | all-to-all | bytes 4194304 | tf_op jit(solution)/shard_map/cond/branch_0_fun/all_to_all | solution.py:412
  28.8 0.2 copy.18
  29.0 37.2 %all_to_all.54 = bf16[8,16,64,128]{3,2,1,0:T(8,128)(2,1)S(1)} all-to-all(bf16[8,16,64,128]{3,2,1,0:T(8,128)(2,1)S(1)} %copy.18), channel_id=1, replica_groups=mesh['xh'=2,'z'=8,'c'=2,'xl'=2,'y'=4] {'z'}, dimensions={0} | all-to-all | bytes 4194304 | tf_op jit(solution)/shard_map/cond/branch_0_fun/all_to_all | solution.py:413
  66.2 0.4 copy.34
  66.6 0.1 take_right.1
  66.7 5.1 %collective-permute-start = (bf16[16,8,32,128]{3,2,1,0:T(8,128)(2,1)S(1)}, bf16[16,8,32,128]{3,2,1,0:T(8,128)(2,1)S(1)}, u32[]{:S(2)}, u32[]{:S(2)}) collective-permute-start(bf16[16,8,32,128]{3,2,1,0:T(8,128)(2,1)S(1)} %take_right.1), channel_id=1, source_target_pairs={{0,8},{8,0},{1,9},{9,1},{2,10},{10,2},{3,11},{11,3},{4,12},{12,4},... | collective-permute-start | bytes 3145736 | tf_op jit(solution)/shard_map/ppermute | solution.py:436
  71.8 2.3 %collective-permute-done.other_ref = bf16[16,8,32,128]{3,2,1,0:T(8,128)(2,1)S(1)} collective-permute-done((bf16[16,8,32,128]{3,2,1,0:T(8,128)(2,1)S(1)}, bf16[16,8,32,128]{3,2,1,0:T(8,128)(2,1)S(1)}, u32[]{:S(2)}, u32[]{:S(2)}) %collective-permute-start) | collective-permute-done | bytes 1048608 | tf_op jit(solution)/shard_map/ppermute | solution.py:436
  74.1 2.6 %outgoing.1 = bf16[8,2,8,32,128]{4,3,2,1,0:T(8,128)(2,1)} custom-call(bf16[2,8,8,2,32,128]{5,4,3,2,1,0:T(8,128)(2,1)S(1)} %get-tuple-element.37.pairs_ref, bf16[16,8,32,128]{3,2,1,0:T(8,128)(2,1)S(1)} %collective-permute-done.other_ref), custom_call_target="tpu_custom_call" | custom-call | tf_op jit(solution)/shard_map/outgoing/pallas_call | solution.py:362
  76.7 0.0 copy-start
  76.7 0.0 copy-start.1
  76.7 0.0 copy-start.2
  76.7 0.0 copy-start.3
  76.7 0.0 copy-start.4
  76.7 0.0 copy-start.5
  76.7 0.0 copy-start.6
  76.8 7.4 %all-to-all-start.12 = ((bf16[128,32,128]{2,1,0:T(8,128)(2,1)}), bf16[128,32,128]{2,1,0:T(8,128)(2,1)S(1)}, u32[]{:S(2)}, u32[]{:S(2)}) async-start(bf16[128,32,128]{2,1,0:T(8,128)(2,1)} %bitcast.19), calls=%async_computation.12 | async-start | bytes 2097152 | tf_op jit(solution)/shard_map/all_to_all | solution.py:431
  84.2 29.1 %all-to-all-done.12 = bf16[128,32,128]{2,1,0:T(8,128)(2,1)S(1)} async-done(((bf16[128,32,128]{2,1,0:T(8,128)(2,1)}), bf16[128,32,128]{2,1,0:T(8,128)(2,1)S(1)}, u32[]{:S(2)}, u32[]{:S(2)}) %all-to-all-start.12) | async-done | bytes 1048608 | tf_op jit(solution)/shard_map/all_to_all | solution.py:431
  113.3 0.0 copy-done
  113.3 0.0 copy-done.1
  113.3 0.0 copy-done.2
  113.3 0.0 copy-done.3
  113.4 0.0 copy-done.4
  113.4 0.0 copy-done.5
  113.4 0.0 copy-done.6
  113.4 4.3 %finish_project.1 = (bf16[32,128,128]{2,1,0:T(8,128)(2,1)S(1)}, bf16[128,2,32,128]{3,2,1,0:T(8,128)(2,1)S(1)}) custom-call(s32[8,128]{1,0:T(8,128)S(1)} %bitcast.32, f32[2,128]{1,0:T(2,128)S(1)} %copy-done.5, f32[2,128]{1,0:T(2,128)S(1)} %copy-done.6, bf16[8,16,32,128]{3,2,1,0:T(8,128)(2,1)S(1)} %bitcast.30, bf16[32,128,128]{2,1,0:T(8,128)(2,1)S(1)} %copy-done, ...), custom_call_target="tpu_custom_call" | custom-call | tf_op jit(solution)/shard_map/finish_project/pallas_call | solution.py:303
  117.7 53.7 %conditional.4 = (bf16[16,8,64,128]{3,2,0,1:T(8,128)(2,1)S(1)}) conditional(s32[]{:T(128)} %convert_element_type.8, bf16[8,16,64,128]{3,2,1,0:T(8,128)(2,1)S(1)} %bitcast.36, bf16[8,16,64,128]{3,2,1,0:T(8,128)(2,1)S(1)} %bitcast.37), branch_computations={%region_2.0_spmd, %region_3.0_spmd} | conditional | bytes 16777224 | solution.py:417
  117.9 32.4 %all_to_all.59 = bf16[8,16,64,128]{3,2,1,0:T(8,128)(2,1)S(1)} all-to-all(bf16[8,16,64,128]{3,2,1,0:T(8,128)(2,1)S(1)} %param.3), channel_id=1, replica_groups=mesh['xh'=2,'z'=8,'c'=2,'xl'=2,'y'=4] {'z'}, dimensions={0} | all-to-all | bytes 4194304 | tf_op jit(solution)/shard_map/cond/branch_1_fun/all_to_all | solution.py:406
  150.3 0.2 copy.22
  150.5 20.8 %all_to_all.60 = bf16[16,8,64,128]{3,2,1,0:T(8,128)(2,1)S(1)} all-to-all(bf16[16,8,64,128]{3,2,1,0:T(8,128)(2,1)S(1)} %copy.22), channel_id=1, replica_groups=mesh['xh'=2,'z'=8,'c'=2,'xl'=2,'y'=4] {'xh','xl','y'}, dimensions={0} | all-to-all | bytes 4194304 | tf_op jit(solution)/shard_map/cond/branch_1_fun/all_to_all | solution.py:407
  171.3 0.2 copy.23
  171.5 0.2 copy.31
  171.7 1.1 incoming_send.1
  172.8 4.0 %collective-permute-start.1 = (bf16[512,1024]{1,0:T(8,128)(2,1)S(1)}, bf16[512,1024]{1,0:T(8,128)(2,1)S(1)}, u32[]{:S(2)}, u32[]{:S(2)}) collective-permute-start(bf16[512,1024]{1,0:T(8,128)(2,1)S(1)} %get-tuple-element.35), channel_id=1, source_target_pairs={{0,8},{8,0},{1,9},{9,1},{2,10},{10,2},{3,11},{11,3},{4,12},{12,4},... | collective-permute-start | bytes 3145736 | tf_op jit(solution)/shard_map/ppermute | solution.py:436
  176.8 1.1 output_gate.1.gate_ref
  177.8 1.2 collective-permute-done.1.other_ref
  179.1 0.7 incoming.1
  179.8 35.5 %conditional.5 = (bf16[16,8,32,128]{3,2,1,0:T(8,128)(2,1)S(1)}) conditional(s32[]{:T(128)} %convert_element_type.7, (bf16[8,2,8,32,128]{4,3,2,1,0:T(8,128)(2,1)S(1)}) %tuple.34, (bf16[8,2,8,32,128]{4,3,2,1,0:T(8,128)(2,1)S(1)}) %tuple.34), branch_computations={%region_4.0_spmd, %region_5.0_spmd} | conditional | bytes 10485768 | solution.py:417
  179.8 0.1 copy.43
  179.9 14.7 %all_to_all.61 = bf16[16,8,32,128]{3,2,1,0:T(8,128)(2,1)S(1)} all-to-all(bf16[16,8,32,128]{3,2,1,0:T(8,128)(2,1)S(1)} %bitcast.50), channel_id=1, replica_groups=mesh['xh'=2,'z'=8,'c'=2,'xl'=2,'y'=4] {'xh','xl','y'}, dimensions={0} | all-to-all | bytes 2097152 | tf_op jit(solution)/shard_map/cond/branch_0_fun/all_to_all | solution.py:412
  194.6 0.1 copy.24
  194.7 20.5 %all_to_all.62 = bf16[8,16,32,128]{3,2,1,0:T(8,128)(2,1)S(1)} all-to-all(bf16[8,16,32,128]{3,2,1,0:T(8,128)(2,1)S(1)} %copy.24), channel_id=1, replica_groups=mesh['xh'=2,'z'=8,'c'=2,'xl'=2,'y'=4] {'z'}, dimensions={0} | all-to-all | bytes 2097152 | tf_op jit(solution)/shard_map/cond/branch_0_fun/all_to_all | solution.py:413
  215.2 0.1 copy.36
  215.3 2.4 %finish.1 = bf16[32,128,128]{2,1,0:T(8,128)(2,1)} custom-call(f32[2,128]{1,0:T(2,128)S(1)} %copy-done.6, bf16[16,8,32,128]{3,2,1,0:T(8,128)(2,1)S(1)} %get-tuple-element.38.hidden_ref, bf16[32,128,128]{2,1,0:T(8,128)(2,1)S(1)} %get-tuple-element.36.cells_ref, f32[32,128,128]{2,1,0:T(8,128)S(1)} %output_gate.1.gate_ref, bf16[2,128,128]{2,1,0:T(8,128)(2,1)S(1)} %copy-done.2), custom_call_target="tpu_custom_call" | custom-call | tf_op jit(solution)/shard_map/finish/pallas_call | solution.py:254
Async XLA Ops:
  66.7 7.4 %collective-permute-start = (bf16[16,8,32,128]{3,2,1,0:T(8,128)(2,1)S(1)}, bf16[16,8,32,128]{3,2,1,0:T(8,128)(2,1)S(1)}, u32[]{:S(2)}, u32[]{:S(2)}) collective-permute-start(bf16[16,8,32,128]{3,2,1,0:T(8,128)(2,1)S(1)} %take_right.1), channel_id=1, source_target_pairs={{0,8},{8,0},{1,9},{9,1},{2,10},{10,2},{3,11},{11,3},{4,12},{12,4},... | collective-permute-start | bytes 3145736 | tf_op jit(solution)/shard_map/ppermute | solution.py:436
  76.7 36.6 %copy-start = (bf16[32,128,128]{2,1,0:T(8,128)(2,1)S(1)}, bf16[32,128,128]{2,1,0:T(8,128)(2,1)}, u32[]{:S(2)}) copy-start(bf16[32,128,128]{2,1,0:T(8,128)(2,1)} %get-tuple-element.31.cells_ref) | copy-start | bytes 3145732
  76.7 36.6 %copy-start.1 = (bf16[2,128,512]{2,1,0:T(8,128)(2,1)S(1)}, bf16[2,128,512]{2,1,0:T(8,128)(2,1)}, u32[]{:S(2)}) copy-start(bf16[2,128,512]{2,1,0:T(8,128)(2,1)} %proj_ref.1) | copy-start | bytes 786436
  76.7 36.6 %copy-start.2 = (bf16[2,128,128]{2,1,0:T(8,128)(2,1)S(1)}, bf16[2,128,128]{2,1,0:T(8,128)(2,1)}, u32[]{:S(2)}) copy-start(bf16[2,128,128]{2,1,0:T(8,128)(2,1)} %weight_ref.5) | copy-start | bytes 196612
  76.7 36.6 %copy-start.3 = (bf16[2,128,128]{2,1,0:T(8,128)(2,1)S(1)}, bf16[2,128,128]{2,1,0:T(8,128)(2,1)}, u32[]{:S(2)}) copy-start(bf16[2,128,128]{2,1,0:T(8,128)(2,1)} %weight_ref.4) | copy-start | bytes 196612
  76.7 36.6 %copy-start.4 = (s32[1024]{0:T(1024)S(1)}, s32[1024]{0:T(1024)}, u32[]{:S(2)}) copy-start(s32[1024]{0:T(1024)} %param.14) | copy-start | bytes 12292
  76.7 36.6 %copy-start.5 = (f32[2,128]{1,0:T(2,128)S(1)}, f32[2,128]{1,0:T(2,128)}, u32[]{:S(2)}) copy-start(f32[2,128]{1,0:T(2,128)} %gain_ref.2) | copy-start | bytes 3076
  76.7 36.6 %copy-start.6 = (f32[2,128]{1,0:T(2,128)S(1)}, f32[2,128]{1,0:T(2,128)}, u32[]{:S(2)}) copy-start(f32[2,128]{1,0:T(2,128)} %gain_ref.3) | copy-start | bytes 3076
  76.8 36.6 %all-to-all-start.12 = ((bf16[128,32,128]{2,1,0:T(8,128)(2,1)}), bf16[128,32,128]{2,1,0:T(8,128)(2,1)S(1)}, u32[]{:S(2)}, u32[]{:S(2)}) async-start(bf16[128,32,128]{2,1,0:T(8,128)(2,1)} %bitcast.19), calls=%async_computation.12 | async-start | bytes 2097152 | tf_op jit(solution)/shard_map/all_to_all | solution.py:431
  172.8 6.2 %collective-permute-start.1 = (bf16[512,1024]{1,0:T(8,128)(2,1)S(1)}, bf16[512,1024]{1,0:T(8,128)(2,1)S(1)}, u32[]{:S(2)}, u32[]{:S(2)}) collective-permute-start(bf16[512,1024]{1,0:T(8,128)(2,1)S(1)} %get-tuple-element.35), channel_id=1, source_target_pairs={{0,8},{8,0},{1,9},{9,1},{2,10},{10,2},{3,11},{11,3},{4,12},{12,4},... | collective-permute-start | bytes 3145736 | tf_op jit(solution)/shard_map/ppermute | solution.py:436
